TPU v7x, 32 devices: a whole 2x2x4 slice. The times are simulated.
32 devices in a mesh: row: 8 (over y, x, core), col: 4 (over z).
Axes of the slice: x: 2, y: 2, z: 4, core: 2. Of those that a mesh axis runs over, the one named last changes fastest.
Arguments:
- tokens: bfloat16 [8192, 1536], P('row', 'col'), may hold values from -6 to 6
- cotangent: bfloat16 [8192, 1536], P('row', 'col'), may hold values from -6 to 6
- adapter_ids: int32 [4], replicated, may hold values from 0 to 7
- doc_lengths: int32 [4], replicated, may hold values from 1 to 7679, as said below
- norm_gain: float32 [2, 2, 1536], P(None, None, 'col'), may hold values from 0.5 to 1.5
- inlet_weight: bfloat16 [2, 1536, 2, 2048], P(None, 'row', None, 'col'), may hold values from -0.15625 to 0.15625
- inlet_lower: bfloat16 [2, 1536, 2, 8, 16], replicated, may hold values from -0.15625 to 0.15625
- inlet_upper: bfloat16 [2, 2, 8, 16, 2048], P(None, None, None, None, 'col'), may hold values from -0.8984375 to 0.8984375
- conv_weight: float32 [2, 4, 2048], P(None, None, 'col'), may hold values from -3 to 3
- conv_bias: float32 [2, 2048], P(None, 'col'), may hold values from -1.8 to 1.8
- gate_weight: bfloat16 [2, 2, 8, 256, 256], P(None, None, 'col'), may hold values from -0.375 to 0.375
- gate_bias: float32 [2, 2, 2048], P(None, None, 'col'), may hold values from -3 to 3
- decay_param: float32 [2, 2048], P(None, 'col'), may hold values from -30 to -4
- outlet_weight: bfloat16 [2, 1536, 2048], P(None, 'row', 'col'), may hold values from -0.125 to 0.125
- outlet_lower: bfloat16 [2, 2048, 8, 16], P(None, 'col'), may hold values from -0.125 to 0.125
- outlet_upper: bfloat16 [2, 8, 16, 1536], replicated, may hold values from -0.8984375 to 0.8984375
- expand_weight: bfloat16 [2, 1536, 2, 4608], P(None, 'row', None, 'col'), may hold values from -0.15625 to 0.15625
- expand_lower: bfloat16 [2, 1536, 2, 8, 16], replicated, may hold values from -0.15625 to 0.15625
- expand_upper: bfloat16 [2, 2, 8, 16, 4608], P(None, None, None, None, 'col'), may hold values from -0.8984375 to 0.8984375
- shrink_weight: bfloat16 [2, 1536, 4608], P(None, 'row', 'col'), may hold values from -0.09375 to 0.09375
- shrink_lower: bfloat16 [2, 4608, 8, 16], P(None, 'col'), may hold values from -0.09375 to 0.09375
- shrink_upper: bfloat16 [2, 8, 16, 1536], replicated, may hold values from -0.8984375 to 0.8984375
Outputs:
- states: bfloat16 [2, 8192, 1536], P(None, 'row', 'col')
- tokens_grad: float32 [8192, 1536], P('row', 'col')
- inlet_lower_grad: float32 [2, 1536, 2, 8, 16], replicated
- inlet_upper_grad: float32 [2, 2, 8, 16, 2048], P(None, None, None, None, 'col')
- outlet_lower_grad: float32 [2, 2048, 8, 16], P(None, 'col')
- outlet_upper_grad: float32 [2, 8, 16, 1536], replicated
- expand_lower_grad: float32 [2, 1536, 2, 8, 16], replicated
- expand_upper_grad: float32 [2, 2, 8, 16, 4608], P(None, None, None, None, 'col')
- shrink_lower_grad: float32 [2, 4608, 8, 16], P(None, 'col')
- shrink_upper_grad: float32 [2, 8, 16, 1536], replicated
Inputs may be any that keep to these rules, and one draw needn't show every extreme that they name: `doc_lengths`: each document has at least one token and the lengths sum to 8192; one of them, at a place drawn from the seed, is the longest, with more than 7168 tokens.
All inputs are finite; a program needn't handle non-finite values.
Results may differ from a plain program's by a relative error of at most 0.03.
Values may be sent and summed in bfloat16 or wider, within the bound.
A program may use at most 384 MiB of HBM per device.

v0:
```python
from functools import partial

import jax
import jax.numpy as jnp
from jax import lax
from jax.sharding import PartitionSpec as P

D = 1536
HS = 256
CONV = 4
ADAPTERS = 8
RANK = 16
LAYERS = 2


EPSILON = 1e-06
FLOAT = jnp.float32
BRAIN = jnp.bfloat16


def for_sending(shard):

    def short(part):
        return part.astype(jnp.bfloat16) if part.dtype == jnp.float32 else part

    return jax.tree.map(short, shard)


def passed_along(shard, axis, by):
    peers = lax.axis_size(axis)
    pairs = [(i, i + by) for i in range(peers) if 0 <= i + by < peers]
    return lax.ppermute(shard, axis, pairs)


def gelu_tanh(value):
    return jax.nn.gelu(value, approximate=True)


def gated_mix(hidden, gate):
    return hidden * gelu_tanh(gate)


def geglu(gate, upper):
    return gelu_tanh(gate) * upper


def recurrence_terms(conv_value, logit_rate, logit_input, softness, first):
    rate = jax.nn.sigmoid(logit_rate)
    inward = jax.nn.sigmoid(logit_input)
    log_decay = -8.0 * softness * rate
    keep = 1.0 - first
    decay = jnp.exp(log_decay) * keep
    scale = keep * jnp.sqrt(-jnp.expm1(2.0 * log_decay)) + first
    return (decay, scale * inward * conv_value)


def locate(places, doc_lengths, adapter_ids):
    ends = jnp.cumsum(doc_lengths)
    starts = ends - doc_lengths
    inside = (places[:, None] >= starts[None, :]) & (places[:, None] < ends[None, :])
    begin = jnp.sum(jnp.where(inside, starts[None, :], 0), axis=1)
    chosen = jnp.sum(jnp.where(inside, adapter_ids[None, :], 0), axis=1)
    pick = (chosen[:, None] == jnp.arange(ADAPTERS, dtype=jnp.int32)[None, :]).astype(FLOAT)
    offset = places - begin
    first = (offset == 0).astype(FLOAT)[:, None]
    return (offset, pick, first)


def mask_rows(inner, pick):
    shaped = inner.reshape(inner.shape[:-1] + (ADAPTERS, RANK))
    spread = pick.reshape((pick.shape[0],) + (1,) * (inner.ndim - 2) + (ADAPTERS, 1))
    return (shaped * spread).reshape(inner.shape).astype(BRAIN)


def affine_join(earlier, later):
    return (earlier[0] * later[0], later[0] * earlier[1] + later[1])


def col_total(values):
    return lax.psum(values, "col")


def gather_features(rows_local):
    return lax.all_gather(rows_local, "col", axis=1, tiled=True)


def feature_share(partial_sum):
    return lax.psum_scatter(
        partial_sum.astype(jnp.bfloat16), "col", scatter_dimension=1, tiled=True
    ).astype(jnp.float32)


def into_width(left, weight):
    empty = jnp.zeros((left.shape[0], weight.shape[1]), FLOAT)
    piece = jax.tree.map(
        lambda part: lax.all_gather(part, "row", axis=0, tiled=True), for_sending(weight)
    )
    columns = lax.slice_in_dim(left, 0, piece.shape[0], axis=1)
    return empty + jnp.dot(columns, piece, preferred_element_type=FLOAT)


def back_width(left, weight):

    def columns(piece, start):
        return lax.dot_general(left, piece, (((1,), (1,)), ((), ())), preferred_element_type=FLOAT)

    return columns(lax.all_gather(for_sending(weight), "row", axis=0, tiled=True), jnp.int32(0))


def carry_forward(total_decay, total_state):

    def advance(turn, incoming):
        return passed_along(total_decay * incoming + total_state, "row", 1)

    return lax.fori_loop(0, lax.axis_size("row") - 1, advance, jnp.zeros_like(total_state))


def carry_backward(total_decay, total_state):

    def retreat(turn, incoming):
        return passed_along(total_decay * incoming + total_state, "row", -1)

    return lax.fori_loop(0, lax.axis_size("row") - 1, retreat, jnp.zeros_like(total_state))


def conv_forward(lead, weight, bias, offset):
    rows = lead.shape[0]
    rim = passed_along(lead[rows - (CONV - 1) :], "row", 1)
    extended = jnp.concatenate([rim, lead], axis=0)
    result = bias[None, :] + weight[0][None, :] * lead
    for shift_by in range(1, CONV):
        moved = extended[CONV - 1 - shift_by : CONV - 1 - shift_by + rows]
        valid = (offset >= shift_by).astype(FLOAT)[:, None]
        result = result + weight[shift_by][None, :] * moved * valid
    return result


def conv_backward(d_conv, weight, offset):
    rows = d_conv.shape[0]
    terms = [
        weight[shift_by][None, :] * d_conv * (offset >= shift_by).astype(FLOAT)[:, None]
        for shift_by in range(CONV)
    ]
    leading = jnp.stack([term[: CONV - 1] for term in terms[1:]], axis=0)
    arrived = passed_along(leading, "row", -1)
    result = terms[0]
    for shift_by in range(1, CONV):
        padded = jnp.concatenate([terms[shift_by], arrived[shift_by - 1]], axis=0)
        result = result + padded[shift_by : shift_by + rows]
    return result


def norm_forward(stream, gain):
    scale = lax.rsqrt(col_total(jnp.sum(stream * stream, axis=1)) / D + EPSILON)
    return (scale, stream * scale[:, None] * gain[None, :])


def norm_backward(stream, scale, gain, d_normed):
    total = col_total(jnp.sum(d_normed * gain[None, :] * stream, axis=1))
    return (
        scale[:, None] * gain[None, :] * d_normed
        - stream * (scale * scale * scale * total / D)[:, None]
    )


def local_weights(params, layer):
    inlet = params["inlet_weight"][layer]
    expand = params["expand_weight"][layer]
    return (
        inlet.reshape(inlet.shape[0], -1),
        params["outlet_weight"][layer],
        expand.reshape(expand.shape[0], -1),
        params["shrink_weight"][layer],
    )


def transposed(left, right):
    return lax.dot_general(left, right, (((1,), (1,)), ((), ())), preferred_element_type=FLOAT)


def layer_forward(stream, params, layer, offset, pick, first):
    rows = stream.shape[0]
    ranks = ADAPTERS * RANK
    inlet, outlet, expand, shrink = local_weights(params, layer)
    width = outlet.shape[1]
    spread = shrink.shape[1]
    gains = params["norm_gain"][layer]
    scale_one, normed = norm_forward(stream, gains[0])
    normed_full = gather_features(normed.astype(BRAIN))
    main = into_width(normed_full, inlet).reshape(rows, 2, width)
    lower_in = params["inlet_lower"][layer].reshape(D, 2 * ranks)
    inner = mask_rows(
        jnp.dot(normed_full, lower_in, preferred_element_type=FLOAT).reshape(rows, 2, ranks), pick
    )
    upper_in = params["inlet_upper"][layer].reshape(2, ranks, width)
    branch = main + jnp.einsum("tbk,bkc->tbc", inner, upper_in, preferred_element_type=FLOAT)
    gate = branch[:, 1]
    conv = conv_forward(
        branch[:, 0], params["conv_weight"][layer], params["conv_bias"][layer], offset
    ).astype(BRAIN)
    logits = jnp.einsum(
        "thi,jhio->jtho",
        conv.reshape(rows, -1, HS),
        params["gate_weight"][layer],
        preferred_element_type=FLOAT,
    )
    logits = logits.reshape(2, rows, width) + params["gate_bias"][layer][:, None, :]
    softness = jax.nn.softplus(params["decay_param"][layer])
    conv_value = conv.astype(FLOAT)
    decay, drive = recurrence_terms(conv_value, logits[0], logits[1], softness, first)
    cum_decay, partial_state = lax.associative_scan(affine_join, (decay, drive), axis=0)
    state_in = carry_forward(cum_decay[rows - 1], partial_state[rows - 1])
    hidden = partial_state + cum_decay * state_in[None, :]
    mixed = gated_mix(hidden, gate).astype(BRAIN)
    lowrank = mask_rows(
        jnp.dot(
            mixed, params["outlet_lower"][layer].reshape(width, ranks), preferred_element_type=FLOAT
        ),
        pick,
    )
    out_upper = params["outlet_upper"][layer].reshape(ranks, D)
    summed = back_width(mixed, outlet) + jnp.dot(lowrank, out_upper, preferred_element_type=FLOAT)
    middle = stream + feature_share(summed)
    scale_two, normed_two = norm_forward(middle, gains[1])
    normed_two_full = gather_features(normed_two.astype(BRAIN))
    main_two = into_width(normed_two_full, expand).reshape(rows, 2, spread)
    lower_two = params["expand_lower"][layer].reshape(D, 2 * ranks)
    inner_two = mask_rows(
        jnp.dot(normed_two_full, lower_two, preferred_element_type=FLOAT).reshape(rows, 2, ranks),
        pick,
    )
    upper_two = params["expand_upper"][layer].reshape(2, ranks, spread)
    branch_two = main_two + jnp.einsum(
        "tbk,bkf->tbf", inner_two, upper_two, preferred_element_type=FLOAT
    )
    product = geglu(branch_two[:, 0], branch_two[:, 1]).astype(BRAIN)
    lowrank_two = mask_rows(
        jnp.dot(
            product,
            params["shrink_lower"][layer].reshape(spread, ranks),
            preferred_element_type=FLOAT,
        ),
        pick,
    )
    shrink_up = params["shrink_upper"][layer].reshape(ranks, D)
    summed_two = back_width(product, shrink) + jnp.dot(
        lowrank_two, shrink_up, preferred_element_type=FLOAT
    )
    result = middle + feature_share(summed_two)
    kept = dict(
        stream=stream,
        scale_one=scale_one,
        normed_full=normed_full,
        inner=inner,
        gate=gate,
        conv_value=conv_value,
        logits=logits,
        decay=decay,
        hidden=hidden,
        state_in=state_in,
        mixed=mixed,
        lowrank=lowrank,
        middle=middle,
        scale_two=scale_two,
        normed_two_full=normed_two_full,
        inner_two=inner_two,
        branch_two=branch_two,
        product=product,
        lowrank_two=lowrank_two,
    )
    return (result, kept)


def layer_backward(d_stream, params, layer, kept, offset, pick, first):
    rows = d_stream.shape[0]
    ranks = ADAPTERS * RANK
    inlet, outlet, expand, shrink = local_weights(params, layer)
    width = outlet.shape[1]
    spread = shrink.shape[1]
    gains = params["norm_gain"][layer]
    d_out_full = gather_features(d_stream.astype(BRAIN))
    shrink_up = params["shrink_upper"][layer].reshape(ranks, D)
    shrink_low = params["shrink_lower"][layer].reshape(spread, ranks)
    d_low_two = mask_rows(transposed(d_out_full, shrink_up), pick)
    d_product = into_width(d_out_full, shrink) + transposed(d_low_two, shrink_low)
    grad_shrink_upper = jnp.einsum(
        "tk,td->kd", kept["lowrank_two"], d_out_full, preferred_element_type=FLOAT
    )
    grad_shrink_lower = jnp.einsum(
        "tf,tk->fk", kept["product"], d_low_two, preferred_element_type=FLOAT
    )
    _, pull = jax.vjp(geglu, kept["branch_two"][:, 0], kept["branch_two"][:, 1])
    d_gate_two, d_up_two = pull(d_product)
    d_branch_two = jnp.stack([d_gate_two, d_up_two], axis=1).astype(BRAIN)
    upper_two = params["expand_upper"][layer].reshape(2, ranks, spread)
    lower_two = params["expand_lower"][layer].reshape(D, 2, ranks)
    d_inner_two = mask_rows(
        jnp.einsum("tbf,bkf->tbk", d_branch_two, upper_two, preferred_element_type=FLOAT), pick
    )
    d_normed_two = back_width(d_branch_two.reshape(rows, 2 * spread), expand)
    d_normed_two = d_normed_two + jnp.einsum(
        "tbk,dbk->td", d_inner_two, lower_two, preferred_element_type=FLOAT
    )
    grad_expand_lower = jnp.einsum(
        "td,tbk->dbk", kept["normed_two_full"], d_inner_two, preferred_element_type=FLOAT
    )
    grad_expand_upper = jnp.einsum(
        "tbk,tbf->bkf", kept["inner_two"], d_branch_two, preferred_element_type=FLOAT
    )
    d_middle = d_stream + norm_backward(
        kept["middle"], kept["scale_two"], gains[1], feature_share(d_normed_two)
    )
    d_mid_full = gather_features(d_middle.astype(BRAIN))
    out_upper = params["outlet_upper"][layer].reshape(ranks, D)
    out_lower = params["outlet_lower"][layer].reshape(width, ranks)
    d_low = mask_rows(transposed(d_mid_full, out_upper), pick)
    d_mixed = into_width(d_mid_full, outlet) + transposed(d_low, out_lower)
    grad_outlet_upper = jnp.einsum(
        "tk,td->kd", kept["lowrank"], d_mid_full, preferred_element_type=FLOAT
    )
    grad_outlet_lower = jnp.einsum("tc,tk->ck", kept["mixed"], d_low, preferred_element_type=FLOAT)
    _, pull = jax.vjp(gated_mix, kept["hidden"], kept["gate"])
    d_hidden, d_gate = pull(d_mixed)
    decay = kept["decay"]
    next_decay = jnp.concatenate([decay[1:], jnp.ones_like(decay[:1])], axis=0)
    reach, local_grad = lax.associative_scan(
        affine_join, (next_decay, d_hidden), reverse=True, axis=0
    )
    arriving = carry_backward(decay[0] * reach[0], decay[0] * local_grad[0])
    d_state = local_grad + reach * arriving[None, :]
    prior = jnp.concatenate([kept["state_in"][None, :], kept["hidden"][: rows - 1]], axis=0)
    softness = jax.nn.softplus(params["decay_param"][layer])
    terms = partial(recurrence_terms, softness=softness, first=first)
    _, pull = jax.vjp(terms, kept["conv_value"], kept["logits"][0], kept["logits"][1])
    d_conv, d_rate, d_input = pull((d_state * prior, d_state))
    d_logits = jnp.stack([d_rate, d_input], axis=0).astype(BRAIN).reshape(2, rows, -1, HS)
    d_conv = d_conv + jnp.einsum(
        "jtho,jhio->thi", d_logits, params["gate_weight"][layer], preferred_element_type=FLOAT
    ).reshape(rows, width)
    d_lead = conv_backward(d_conv, params["conv_weight"][layer], offset)
    d_branch = jnp.stack([d_lead, d_gate], axis=1).astype(BRAIN)
    upper_in = params["inlet_upper"][layer].reshape(2, ranks, width)
    lower_in = params["inlet_lower"][layer].reshape(D, 2, ranks)
    d_inner = mask_rows(
        jnp.einsum("tbc,bkc->tbk", d_branch, upper_in, preferred_element_type=FLOAT), pick
    )
    d_normed = back_width(d_branch.reshape(rows, 2 * width), inlet)
    d_normed = d_normed + jnp.einsum("tbk,dbk->td", d_inner, lower_in, preferred_element_type=FLOAT)
    grad_inlet_lower = jnp.einsum(
        "td,tbk->dbk", kept["normed_full"], d_inner, preferred_element_type=FLOAT
    )
    grad_inlet_upper = jnp.einsum(
        "tbk,tbc->bkc", kept["inner"], d_branch, preferred_element_type=FLOAT
    )
    d_input = d_middle + norm_backward(
        kept["stream"], kept["scale_one"], gains[0], feature_share(d_normed)
    )
    grads = (
        grad_inlet_lower.reshape(D, 2, ADAPTERS, RANK),
        grad_inlet_upper.reshape(2, ADAPTERS, RANK, width),
        grad_outlet_lower.reshape(width, ADAPTERS, RANK),
        grad_outlet_upper.reshape(ADAPTERS, RANK, D),
        grad_expand_lower.reshape(D, 2, ADAPTERS, RANK),
        grad_expand_upper.reshape(2, ADAPTERS, RANK, spread),
        grad_shrink_lower.reshape(spread, ADAPTERS, RANK),
        grad_shrink_upper.reshape(ADAPTERS, RANK, D),
    )
    return (d_input, grads)


def local(
    tokens,
    cotangent,
    adapter_ids,
    doc_lengths,
    norm_gain,
    inlet_weight,
    inlet_lower,
    inlet_upper,
    conv_weight,
    conv_bias,
    gate_weight,
    gate_bias,
    decay_param,
    outlet_weight,
    outlet_lower,
    outlet_upper,
    expand_weight,
    expand_lower,
    expand_upper,
    shrink_weight,
    shrink_lower,
    shrink_upper,
):
    params = dict(
        norm_gain=norm_gain,
        inlet_weight=inlet_weight,
        inlet_lower=inlet_lower,
        inlet_upper=inlet_upper,
        conv_weight=conv_weight,
        conv_bias=conv_bias,
        gate_weight=gate_weight,
        gate_bias=gate_bias,
        decay_param=decay_param,
        outlet_weight=outlet_weight,
        outlet_lower=outlet_lower,
        outlet_upper=outlet_upper,
        expand_weight=expand_weight,
        expand_lower=expand_lower,
        expand_upper=expand_upper,
        shrink_weight=shrink_weight,
        shrink_lower=shrink_lower,
        shrink_upper=shrink_upper,
    )
    rows = tokens.shape[0]
    places = lax.axis_index("row") * rows + jnp.arange(rows, dtype=jnp.int32)
    offset, pick, first = locate(places, doc_lengths, adapter_ids)
    stream = tokens.astype(FLOAT)
    outputs = []
    saved = []
    wholes = []
    for layer in range(LAYERS):
        whole = (None, None, None, None)
        stream, kept = layer_forward(stream, params, layer, offset, pick, first)
        outputs.append(stream.astype(BRAIN))
        saved.append(kept)
        wholes.append(whole)
    d_stream = cotangent.astype(FLOAT)
    collected = []
    for layer in reversed(range(LAYERS)):
        d_stream, layer_grads = layer_backward(
            d_stream, params, layer, saved[layer], offset, pick, first
        )
        collected.insert(0, layer_grads)
    stacked = [jnp.stack([entry[member] for entry in collected], axis=0) for member in range(8)]
    grid = lax.psum((stacked[0], stacked[3], stacked[4], stacked[7]), ("row", "col"))
    along = (
        lax.psum(stacked[1].astype(jnp.bfloat16), "row").astype(jnp.float32),
        lax.psum(stacked[2].astype(jnp.bfloat16), "row").astype(jnp.float32),
        lax.psum(stacked[5].astype(jnp.bfloat16), "row").astype(jnp.float32),
        lax.psum(stacked[6].astype(jnp.bfloat16), "row").astype(jnp.float32),
    )
    return (
        jnp.stack(outputs, axis=0),
        d_stream,
        grid[0],
        along[0],
        along[1],
        grid[1],
        grid[2],
        along[2],
        along[3],
        grid[3],
    )


def solution(mesh):
    return jax.shard_map(
        local,
        mesh=mesh,
        in_specs=(
            P("row", "col"),
            P("row", "col"),
            P(),
            P(),
            P(None, None, "col"),
            P(None, "row", None, "col"),
            P(),
            P(None, None, None, None, "col"),
            P(None, None, "col"),
            P(None, "col"),
            P(None, None, "col", None, None),
            P(None, None, "col"),
            P(None, "col"),
            P(None, "row", "col"),
            P(None, "col", None, None),
            P(),
            P(None, "row", None, "col"),
            P(),
            P(None, None, None, None, "col"),
            P(None, "row", "col"),
            P(None, "col", None, None),
            P(),
        ),
        out_specs=(
            P(None, "row", "col"),
            P("row", "col"),
            P(),
            P(None, None, None, None, "col"),
            P(None, "col", None, None),
            P(),
            P(),
            P(None, None, None, None, "col"),
            P(None, "col", None, None),
            P(),
        ),
        check_vma=False,
    )
```

profile of v0, /device:TPU:0, one launch (start us, length us, event | category | flops | bytes accessed | tf_op | source)
XLA Modules:
  0.0 2989.4 jit_solution(4666341594559579200)
XLA Ops:
  37.7 50.4 %all-gather.21.cloned.1.call-done = bf16[1024,1536]{1,0:T(8,128)(2,1)} async-done(((bf16[1024,384]{1,0:T(8,128)(2,1)}), bf16[1024,1536]{1,0:T(8,128)(2,1)}) %all-gather.21.cloned.1.call-update) | async-done | bytes 3145744 | tf_op jit(solution)/shard_map/all_gather | solution.py:84
  91.0 30.5 %all-gather.23.cloned.1.call-done = bf16[1536,1024]{1,0:T(8,128)(2,1)} async-done(((bf16[192,1024]{1,0:T(8,128)(2,1)}), bf16[1536,1024]{1,0:T(8,128)(2,1)}) %all-gather.23.cloned.1.call-update) | async-done | bytes 3145744 | tf_op jit(solution)/shard_map/all_gather | solution.py:96
  357.9 34.1 %while.40 = (s32[]{:T(128)}, f32[512]{0:T(512)S(1)}, f32[512]{0:T(512)S(1)}, f32[512]{0:T(512)S(1)}, s32[]{:T(128)}) while((s32[]{:T(128)}, f32[512]{0:T(512)S(1)}, f32[512]{0:T(512)S(1)}, f32[512]{0:T(512)S(1)}, s32[]{:T(128)}) %tuple.285), condition=%wide.region_6.7_spmd, body=%wide.region_5.6_spmd.sunk | while | flops 1026 | bytes 16485 | solution.py:115
  406.8 69.7 %reduce-scatter.25.cloned.1.call-done = bf16[384,1024]{1,0:T(8,128)(2,1)} async-done(((bf16[1536,1024]{1,0:T(8,128)(2,1)}), bf16[384,1024]{1,0:T(8,128)(2,1)}) %reduce-scatter.25.cloned.1.call-update) | async-done | bytes 786448
  500.4 51.5 %all-gather.25.cloned.1.call-done = bf16[1024,1536]{1,0:T(8,128)(2,1)} async-done(((bf16[1024,384]{1,0:T(8,128)(2,1)}), bf16[1024,1536]{1,0:T(8,128)(2,1)}) %all-gather.25.cloned.1.call-update) | async-done | bytes 3145744 | tf_op jit(solution)/shard_map/all_gather | solution.py:84
  555.0 46.7 %all-gather.27.cloned.1.call-done = bf16[1536,2304]{1,0:T(8,128)(2,1)} async-done(((bf16[192,2304]{1,0:T(8,128)(2,1)}), bf16[1536,2304]{1,0:T(8,128)(2,1)}) %all-gather.27.cloned.1.call-update) | async-done | bytes 7077904 | tf_op jit(solution)/shard_map/all_gather | solution.py:96
  619.8 18.4 all-gather.47.cloned.1.call-done
  655.6 58.6 %reduce-scatter.27.cloned.1.call-done = bf16[384,1024]{1,0:T(8,128)(2,1)} async-done(((bf16[1536,1024]{1,0:T(8,128)(2,1)}), bf16[384,1024]{1,0:T(8,128)(2,1)}) %reduce-scatter.27.cloned.1.call-update) | async-done | bytes 786448
  749.0 65.4 %all-gather.29.cloned.1.call-done = bf16[1024,1536]{1,0:T(8,128)(2,1)} async-done(((bf16[1024,384]{1,0:T(8,128)(2,1)}), bf16[1024,1536]{1,0:T(8,128)(2,1)}) %all-gather.29.cloned.1.call-update) | async-done | bytes 3145744 | tf_op jit(solution)/shard_map/all_gather | solution.py:84
  1070.2 34.7 %while.41 = (s32[]{:T(128)}, f32[512]{0:T(512)S(1)}, f32[512]{0:T(512)S(1)}, f32[512]{0:T(512)S(1)}, s32[]{:T(128)}) while((s32[]{:T(128)}, f32[512]{0:T(512)S(1)}, f32[512]{0:T(512)S(1)}, f32[512]{0:T(512)S(1)}, s32[]{:T(128)}) %tuple.287), condition=%wide.region_14.15_spmd, body=%wide.region_13.14_spmd.sunk | while | flops 1026 | bytes 16485 | solution.py:115
  1125.4 64.9 %reduce-scatter.29.cloned.1.call-done = bf16[384,1024]{1,0:T(8,128)(2,1)} async-done(((bf16[1536,1024]{1,0:T(8,128)(2,1)}), bf16[384,1024]{1,0:T(8,128)(2,1)}) %reduce-scatter.29.cloned.1.call-update) | async-done | bytes 786448
  1208.3 47.0 %all-gather.37.cloned.1.call-done = bf16[1024,1536]{1,0:T(8,128)(2,1)} async-done(((bf16[1024,384]{1,0:T(8,128)(2,1)}), bf16[1024,1536]{1,0:T(8,128)(2,1)}) %all-gather.37.cloned.1.call-update) | async-done | bytes 3145744 | tf_op jit(solution)/shard_map/all_gather | solution.py:84
  1259.1 30.6 %all-gather.51.cloned.1.call-done = bf16[1,1536,1152]{2,1,0:T(8,128)(2,1)} async-done(((bf16[1,192,1152]{2,1,0:T(8,128)(2,1)}), bf16[1,1536,1152]{2,1,0:T(8,128)(2,1)}) %all-gather.51.cloned.1.call-update) | async-done | bytes 3538960 | tf_op jit(solution)/shard_map/all_gather | solution.py:107
  1299.1 41.8 %all-gather.35.cloned.1.call-done = bf16[1536,2304]{1,0:T(8,128)(2,1)} async-done(((bf16[192,2304]{1,0:T(8,128)(2,1)}), bf16[1536,2304]{1,0:T(8,128)(2,1)}) %all-gather.35.cloned.1.call-update) | async-done | bytes 7077904 | tf_op jit(solution)/shard_map/all_gather | solution.py:96
  1340.9 65.4 %all-gather.33.cloned.1.call-done = bf16[1024,1536]{1,0:T(8,128)(2,1)} async-done(((bf16[1024,384]{1,0:T(8,128)(2,1)}), bf16[1024,1536]{1,0:T(8,128)(2,1)}) %all-gather.33.cloned.1.call-update) | async-done | bytes 3145744 | tf_op jit(solution)/shard_map/all_gather | solution.py:84
  1475.8 59.0 %reduce-scatter.33.cloned.1.call-done = bf16[384,1024]{1,0:T(8,128)(2,1)} async-done(((bf16[1536,1024]{1,0:T(8,128)(2,1)}), bf16[384,1024]{1,0:T(8,128)(2,1)}) %reduce-scatter.33.cloned.1.call-update) | async-done | bytes 786448
  1897.2 32.3 %while.42 = (s32[]{:T(128)}, f32[512]{0:T(512)S(1)}, f32[512]{0:T(512)S(1)}, f32[512]{0:T(512)S(1)}, s32[]{:T(128)}) while((s32[]{:T(128)}, f32[512]{0:T(512)S(1)}, f32[512]{0:T(512)S(1)}, f32[512]{0:T(512)S(1)}, s32[]{:T(128)}) %tuple.283), condition=%wide.region_23.24_spmd, body=%wide.region_22.23_spmd.sunk | while | flops 1026 | bytes 16485 | solution.py:123
  1990.2 62.6 %reduce-scatter.35.cloned.1.call-done = bf16[384,1024]{1,0:T(8,128)(2,1)} async-done(((bf16[1536,1024]{1,0:T(8,128)(2,1)}), bf16[384,1024]{1,0:T(8,128)(2,1)}) %reduce-scatter.35.cloned.1.call-update) | async-done | bytes 786448
  2071.0 61.8 %all-gather.41.cloned.1.call-done = bf16[1024,1536]{1,0:T(8,128)(2,1)} async-done(((bf16[1024,384]{1,0:T(8,128)(2,1)}), bf16[1024,1536]{1,0:T(8,128)(2,1)}) %all-gather.41.cloned.1.call-update) | async-done | bytes 3145744 | tf_op jit(solution)/shard_map/all_gather | solution.py:84
  2177.0 58.9 %reduce-scatter.37.cloned.1.call-done = bf16[384,1024]{1,0:T(8,128)(2,1)} async-done(((bf16[1536,1024]{1,0:T(8,128)(2,1)}), bf16[384,1024]{1,0:T(8,128)(2,1)}) %reduce-scatter.37.cloned.1.call-update) | async-done | bytes 786448
  2563.1 32.9 %while.43 = (s32[]{:T(128)}, f32[512]{0:T(512)S(1)}, f32[512]{0:T(512)S(1)}, f32[512]{0:T(512)S(1)}, s32[]{:T(128)}) while((s32[]{:T(128)}, f32[512]{0:T(512)S(1)}, f32[512]{0:T(512)S(1)}, f32[512]{0:T(512)S(1)}, s32[]{:T(128)}) %tuple.281), condition=%wide.region_31.32_spmd, body=%wide.region_30.31_spmd.sunk | while | flops 1026 | bytes 16485 | solution.py:123
  2678.8 30.9 %all-reduce.171.cloned.1.call-done = (bf16[2,2,8,16,512]{4,3,2,1,0:T(8,128)(2,1)}, bf16[2,512,8,16]{1,3,2,0:T(8,128)(2,1)}, bf16[2,2,8,16,1152]{4,3,2,1,0:T(8,128)(2,1)}, bf16[2,1152,8,16]{1,3,2,0:T(8,128)(2,1)}) async-done(((bf16[2,2,8,16,512]{4,3,2,1,0:T(8,128)(2,1)}, bf16[2,512,8,16]{1,3,2,0:T(8,128)(2,1)}, bf16[2,2,8,16,1152]{4,3,2,1,0:T(8,128)(2,1)}, bf16[2,1152,8,16]{1,3,2,0:T(8,128)(2,1)}), ...) | async-done | bytes 2555920 | tf_op jit(solution)/shard_map/psum | solution.py:438
  2715.8 56.8 %reduce-scatter.39.cloned.1.call-done = bf16[384,1024]{1,0:T(8,128)(2,1)} async-done(((bf16[1536,1024]{1,0:T(8,128)(2,1)}), bf16[384,1024]{1,0:T(8,128)(2,1)}) %reduce-scatter.39.cloned.1.call-update) | async-done | bytes 786448
  2790.0 182.3 %all-reduce.169.cloned.1.call-done = (f32[2,1536,2,8,16]{1,4,3,2,0:T(8,128)}, f32[2,8,16,1536]{3,2,1,0:T(8,128)}, f32[2,1536,2,8,16]{1,4,3,2,0:T(8,128)}, f32[2,8,16,1536]{3,2,1,0:T(8,128)}) async-done(((f32[2,1536,2,8,16]{1,4,3,2,0:T(8,128)}, f32[2,8,16,1536]{3,2,1,0:T(8,128)}, f32[2,1536,2,8,16]{1,4,3,2,0:T(8,128)}, f32[2,8,16,1536]{3,2,1,0:T(8,128)}), (f32[2,1536,2,8,16]{1,4,3,2,0:T(8,128)}, ...) | async-done | bytes 9437200 | tf_op jit(solution)/shard_map/psum | solution.py:436
  (1806 shorter events, 1815.8 us)
Async XLA Ops:
  28.6 370.9 %all-gather.45.cloned.1.call-start = ((), (), s32[]{:S(2)}) async-start(), calls=%async_computation.20 | async-start | bytes 1769472 | tf_op jit(solution)/shard_map/all_gather | solution.py:107
  29.4 447.0 %reduce-scatter.25.cloned.1.call-start = ((), (), s32[]{:S(2)}) async-start(), calls=%async_computation.24 | async-start | bytes 3932160
  406.7 145.2 %all-gather.25.cloned.1.call-start = ((), (), s32[]{:S(2)}) async-start(), calls=%async_computation.10 | async-start | bytes 3932160 | tf_op jit(solution)/shard_map/all_gather | solution.py:84
  490.0 111.7 %all-gather.27.cloned.1.call-start = ((), (), s32[]{:S(2)}) async-start(), calls=%async_computation.11 | async-start | bytes 7962624 | tf_op jit(solution)/shard_map/all_gather | solution.py:96
  494.7 143.4 %all-gather.47.cloned.1.call-start = ((), (), s32[]{:S(2)}) async-start(), calls=%async_computation.21 | async-start | bytes 3981312 | tf_op jit(solution)/shard_map/all_gather | solution.py:107
  496.2 218.0 %reduce-scatter.27.cloned.1.call-start = ((), (), s32[]{:S(2)}) async-start(), calls=%async_computation.25 | async-start | bytes 3932160
  653.8 95.2 %all-gather.31.cloned.1.call-start = ((), (), s32[]{:S(2)}) async-start(), calls=%async_computation.13 | async-start | bytes 3538944 | tf_op jit(solution)/shard_map/all_gather | solution.py:96
  655.6 158.8 %all-gather.29.cloned.1.call-start = ((), (), s32[]{:S(2)}) async-start(), calls=%async_computation.12 | async-start | bytes 3932160 | tf_op jit(solution)/shard_map/all_gather | solution.py:84
  730.6 381.6 %all-gather.49.cloned.1.call-start = ((), (), s32[]{:S(2)}) async-start(), calls=%async_computation.22 | async-start | bytes 1769472 | tf_op jit(solution)/shard_map/all_gather | solution.py:107
  731.4 459.0 %reduce-scatter.29.cloned.1.call-start = ((), (), s32[]{:S(2)}) async-start(), calls=%async_computation.26 | async-start | bytes 3932160
  1123.0 132.4 %all-gather.37.cloned.1.call-start = ((), (), s32[]{:S(2)}) async-start(), calls=%async_computation.16 | async-start | bytes 3932160 | tf_op jit(solution)/shard_map/all_gather | solution.py:84
  1123.7 166.0 %all-gather.51.cloned.1.call-start = ((), (), s32[]{:S(2)}) async-start(), calls=%async_computation.23 | async-start | bytes 3981312 | tf_op jit(solution)/shard_map/all_gather | solution.py:107
  1124.3 216.6 %all-gather.35.cloned.1.call-start = ((), (), s32[]{:S(2)}) async-start(), calls=%async_computation.15 | async-start | bytes 7962624 | tf_op jit(solution)/shard_map/all_gather | solution.py:96
  1125.4 280.9 %all-gather.33.cloned.1.call-start = ((), (), s32[]{:S(2)}) async-start(), calls=%async_computation.14 | async-start | bytes 3932160 | tf_op jit(solution)/shard_map/all_gather | solution.py:84
  1203.8 331.0 %reduce-scatter.33.cloned.1.call-start = ((), (), s32[]{:S(2)}) async-start(), calls=%async_computation.28 | async-start | bytes 3932160
  1475.8 141.2 %all-gather.39.cloned.1.call-start = ((), (), s32[]{:S(2)}) async-start(), calls=%async_computation.17 | async-start | bytes 3932160 | tf_op jit(solution)/shard_map/all_gather | solution.py:84
  1549.8 438.1 %reduce-scatter.31.cloned.1.call-start = ((), (), s32[]{:S(2)}) async-start(), calls=%async_computation.27 | async-start | bytes 3932160
  1616.9 435.9 %reduce-scatter.35.cloned.1.call-start = ((), (), s32[]{:S(2)}) async-start(), calls=%async_computation.29 | async-start | bytes 3932160
  1987.8 145.0 %all-gather.41.cloned.1.call-start = ((), (), s32[]{:S(2)}) async-start(), calls=%async_computation.18 | async-start | bytes 3932160 | tf_op jit(solution)/shard_map/all_gather | solution.py:84
  2070.9 165.0 %reduce-scatter.37.cloned.1.call-start = ((), (), s32[]{:S(2)}) async-start(), calls=%async_computation.30 | async-start | bytes 3932160
  2177.0 136.2 %all-gather.43.cloned.1.call-start = ((), (), s32[]{:S(2)}) async-start(), calls=%async_computation.19 | async-start | bytes 3932160 | tf_op jit(solution)/shard_map/all_gather | solution.py:84
  2251.3 458.4 %all-reduce.171.cloned.1.call-start = ((), (), s32[]{:S(2)}) async-start(), calls=%async_computation.33 | async-start | bytes 5111808 | tf_op jit(solution)/shard_map/psum | solution.py:438
  2639.4 133.2 %reduce-scatter.39.cloned.1.call-start = ((), (), s32[]{:S(2)}) async-start(), calls=%async_computation.31 | async-start | bytes 3932160
  2653.2 319.1 %all-reduce.169.cloned.1.call-start = ((), (), s32[]{:S(2)}) async-start(), calls=%async_computation.32 | async-start | bytes 18874368 | tf_op jit(solution)/shard_map/psum | solution.py:436
  (413 other events, 10442.7 us)
Sparse Core Ops, SparseCore 0:
  26.5 61.5 all-gather.20
  90.6 30.8 all-gather.22
  406.9 69.5 reduce-scatter.24
  490.1 61.7 all-gather.24
  554.2 47.4 all-gather.26
  604.2 33.9 all-gather.46
  653.9 60.2 reduce-scatter.26
  716.7 32.3 all-gather.30
  751.0 63.3 all-gather.28
  1123.1 67.2 reduce-scatter.28
  1191.9 63.3 all-gather.36
  1257.1 32.5 all-gather.50
  1292.0 48.8 all-gather.34
  1342.9 63.3 all-gather.32
  1475.9 58.8 reduce-scatter.32
  1549.9 61.6 all-gather.38
  1617.0 58.6 reduce-scatter.30
  1987.9 64.8 reduce-scatter.34
  2071.0 61.6 all-gather.40
  2177.1 58.8 reduce-scatter.36
  2251.4 61.7 all-gather.42
  2639.5 70.1 all-reduce.170
  2712.7 59.9 reduce-scatter.38
  2780.3 191.9 all-reduce.168
  (2 shorter events, 50.0 us)
where the time goes:
time: 3030 us; the launch traced here: 2990 us
  waiting for transfers between devices  1250 us (41%)
  local copies, waits for them, and re-layouts  1030 us (34%)
  other arithmetic  291 us (10%)
  matrix products  226 us (7%)
  blocking collectives  86.7 us (3%)
  starting transfers between devices  84.5 us (3%)
    unnamed x34, waiting for transfers between devices  433 us
    all_gather x8, waiting for transfers between devices, gather_features(): return lax.all_gather(rows_local, 'col', axis=1, tiled=True)  356 us
    slice x146, local copies, waits for them, and re-layouts, layer_backward(): lax.associative_scan(affine_join, (next_decay, d_hidden), reverse=True, a...  332 us
    slice x136, local copies, waits for them, and re-layouts, layer_forward(): lax.associative_scan(affine_join, (decay, drive), axis=0)  250 us
    psum x1, waiting for transfers between devices, local(): lax.psum((stacked[0], stacked[3], stacked[4], stacked[7]), ('row', 'col'))  182 us
    all_gather x4, waiting for transfers between devices, into_width(): lax.all_gather(part, 'row', axis=0, tiled=True)  136 us
    unnamed x784, local copies, waits for them, and re-layouts  104 us
    pad x72, local copies, waits for them, and re-layouts, layer_backward(): lax.associative_scan(affine_join, (next_decay, d_hidden), reverse=True, a...  87 us
  transfers between devices with their start and end apart: 58, of which 54 were waited for; matrix products, arithmetic and copies ran while one was open for 35% of the time, Pallas kernels for 0%

commit v1 on v0

v1 whole, which is shorter than its diff:
```python
from functools import partial

import jax
import jax.numpy as jnp
from jax import lax
from jax.experimental import pallas as pl
from jax.experimental.pallas import tpu as pltpu
from jax.sharding import PartitionSpec as P

HS = 256
CONV = 4
LAYERS = 2
SEGS = 8

EPSILON = 1e-06
FLOAT = jnp.float32
BRAIN = jnp.bfloat16
VMEM_BYTES = 48 * 1024 * 1024
CURVE = 0.7978845608028654
CUBIC = 0.044715
LANES = 128
SLABS = HS // LANES


def nn(left, right):
    return lax.dot_general(left, right, (((1,), (0,)), ((), ())), preferred_element_type=FLOAT)


def nt(left, right):
    return lax.dot_general(left, right, (((1,), (1,)), ((), ())), preferred_element_type=FLOAT)


def tn(left, right):
    return lax.dot_general(left, right, (((0,), (0,)), ((), ())), preferred_element_type=FLOAT)


def gelu_tanh(value):
    return 0.5 * value * (1.0 + jnp.tanh(CURVE * (value + CUBIC * value * value * value)))


def gelu_pair(value):
    square = value * value
    bend = jnp.tanh(CURVE * value * (1.0 + CUBIC * square))
    half = 0.5 * (1.0 + bend)
    slope = half + 0.5 * value * (1.0 - bend * bend) * CURVE * (1.0 + 3.0 * CUBIC * square)
    return value * half, slope


def put(slabs, value, rows=slice(None)):
    for slab in range(SLABS):
        slabs[slab, rows] = value[:, slab * LANES : (slab + 1) * LANES]


def take(slabs, rows=slice(None)):
    return jnp.concatenate([slabs[slab, rows] for slab in range(SLABS)], axis=1)


def flat(parts):
    return jnp.concatenate(parts, axis=1)


def one_less_square(twice, square):
    series = -twice * (
        1.0 + twice * (0.5 + twice * (1.0 / 6.0 + twice * (1.0 / 24.0 + twice * (1.0 / 120.0))))
    )
    return jnp.where(twice > -0.1, series, 1.0 - square)


def gate_values(conv, gate_w, gate_b, soft):
    rate = jax.nn.sigmoid(nn(conv, gate_w[0]) + gate_b[0:1])
    inward = jax.nn.sigmoid(nn(conv, gate_w[1]) + gate_b[1:2])
    log_decay = (-8.0 * soft) * rate
    raw = jnp.exp(log_decay)
    gap = one_less_square(2.0 * log_decay, raw * raw)
    return rate, inward, raw, gap


def forward_kernel(
    par, lead, halo, offset, conv_w, conv_b, gate_w, gate_b, soft,
    conv_out, decay_out, state_out, cum_out, seg_out, ext, drive,
):
    rows = lead.shape[0]
    half = rows // 2
    span = rows // SEGS
    start = pl.multiple_of(par[0] * half, half)
    other = pl.multiple_of(half - par[0] * half, half)
    ext[0:8] = halo[...]
    ext[8 : 8 + half] = lead[pl.ds(start, half), :]
    ext[8 + half : 8 + rows] = lead[pl.ds(other, half), :]
    place = offset[...]
    total = conv_b[...] + conv_w[0:1] * ext[8 : 8 + rows]
    for step in range(1, CONV):
        valid = (place >= step).astype(FLOAT)
        total = total + conv_w[step : step + 1] * ext[8 - step : 8 - step + rows] * valid
    conv = total.astype(BRAIN)
    conv_out[...] = conv
    rate, inward, raw, gap = gate_values(conv, gate_w, gate_b, soft[...])
    first = (place == 0).astype(FLOAT)
    keep = 1.0 - first
    put(decay_out, raw * keep)
    put(drive, (keep * jnp.sqrt(gap) + first) * inward * conv.astype(FLOAT))

    def advance(step, carried):
        where = pl.ds(step, SEGS, stride=span)
        after = []
        for slab, (state, cum) in enumerate(carried):
            rates = decay_out[slab, where, :]
            state = rates * state + drive[slab, where, :]
            cum = rates * cum
            state_out[slab, where, :] = state
            cum_out[slab, where, :] = cum
            after.append((state, cum))
        return tuple(after)

    shape = (SEGS, lead.shape[1])
    fresh = (jnp.zeros((SEGS, LANES), FLOAT), jnp.ones((SEGS, LANES), FLOAT))
    ends = lax.fori_loop(0, span, advance, (fresh,) * SLABS, unroll=8)
    state, cum = (flat(parts) for parts in zip(*ends))
    run_state = jnp.zeros((1, shape[1]), FLOAT)
    run_cum = jnp.ones((1, shape[1]), FLOAT)
    for seg in range(SEGS):
        seg_out[seg : seg + 1] = run_state
        seg_out[SEGS + seg : SEGS + seg + 1] = run_cum
        run_state = cum[seg : seg + 1] * run_state + state[seg : seg + 1]
        run_cum = cum[seg : seg + 1] * run_cum
    seg_out[2 * SEGS : 2 * SEGS + 1] = run_cum
    seg_out[2 * SEGS + 1 : 2 * SEGS + 2] = run_state
    seg_out[2 * SEGS + 2 : 3 * SEGS] = jnp.zeros((SEGS - 2, shape[1]), FLOAT)


def mix_kernel(par, state, cum, seg, carry, gate, hidden_out, mixed_out, hidden):
    rows = gate.shape[0]
    half = rows // 2
    span = rows // SEGS
    start = pl.multiple_of(par[0] * half, half)
    other = pl.multiple_of(half - par[0] * half, half)
    entering = seg[0:SEGS] + seg[SEGS : 2 * SEGS] * carry[0:1]
    for at in range(SEGS):
        part = slice(at * span, (at + 1) * span)
        hidden[part] = take(state, part) + take(cum, part) * entering[at : at + 1]
    put(hidden_out, hidden[...])
    for place, part in ((start, slice(0, half)), (other, slice(half, rows))):
        mixed_out[pl.ds(place, half), :] = (
            hidden[part] * gelu_tanh(gate[pl.ds(place, half), :])
        ).astype(BRAIN)


def backward_kernel(
    par, grad, gate, hidden, decay, gate_grad, local_out, reach_out, seg_out, ext, grads
):
    rows = grad.shape[0]
    half = rows // 2
    span = rows // SEGS
    start = pl.multiple_of(par[0] * half, half)
    other = pl.multiple_of(half - par[0] * half, half)
    for place, part in ((start, slice(0, half)), (other, slice(half, rows))):
        value, slope = gelu_pair(gate[pl.ds(place, half), :])
        coming = grad[pl.ds(place, half), :]
        put(grads, coming * value, part)
        gate_grad[pl.ds(place, half), :] = (coming * take(hidden, part) * slope).astype(BRAIN)
    ext[:, 0:rows] = decay[...]
    ext[:, rows : rows + 8] = jnp.ones((SLABS, 8, LANES), FLOAT)

    def retreat(turn, carried):
        step = span - 1 - turn
        follows = pl.ds(step + 1, SEGS, stride=span)
        where = pl.ds(step, SEGS, stride=span)
        after = []
        for slab, (state, cum) in enumerate(carried):
            rates = ext[slab, follows, :]
            state = rates * state + grads[slab, where, :]
            cum = rates * cum
            local_out[slab, where, :] = state
            reach_out[slab, where, :] = cum
            after.append((state, cum))
        return tuple(after)

    shape = (SEGS, grad.shape[1])
    fresh = (jnp.zeros((SEGS, LANES), FLOAT), jnp.ones((SEGS, LANES), FLOAT))
    ends = lax.fori_loop(0, span, retreat, (fresh,) * SLABS, unroll=8)
    state, cum = (flat(parts) for parts in zip(*ends))
    run_state = jnp.zeros((1, shape[1]), FLOAT)
    run_cum = jnp.ones((1, shape[1]), FLOAT)
    for seg in reversed(range(SEGS)):
        seg_out[seg : seg + 1] = run_state
        seg_out[SEGS + seg : SEGS + seg + 1] = run_cum
        run_state = cum[seg : seg + 1] * run_state + state[seg : seg + 1]
        run_cum = cum[seg : seg + 1] * run_cum
    opening = take(decay, slice(0, 1))
    seg_out[2 * SEGS : 2 * SEGS + 1] = run_cum * opening
    seg_out[2 * SEGS + 1 : 2 * SEGS + 2] = run_state * opening
    seg_out[2 * SEGS + 2 : 3 * SEGS] = jnp.zeros((SEGS - 2, shape[1]), FLOAT)


def terms_kernel(
    par, local, reach, seg, carry, hidden, state_in, conv, offset,
    conv_w, gate_w, gate_b, soft,
    lead_grad, tail_out, head_out, ext, prior,
):
    rows = conv.shape[0]
    half = rows // 2
    span = rows // SEGS
    start = pl.multiple_of(par[0] * half, half)
    other = pl.multiple_of(half - par[0] * half, half)
    entering = seg[0:SEGS] + seg[SEGS : 2 * SEGS] * carry[0:1]
    for at in range(SEGS):
        part = slice(at * span, (at + 1) * span)
        ext[part] = take(local, part) + take(reach, part) * entering[at : at + 1]
    carried = ext[0:rows]
    prior[7:8] = state_in[0:1]
    prior[8 : 8 + rows] = take(hidden)
    before = prior[7 : 7 + rows]
    low = conv[...]
    value = low.astype(FLOAT)
    place = offset[...]
    first = (place == 0).astype(FLOAT)
    keep = 1.0 - first
    rate, inward, raw, gap = gate_values(low, gate_w, gate_b, soft[...])
    root = jnp.sqrt(gap)
    scale = keep * root + first
    pushed = carried * inward
    log_grad = keep * raw * (carried * before - pushed * value * (raw / root))
    rate_grad = ((-8.0 * soft[...]) * log_grad * rate * (1.0 - rate)).astype(BRAIN)
    scaled = carried * scale
    input_grad = (scaled * value * inward * (1.0 - inward)).astype(BRAIN)
    conv_grad = scaled * inward + nt(rate_grad, gate_w[0]) + nt(input_grad, gate_w[1])
    ext[0:rows] = conv_grad
    ext[rows : rows + 8] = jnp.zeros((8, conv.shape[1]), FLOAT)
    prior[0:rows] = conv_w[0:1] * conv_grad
    head = jnp.zeros((8, conv.shape[1]), FLOAT)
    for step in range(1, CONV):
        valid = (place >= step).astype(FLOAT)
        prior_term = conv_w[step : step + 1] * conv_grad * valid
        ext[0:rows] = prior_term
        prior[0:rows] = prior[0:rows] + ext[step : step + rows]
        lines = lax.broadcasted_iota(jnp.int32, (8, 1), 0)
        moved = pltpu.roll(prior_term[0:8], 8 - step, 0)
        head = head + jnp.where(lines >= 8 - step, moved, 0.0)
    head_out[...] = head
    tail_out[...] = prior[rows - 8 : rows]
    lead_grad[pl.ds(start, half), :] = prior[0:half].astype(BRAIN)
    lead_grad[pl.ds(other, half), :] = prior[half:rows].astype(BRAIN)


def column_call(kernel, parity, operands, kinds, outs, out_kinds, scratch, width):
    def spec(kind, shape):
        if kind == "all":
            return pl.BlockSpec(shape, lambda at, par: (0,) * len(shape))
        if kind == "heads":
            return pl.BlockSpec((shape[0], None) + shape[2:], lambda at, par: (0, at, 0, 0))
        if kind == "slabs":
            return pl.BlockSpec((SLABS,) + shape[1:], lambda at, par: (at, 0, 0))
        return pl.BlockSpec((shape[0], HS), lambda at, par: (0, at))

    return pl.pallas_call(
        kernel,
        out_shape=[jax.ShapeDtypeStruct(*out) for out in outs],
        grid_spec=pltpu.PrefetchScalarGridSpec(
            num_scalar_prefetch=1,
            grid=(width // HS,),
            in_specs=[spec(kind, value.shape) for kind, value in zip(kinds, operands)],
            out_specs=[spec(kind, out[0]) for kind, out in zip(out_kinds, outs)],
            scratch_shapes=scratch,
        ),
        compiler_params=pltpu.CompilerParams(vmem_limit_bytes=VMEM_BYTES),
    )(parity, *operands)


def partner(value):
    peers = lax.axis_size("col")
    return lax.ppermute(value, "col", [(at, at ^ 1) for at in range(peers)])


def from_shard(value, turn):
    peers = lax.axis_size("col")
    return lax.ppermute(value, "col", [((at + 2 * turn) % peers, at) for at in range(peers)])


def to_shard(value, turn):
    peers = lax.axis_size("col")
    return lax.ppermute(value, "col", [(at, (at + 2 * turn) % peers) for at in range(peers)])


def all_shards(value):
    return [value] + [from_shard(value, turn) for turn in range(1, lax.axis_size("col") // 2)]


def along_tokens(value, by):
    shards = lax.axis_size("col") // 2
    size = lax.axis_size("row") * lax.axis_size("col")
    pairs = [(at, at + 2 * by) for at in range(size) if 0 <= at + 2 * by < size]
    moved = lax.ppermute(value, ("row", "col"), pairs)
    return jnp.roll(moved, -by * (value.shape[-1] // shards), axis=-1)


def carry_in(total, direction):
    blocks = lax.axis_size("row") * lax.axis_size("col") // 2
    reach = 1
    while reach < blocks:
        earlier = along_tokens(total, direction * reach)
        total = jnp.stack([total[0] * earlier[0], total[0] * earlier[1] + total[1]])
        reach *= 2
    return along_tokens(total[1:2], direction)


def to_sequence(value):
    return lax.all_to_all(value, "col", split_axis=0, concat_axis=1, tiled=True)


def from_sequence(value):
    return lax.all_to_all(value, "col", split_axis=1, concat_axis=0, tiled=True)


def both_halves(value):
    return jnp.concatenate([value, partner(value)], axis=0)


def half_share(own, other):
    return own + partner(other.astype(BRAIN)).astype(FLOAT)


def norm_forward(stream, gain):
    scale = lax.rsqrt(jnp.mean(stream * stream, axis=1, keepdims=True) + EPSILON)
    return scale, (stream * scale * gain[None, :]).astype(BRAIN)


def norm_backward(stream, scale, gain, d_normed):
    gained = d_normed * gain[None, :]
    total = jnp.mean(gained * stream, axis=1, keepdims=True)
    return scale * gained - stream * (scale * scale * scale * total)


def masked(value, pick):
    return (value * pick).astype(BRAIN)


def layer_forward(stream, wide, small, gains, ctx):
    inlet, outlet, expand, shrink = wide
    pick, offset, parity = ctx["pick"], ctx["offset"], ctx["parity"]
    ranks = pick.shape[1]
    own = stream.shape[0]
    rows = 2 * own
    width = outlet.shape[1]
    spread = shrink.shape[1]

    scale_one, normed = norm_forward(stream, gains[0])
    normed_full = both_halves(normed)
    low = nt(normed_full, small["inlet_lower"])
    inner = [masked(low[:, b * ranks : (b + 1) * ranks], pick) for b in range(2)]
    branch = nn(normed_full, inlet)
    lead = branch[:, :width] + nn(inner[0], small["inlet_upper"][0])
    gate = branch[:, width:] + nn(inner[1], small["inlet_upper"][1])
    last = lax.dynamic_slice_in_dim(lead, (1 - parity[0]) * own + own - 8, 8, axis=0)
    halo = along_tokens(last, 1)
    full, slabs = (rows, width), (width // LANES, rows, LANES)
    conv, decay, state, cum, seg = column_call(
        forward_kernel,
        parity,
        [lead, halo, offset, small["conv_weight"], small["conv_bias"], small["gate_weight"],
         small["gate_bias"], small["soft"]],
        ["cols", "cols", "all", "cols", "cols", "heads", "cols", "cols"],
        [(full, BRAIN), (slabs, FLOAT), (slabs, FLOAT), (slabs, FLOAT), ((3 * SEGS, width), FLOAT)],
        ["cols", "slabs", "slabs", "slabs", "cols"],
        [pltpu.VMEM((rows + 8, HS), FLOAT), pltpu.VMEM((SLABS, rows, LANES), FLOAT)],
        width,
    )
    state_in = carry_in(seg[2 * SEGS : 2 * SEGS + 2], 1)
    hidden, mixed = column_call(
        mix_kernel,
        parity,
        [state, cum, seg, state_in, gate],
        ["slabs", "slabs", "cols", "cols", "cols"],
        [(slabs, FLOAT), (full, BRAIN)],
        ["slabs", "cols"],
        [pltpu.VMEM((rows, HS), FLOAT)],
        width,
    )
    lowrank = masked(nt(mixed, small["outlet_lower"]), pick)

    def outward(part):
        return nt(mixed[part], outlet) + nn(lowrank[part], small["outlet_upper"])

    middle = stream + half_share(outward(slice(0, own)), outward(slice(own, rows)))
    scale_two, normed_two = norm_forward(middle, gains[1])
    normed_two_full = both_halves(normed_two)
    low_two = nt(normed_two_full, small["expand_lower"])
    inner_two = [masked(low_two[:, b * ranks : (b + 1) * ranks], pick) for b in range(2)]
    branch_two = nn(normed_two_full, expand)
    up_gate = branch_two[:, :spread] + nn(inner_two[0], small["expand_upper"][0])
    up_value = branch_two[:, spread:] + nn(inner_two[1], small["expand_upper"][1])
    product = (gelu_tanh(up_gate) * up_value).astype(BRAIN)
    lowrank_two = masked(nt(product, small["shrink_lower"]), pick)

    def downward(part):
        return nt(product[part], shrink) + nn(lowrank_two[part], small["shrink_upper"])

    result = middle + half_share(downward(slice(0, own)), downward(slice(own, rows)))
    kept = dict(
        stream=stream, scale_one=scale_one, normed_full=normed_full, inner=inner, gate=gate,
        conv=conv, decay=decay, hidden=hidden, state_in=state_in, mixed=mixed, lowrank=lowrank,
        middle=middle, scale_two=scale_two, normed_two_full=normed_two_full, inner_two=inner_two,
        up_gate=up_gate, up_value=up_value, product=product, lowrank_two=lowrank_two,
    )
    return result, kept


def layer_backward(d_stream, wide, small, gains, kept, ctx):
    inlet, outlet, expand, shrink = wide
    pick, offset, parity = ctx["pick"], ctx["offset"], ctx["parity"]
    own = d_stream.shape[0]
    rows = 2 * own
    width = outlet.shape[1]
    spread = shrink.shape[1]

    d_out = both_halves(d_stream.astype(BRAIN))
    d_low_two = masked(nt(d_out, small["shrink_upper"]), pick)
    d_product = nn(d_out, shrink) + nn(d_low_two, small["shrink_lower"])
    shrink_upper_grad = tn(kept["lowrank_two"], d_out)
    shrink_lower_grad = tn(d_low_two, kept["product"])
    value, slope = gelu_pair(kept["up_gate"])
    d_branch_two = jnp.concatenate(
        [(slope * kept["up_value"] * d_product).astype(BRAIN), (value * d_product).astype(BRAIN)],
        axis=1,
    )
    d_inner_two = jnp.concatenate(
        [
            masked(nt(d_branch_two[:, b * spread : (b + 1) * spread], small["expand_upper"][b]), pick)
            for b in range(2)
        ],
        axis=1,
    )

    def inward_two(part):
        return nt(d_branch_two[part], expand) + nn(d_inner_two[part], small["expand_lower"])

    d_normed_two = half_share(inward_two(slice(0, own)), inward_two(slice(own, rows)))
    expand_lower_grad = tn(d_inner_two, kept["normed_two_full"])
    expand_upper_grad = jnp.concatenate(
        [
            tn(kept["inner_two"][b], d_branch_two[:, b * spread : (b + 1) * spread])
            for b in range(2)
        ],
        axis=0,
    )
    d_middle = d_stream + norm_backward(kept["middle"], kept["scale_two"], gains[1], d_normed_two)

    d_mid = both_halves(d_middle.astype(BRAIN))
    d_low = masked(nt(d_mid, small["outlet_upper"]), pick)
    d_mixed = nn(d_mid, outlet) + nn(d_low, small["outlet_lower"])
    outlet_upper_grad = tn(kept["lowrank"], d_mid)
    outlet_lower_grad = tn(d_low, kept["mixed"])
    full, slabs = (rows, width), (width // LANES, rows, LANES)
    d_gate, local_grad, reach, seg = column_call(
        backward_kernel,
        parity,
        [d_mixed, kept["gate"], kept["hidden"], kept["decay"]],
        ["cols", "cols", "slabs", "slabs"],
        [(full, BRAIN), (slabs, FLOAT), (slabs, FLOAT), ((3 * SEGS, width), FLOAT)],
        ["cols", "slabs", "slabs", "cols"],
        [
            pltpu.VMEM((SLABS, rows + 8, LANES), FLOAT),
            pltpu.VMEM((SLABS, rows, LANES), FLOAT),
        ],
        width,
    )
    arriving = carry_in(seg[2 * SEGS : 2 * SEGS + 2], -1)
    d_lead, tail, head = column_call(
        terms_kernel,
        parity,
        [local_grad, reach, seg, arriving, kept["hidden"], kept["state_in"], kept["conv"], offset,
         small["conv_weight"], small["gate_weight"], small["gate_bias"], small["soft"]],
        ["slabs", "slabs", "cols", "cols", "slabs", "cols", "cols", "all", "cols", "heads", "cols",
         "cols"],
        [(full, BRAIN), ((8, width), FLOAT), ((8, width), FLOAT)],
        ["cols"] * 3,
        [pltpu.VMEM((rows + 8, HS), FLOAT), pltpu.VMEM((rows + 8, HS), FLOAT)],
        width,
    )
    tail = (tail + along_tokens(head, -1)).astype(BRAIN)
    d_lead = lax.dynamic_update_slice_in_dim(
        d_lead, tail, (1 - parity[0]) * own + own - 8, axis=0
    )
    d_branch = jnp.concatenate([d_lead, d_gate], axis=1)
    d_inner = jnp.concatenate(
        [
            masked(nt(d_branch[:, b * width : (b + 1) * width], small["inlet_upper"][b]), pick)
            for b in range(2)
        ],
        axis=1,
    )

    def inward(part):
        return nt(d_branch[part], inlet) + nn(d_inner[part], small["inlet_lower"])

    d_normed = half_share(inward(slice(0, own)), inward(slice(own, rows)))
    inlet_lower_grad = tn(d_inner, kept["normed_full"])
    inlet_upper_grad = jnp.concatenate(
        [tn(kept["inner"][b], d_branch[:, b * width : (b + 1) * width]) for b in range(2)], axis=0
    )
    d_input = d_middle + norm_backward(kept["stream"], kept["scale_one"], gains[0], d_normed)
    shared = jnp.concatenate(
        [inlet_lower_grad, outlet_upper_grad, expand_lower_grad, shrink_upper_grad], axis=0
    )
    split = (
        jnp.concatenate([inlet_upper_grad, outlet_lower_grad], axis=0),
        jnp.concatenate([expand_upper_grad, shrink_lower_grad], axis=0),
    )
    return d_input, shared, split


def owned(grad, shards):
    piece = grad.shape[1] // shards
    parts = [grad[:, turn * piece : (turn + 1) * piece].astype(BRAIN) for turn in range(shards)]
    total = parts[0].astype(FLOAT)
    for turn in range(1, shards):
        total = total + to_shard(parts[turn], turn).astype(FLOAT)
    return total.astype(BRAIN)


def local(
    tokens, cotangent, adapter_ids, doc_lengths, norm_gain, inlet_weight, inlet_lower, inlet_upper,
    conv_weight, conv_bias, gate_weight, gate_bias, decay_param, outlet_weight, outlet_lower,
    outlet_upper, expand_weight, expand_lower, expand_upper, shrink_weight, shrink_lower,
    shrink_upper,
):
    row_at, col_at = lax.axis_index("row"), lax.axis_index("col")
    cols = lax.axis_size("col")
    shards = cols // 2
    rows = tokens.shape[0]
    own = rows // cols
    block = 2 * own
    docs = adapter_ids.shape[0]
    adapters, rank = inlet_lower.shape[3:]
    depth, part_width = inlet_weight.shape[1], inlet_weight.shape[3]
    part_spread = expand_weight.shape[3]
    d_model = inlet_lower.shape[1]

    parity = (col_at % 2).astype(jnp.int32)
    ends = jnp.cumsum(doc_lengths)
    starts = ends - doc_lengths
    ordered = row_at * rows + (col_at // 2) * block + jnp.arange(block, dtype=jnp.int32)
    inside = (ordered[:, None] >= starts[None, :]) & (ordered[:, None] < ends[None, :])
    offset = (ordered - jnp.sum(jnp.where(inside, starts[None, :], 0), axis=1))[:, None]
    halves = (parity * own, own - parity * own)
    at_home = jnp.concatenate(
        [ordered[0] + begin + jnp.arange(own, dtype=jnp.int32) for begin in halves]
    )
    within = (at_home[:, None] >= starts[None, :]) & (at_home[:, None] < ends[None, :])
    pick = jnp.repeat(within.astype(FLOAT), rank, axis=1)
    ctx = dict(pick=pick, offset=offset, parity=parity[None])

    stream = to_sequence(tokens).astype(FLOAT)
    d_stream = to_sequence(cotangent).astype(FLOAT)
    gains = lax.all_gather(norm_gain, "col", axis=2, tiled=True)

    def by_doc(factor, axis):
        return jnp.concatenate(
            [lax.dynamic_slice_in_dim(factor, adapter_ids[at], 1, axis) for at in range(docs)], axis
        )

    def gather_rows(value):
        return lax.all_gather(value, "row", axis=0, tiled=True)

    def joined(value, lead_shape, piece):
        parts = [part.reshape(lead_shape + (1, piece)) for part in all_shards(value)]
        return jnp.concatenate(parts, axis=-2).reshape(depth, -1)

    wides, smalls = [], []
    for layer in range(LAYERS):
        wide_inlet = gather_rows(joined(inlet_weight[layer], (depth, 2), part_width))
        wide_outlet = gather_rows(joined(outlet_weight[layer], (depth,), part_width))
        wide_expand = gather_rows(joined(expand_weight[layer], (depth, 2), part_spread))
        wide_shrink = gather_rows(joined(shrink_weight[layer], (depth,), part_spread))
        wides.append((wide_inlet, wide_outlet, wide_expand, wide_shrink))

        def lower_t(factor):
            return by_doc(jnp.moveaxis(factor[layer], 0, -1), factor.ndim - 4)

        def upper_t(factor):
            return by_doc(factor[layer], factor.ndim - 4)

        narrow = jnp.concatenate(
            [
                upper_t(inlet_upper).reshape(-1, part_width),
                lower_t(outlet_lower).reshape(-1, part_width),
            ]
        )
        broad = jnp.concatenate(
            [
                upper_t(expand_upper).reshape(-1, part_spread),
                lower_t(shrink_lower).reshape(-1, part_spread),
            ]
        )
        vectors = jnp.concatenate(
            [conv_weight[layer], gate_bias[layer], conv_bias[layer][None], decay_param[layer][None]]
        )
        narrow, broad, vectors = (
            jnp.concatenate(all_shards(value), axis=1) for value in (narrow, broad, vectors)
        )
        ranks = docs * rank
        smalls.append(
            dict(
                inlet_lower=lower_t(inlet_lower).reshape(2 * ranks, d_model),
                inlet_upper=narrow[: 2 * ranks].reshape(2, ranks, -1),
                outlet_lower=narrow[2 * ranks :],
                outlet_upper=upper_t(outlet_upper).reshape(ranks, d_model),
                expand_lower=lower_t(expand_lower).reshape(2 * ranks, d_model),
                expand_upper=broad[: 2 * ranks].reshape(2, ranks, -1),
                shrink_lower=broad[2 * ranks :],
                shrink_upper=upper_t(shrink_upper).reshape(ranks, d_model),
                conv_weight=vectors[:CONV],
                gate_bias=vectors[CONV : CONV + 2],
                conv_bias=vectors[CONV + 2 : CONV + 3],
                soft=jax.nn.softplus(vectors[CONV + 3 : CONV + 4]),
                gate_weight=jnp.concatenate(all_shards(gate_weight[layer]), axis=1),
            )
        )

    outputs, saved = [], []
    for layer in range(LAYERS):
        stream, kept = layer_forward(stream, wides[layer], smalls[layer], gains[layer], ctx)
        outputs.append(from_sequence(stream.astype(BRAIN)))
        saved.append(kept)
    shared, narrow, broad = [None] * LAYERS, [None] * LAYERS, [None] * LAYERS
    for layer in reversed(range(LAYERS)):
        d_stream, everywhere, split = layer_backward(
            d_stream, wides[layer], smalls[layer], gains[layer], saved[layer], ctx
        )
        shared[layer] = lax.psum(everywhere.astype(BRAIN), ("row", "col")).astype(FLOAT)
        narrow[layer] = lax.psum(owned(split[0], shards), "row").astype(FLOAT)
        broad[layer] = lax.psum(owned(split[1], shards), "row").astype(FLOAT)
    shared, narrow, broad = jnp.stack(shared), jnp.stack(narrow), jnp.stack(broad)
    ranks = docs * rank
    spread_out = (adapter_ids[None, :] == jnp.arange(adapters, dtype=jnp.int32)[:, None])

    def by_adapter(grad, count):
        grad = grad.reshape(LAYERS, count, docs, rank, -1)
        total = 0.0
        for doc in range(docs):
            total = total + jnp.where(
                spread_out[None, None, :, doc, None, None], grad[:, :, doc][:, :, None], 0.0
            )
        return total

    def lower_out(grad, count):
        grad = by_adapter(grad, count)
        if count == 1:
            grad = grad[:, 0]
        return jnp.moveaxis(grad, -1, 1)

    return (
        jnp.stack(outputs, axis=0),
        from_sequence(d_stream),
        lower_out(shared[:, : 2 * ranks], 2),
        by_adapter(narrow[:, : 2 * ranks], 2),
        lower_out(narrow[:, 2 * ranks :], 1),
        by_adapter(shared[:, 2 * ranks : 3 * ranks], 1)[:, 0],
        lower_out(shared[:, 3 * ranks : 5 * ranks], 2),
        by_adapter(broad[:, : 2 * ranks], 2),
        lower_out(broad[:, 2 * ranks :], 1),
        by_adapter(shared[:, 5 * ranks :], 1)[:, 0],
    )


def solution(mesh):
    return jax.shard_map(
        local,
        mesh=mesh,
        in_specs=(
            P("row", "col"),
            P("row", "col"),
            P(),
            P(),
            P(None, None, "col"),
            P(None, "row", None, "col"),
            P(),
            P(None, None, None, None, "col"),
            P(None, None, "col"),
            P(None, "col"),
            P(None, None, "col", None, None),
            P(None, None, "col"),
            P(None, "col"),
            P(None, "row", "col"),
            P(None, "col", None, None),
            P(),
            P(None, "row", None, "col"),
            P(),
            P(None, None, None, None, "col"),
            P(None, "row", "col"),
            P(None, "col", None, None),
            P(),
        ),
        out_specs=(
            P(None, "row", "col"),
            P("row", "col"),
            P(),
            P(None, None, None, None, "col"),
            P(None, "col", None, None),
            P(),
            P(),
            P(None, None, None, None, "col"),
            P(None, "col", None, None),
            P(),
        ),
        check_vma=False,
    )
```

time: 3030 us -> 1290 us (0.43); the launches traced: 2990 us -> 1280 us
  local copies, waits for them, and re-layouts: 1030 us -> 74.8 us
  waiting for transfers between devices: 1250 us -> 604 us
  other arithmetic: 291 us -> 66.5 us
  starting transfers between devices: 84.5 us -> 162 us
  Pallas kernels: 0 us -> 68.8 us
  blocking collectives: 86.7 us -> 38.4 us
    slice x302 -> x37, local copies, waits for them, and re-layouts: 610 us -> 11 us  [the longest x4 4.49 us: lower_t(): return by_doc(jnp.moveaxis(factor[layer], 0, -1), factor.ndim - 4)]
    all_gather x16 -> x8, waiting for transfers between devices: 541 us -> 0.07 us  [gather_rows(): return lax.all_gather(value, 'row', axis=0, tiled=True)]
    unnamed x34 -> x10, waiting for transfers between devices: 433 us -> 0.16 us
    ppermute x32 -> x60, waiting for transfers between devices: 62.4 us -> 444 us  [the longest x16 191 us: partner(): return lax.ppermute(value, 'col', [(at, at ^ 1) for at in range(peers)])]
    pad x144 -> x0, local copies, waits for them, and re-layouts: 159 us -> none  [the longest x72 87 us: layer_backward(): lax.associative_scan(affine_join, (next_decay, d_hidden), reverse=True, a...]
    psum x8 -> x0, blocking collectives: 86.7 us -> none  [col_total(): return lax.psum(values, 'col')]
    unnamed x784 -> x548, local copies, waits for them, and re-layouts: 104 us -> 24.8 us
    add x147 -> x13, other arithmetic: 94.4 us -> 16.2 us  [the longest x6 13.9 us: by_adapter(): total + jnp.where(spread_out[None, None, :, doc, None, None], grad[:, :,...]
  transfers between devices with their start and end apart: 58 -> 75, of which waited for: 54 -> 47; matrix products, arithmetic and copies ran while one was open for 35% -> 24% of each run, Pallas kernels for 0% -> 5%
where the time goes in v1:
time: 1290 us; the launch traced here: 1280 us
  waiting for transfers between devices  604 us (47%)
  matrix products  239 us (19%)
  starting transfers between devices  162 us (13%)
  local copies, waits for them, and re-layouts  74.8 us (6%)
  Pallas kernels  68.8 us (5%)
  other arithmetic  66.5 us (5%)
  blocking collectives  38.4 us (3%)
  between operations  28 us (2%)
    ppermute x16, waiting for transfers between devices, partner(): return lax.ppermute(value, 'col', [(at, at ^ 1) for at in range(peers)])  191 us
    ppermute x16, waiting for transfers between devices, from_shard(): lax.ppermute(value, 'col', [((at + 2 * turn) % peers, at) for at in range...  178 us
    psum x1, waiting for transfers between devices, local(): lax.psum(everywhere.astype(BRAIN), ('row', 'col')).astype(FLOAT)  133 us
    dot_general x36, matrix products, nn(): lax.dot_general(left, right, (((1,), (0,)), ((), ())), preferred_element_...  117 us
    dot_general x36, matrix products, nt(): lax.dot_general(left, right, (((1,), (1,)), ((), ())), preferred_element_...  103 us
    ppermute x24, starting transfers between devices, along_tokens(): moved = lax.ppermute(value, ('row', 'col'), pairs)  83.9 us
    pallas_call x8, Pallas kernels, column_call(): pl.pallas_call(kernel, out_shape=[jax.ShapeDtypeStruct(*out) for out in o...  68.8 us
    ppermute x24, waiting for transfers between devices, along_tokens(): moved = lax.ppermute(value, ('row', 'col'), pairs)  57.4 us
  transfers between devices with their start and end apart: 75, of which 47 were waited for; matrix products, arithmetic and copies ran while one was open for 24% of the time, Pallas kernels for 5%

profile of v1, /device:TPU:0, one launch (start us, length us, event | category | flops | bytes accessed | tf_op | source)
XLA Modules:
  0.0 1281.3 jit_solution(16024278339709818594)
XLA Ops:
  13.9 17.5 %collective-permute-done.1 = bf16[192,2,512]{2,1,0:T(2,128)(2,1)S(1)} collective-permute-done((bf16[192,2,512]{2,1,0:T(2,128)(2,1)S(1)}, bf16[192,2,512]{2,1,0:T(2,128)(2,1)S(1)}, u32[]{:S(2)}, u32[]{:S(2)}) %collective-permute-start.1) | collective-permute-done | bytes 393248 | tf_op jit(solution)/shard_map/ppermute | solution.py:276
  35.5 11.2 collective-permute-done.11
  50.4 39.8 %collective-permute-done.14 = bf16[192,2,1152]{2,1,0:T(2,128)(2,1)S(1)} collective-permute-done((bf16[192,2,1152]{2,1,0:T(2,128)(2,1)S(1)}, bf16[192,2,1152]{2,1,0:T(2,128)(2,1)S(1)}, u32[]{:S(2)}, u32[]{:S(2)}) %collective-permute-start.14) | collective-permute-done | bytes 884768 | tf_op jit(solution)/shard_map/ppermute | solution.py:276
  99.2 21.0 %collective-permute-done.16 = bf16[192,1152]{1,0:T(8,128)(2,1)S(1)} collective-permute-done((bf16[192,1152]{1,0:T(8,128)(2,1)S(1)}, bf16[192,1152]{1,0:T(8,128)(2,1)S(1)}, u32[]{:S(2)}, u32[]{:S(2)}) %collective-permute-start.16) | collective-permute-done | bytes 442400 | tf_op jit(solution)/shard_map/ppermute | solution.py:276
  121.5 20.2 %collective-permute-done.19 = bf16[192,2,512]{2,1,0:T(2,128)(2,1)S(1)} collective-permute-done((bf16[192,2,512]{2,1,0:T(2,128)(2,1)S(1)}, bf16[192,2,512]{2,1,0:T(2,128)(2,1)S(1)}, u32[]{:S(2)}, u32[]{:S(2)}) %collective-permute-start.19) | collective-permute-done | bytes 393248 | tf_op jit(solution)/shard_map/ppermute | solution.py:276
  180.3 44.6 %collective-permute-done.32 = bf16[192,2,1152]{2,1,0:T(2,128)(2,1)S(1)} collective-permute-done((bf16[192,2,1152]{2,1,0:T(2,128)(2,1)}, bf16[192,2,1152]{2,1,0:T(2,128)(2,1)S(1)}, u32[]{:S(2)}, u32[]{:S(2)}) %collective-permute-start.32) | collective-permute-done | bytes 884768 | tf_op jit(solution)/shard_map/ppermute | solution.py:276
  244.3 38.4 %all_gather.27 = f32[2,2,1536]{2,1,0:T(2,128)S(1)} all-gather(f32[2,2,384]{2,1,0:T(2,128)S(1)} %copy-done.255), channel_id=1, replica_groups=mesh['row'=8,'col'=4] {'col'}, dimensions={2}, use_global_device_ids=true | all-gather | bytes 30720 | tf_op jit(solution)/shard_map/all_gather | solution.py:554
  303.2 26.3 %collective-permute-done = bf16[256,1536]{1,0:T(8,128)(2,1)} collective-permute-done((bf16[256,1536]{1,0:T(8,128)(2,1)S(1)}, bf16[256,1536]{1,0:T(8,128)(2,1)}, u32[]{:S(2)}, u32[]{:S(2)}) %collective-permute-start) | collective-permute-done | bytes 786464 | tf_op jit(solution)/shard_map/ppermute | solution.py:271
  344.1 12.7 shard_map.285
  356.7 12.5 collective-permute-start.6
  408.3 16.3 %collective-permute-done.12 = bf16[256,1536]{1,0:T(8,128)(2,1)S(1)} collective-permute-done((bf16[256,1536]{1,0:T(8,128)(2,1)S(1)}, bf16[256,1536]{1,0:T(8,128)(2,1)S(1)}, u32[]{:S(2)}, u32[]{:S(2)}) %collective-permute-start.12) | collective-permute-done | bytes 786464 | tf_op jit(solution)/shard_map/ppermute | solution.py:271
  432.5 20.5 %collective-permute-done.13 = bf16[256,1536]{1,0:T(8,128)(2,1)S(1)} collective-permute-done((bf16[256,1536]{1,0:T(8,128)(2,1)S(1)}, bf16[256,1536]{1,0:T(8,128)(2,1)S(1)}, u32[]{:S(2)}, u32[]{:S(2)}) %collective-permute-start.13) | collective-permute-done | bytes 786464 | tf_op jit(solution)/shard_map/ppermute | solution.py:271
  483.5 12.7 collective-permute-done.17
  507.8 13.4 %collective-permute-done.34 = bf16[192,1152]{1,0:T(8,128)(2,1)S(1)} collective-permute-done((bf16[192,1152]{1,0:T(8,128)(2,1)S(1)}, bf16[192,1152]{1,0:T(8,128)(2,1)S(1)}, u32[]{:S(2)}, u32[]{:S(2)}) %collective-permute-start.34) | collective-permute-done | bytes 442400 | tf_op jit(solution)/shard_map/ppermute | solution.py:276
  540.5 12.6 shard_map.287
  604.3 14.1 %collective-permute-done.30 = bf16[256,1536]{1,0:T(8,128)(2,1)} collective-permute-done((bf16[256,1536]{1,0:T(8,128)(2,1)}, bf16[256,1536]{1,0:T(8,128)(2,1)}, u32[]{:S(2)}, u32[]{:S(2)}) %collective-permute-start.30) | collective-permute-done | bytes 786464 | tf_op jit(solution)/shard_map/ppermute | solution.py:271
  672.3 15.1 %multiply_convert_fusion.3 = (bf16[512,2304]{1,0:T(8,128)(2,1)S(1)}, bf16[512,2304]{1,0:T(8,128)(2,1)S(1)}, bf16[512,2304]{1,0:T(8,128)(2,1)S(1)}) fusion(f32[512,2304]{1,0:T(8,128)} %slice_add_fusion.1, f32[512,2304]{1,0:T(8,128)} %fusion.87, f32[512,4608]{1,0:T(8,128)} %copy-done.97, f32[512,2304]{1,0:T(8,128)} %fusion.83, ...), kind=kOutput, calls=%fused_computation.29 | convolution fusion | flops 3662807040 | bytes 34603008 | tf_op jit(solution)/shard_map/dot_general | solution.py:26
  806.6 18.5 %collective-permute-done.43 = f32[1,1024]{1,0:T(1,128)S(1)} collective-permute-done((f32[1,1024]{1,0:T(1,128)S(1)}, f32[1,1024]{1,0:T(1,128)S(1)}, u32[]{:S(2)}, u32[]{:S(2)}) %collective-permute-start.43) | collective-permute-done | bytes 4128 | tf_op jit(solution)/shard_map/ppermute | solution.py:292
  852.7 15.2 %collective-permute-done.45 = bf16[256,1536]{1,0:T(8,128)(2,1)S(1)} collective-permute-done((bf16[256,1536]{1,0:T(8,128)(2,1)S(1)}, bf16[256,1536]{1,0:T(8,128)(2,1)S(1)}, u32[]{:S(2)}, u32[]{:S(2)}) %collective-permute-start.45) | collective-permute-done | bytes 786464 | tf_op jit(solution)/shard_map/ppermute | solution.py:271
  876.1 14.0 %collective-permute-done.57 = bf16[192,512]{1,0:T(8,128)(2,1)S(1)} collective-permute-done((bf16[192,512]{1,0:T(8,128)(2,1)S(1)}, bf16[192,512]{1,0:T(8,128)(2,1)S(1)}, u32[]{:S(2)}, u32[]{:S(2)}) %collective-permute-start.57) | collective-permute-done | bytes 196640 | tf_op jit(solution)/shard_map/ppermute | solution.py:281
  894.8 11.4 multiply_convert_fusion
  952.9 23.9 %collective-permute-done.48 = bf16[256,1536]{1,0:T(8,128)(2,1)S(1)} collective-permute-done((bf16[256,1536]{1,0:T(8,128)(2,1)S(1)}, bf16[256,1536]{1,0:T(8,128)(2,1)S(1)}, u32[]{:S(2)}, u32[]{:S(2)}) %collective-permute-start.48) | collective-permute-done | bytes 786464 | tf_op jit(solution)/shard_map/ppermute | solution.py:271
  1092.6 27.6 %all-reduce.7.cloned.1.call-done = (bf16[1,192,512]{2,1,0:T(8,128)(2,1)}, bf16[1,192,512]{2,1,0:T(8,128)(2,1)}, bf16[1,192,1152]{2,1,0:T(8,128)(2,1)}, bf16[1,192,1152]{2,1,0:T(8,128)(2,1)}) async-done(((bf16[1,192,512]{2,1,0:T(8,128)(2,1)}, bf16[1,192,512]{2,1,0:T(8,128)(2,1)}, bf16[1,192,1152]{2,1,0:T(8,128)(2,1)}, bf16[1,192,1152]{2,1,0:T(8,128)(2,1)}), (bf16[1,192,512]{2,1,0:T(8,128)(2,1)}, ...) | async-done | bytes 1277968 | tf_op jit(solution)/shard_map/psum | solution.py:630
  1129.5 132.7 %all-reduce.5.cloned.1.call-done = (bf16[1,384,1536]{2,1,0:T(8,128)(2,1)}, bf16[1,384,1536]{2,1,0:T(8,128)(2,1)}) async-done(((bf16[1,384,1536]{2,1,0:T(8,128)(2,1)}, bf16[1,384,1536]{2,1,0:T(8,128)(2,1)}), (bf16[1,384,1536]{2,1,0:T(8,128)(2,1)}, bf16[1,384,1536]{2,1,0:T(8,128)(2,1)})) %all-reduce.5.cloned.1.call-update) | async-done | bytes 2359312 | tf_op jit(solution)/shard_map/psum | solution.py:629
  (1001 shorter events, 661.3 us)
Async XLA Ops:
  7.2 324.5 %all-gather.9.cloned.1.call-start = ((), (), s32[]{:S(2)}) async-start(), calls=%async_computation.5 | async-start | bytes 7077888 | tf_op jit(solution)/shard_map/all_gather | solution.py:562
  35.3 367.8 %all-gather.11.cloned.1.call-start = ((), (), s32[]{:S(2)}) async-start(), calls=%async_computation.6 | async-start | bytes 3538944 | tf_op jit(solution)/shard_map/all_gather | solution.py:562
  47.6 409.6 %all-gather.13.cloned.1.call-start = ((), (), s32[]{:S(2)}) async-start(), calls=%async_computation.7 | async-start | bytes 15925248 | tf_op jit(solution)/shard_map/all_gather | solution.py:562
  97.9 376.2 %all-gather.15.cloned.1.call-start = ((), (), s32[]{:S(2)}) async-start(), calls=%async_computation.8 | async-start | bytes 7962624 | tf_op jit(solution)/shard_map/all_gather | solution.py:562
  121.3 401.0 %all-gather.17.cloned.1.call-start = ((), (), s32[]{:S(2)}) async-start(), calls=%async_computation.9 | async-start | bytes 7077888 | tf_op jit(solution)/shard_map/all_gather | solution.py:562
  145.5 445.6 %all-gather.19.cloned.1.call-start = ((), (), s32[]{:S(2)}) async-start(), calls=%async_computation.10 | async-start | bytes 3538944 | tf_op jit(solution)/shard_map/all_gather | solution.py:562
  157.2 133.2 %all-to-all-start = ((bf16[4,256,384]{2,1,0:T(8,128)(2,1)}), bf16[4,256,384]{2,1,0:T(8,128)(2,1)S(1)}, u32[]{:S(2)}, u32[]{:S(2)}) async-start(bf16[4,256,384]{2,1,0:T(8,128)(2,1)} %bitcast), calls=%async_computation | async-start | bytes 1572864 | tf_op jit(solution)/shard_map/all_to_all | solution.py:307
  161.1 494.0 %all-gather.21.cloned.1.call-start = ((), (), s32[]{:S(2)}) async-start(), calls=%async_computation.11 | async-start | bytes 15925248 | tf_op jit(solution)/shard_map/all_gather | solution.py:562
  161.1 63.8 %collective-permute-start.32 = (bf16[192,2,1152]{2,1,0:T(2,128)(2,1)}, bf16[192,2,1152]{2,1,0:T(2,128)(2,1)S(1)}, u32[]{:S(2)}, u32[]{:S(2)}) collective-permute-start(bf16[192,2,1152]{2,1,0:T(2,128)(2,1)} %get-tuple-element.93), channel_id=1, source_target_pairs={{2,0},{3,1},{0,2},{1,3},{6,4},{7,5},{4,6},{5,7},{10,8},{11,9},{8,1... | collective-permute-start | bytes 2654216 | tf_op jit(solution)/shard_map/ppermute | solution.py:276
  175.5 126.1 %collective-permute-start.2 = (bf16[192,512]{1,0:T(8,128)(2,1)}, bf16[192,512]{1,0:T(8,128)(2,1)}, u32[]{:S(2)}, u32[]{:S(2)}) collective-permute-start(bf16[192,512]{1,0:T(8,128)(2,1)} %pad_maximum_fusion.55), channel_id=1, source_target_pairs={{2,0},{3,1},{0,2},{1,3},{6,4},{7,5},{4,6},{5,7},{10,8},{11,9},{8,1... | collective-permute-start | bytes 589832 | tf_op jit(solution)/shard_map/ppermute | solution.py:276
  177.4 121.7 %collective-permute-start.4 = (f32[8,512]{1,0:T(8,128)}, f32[8,512]{1,0:T(8,128)S(1)}, u32[]{:S(2)}, u32[]{:S(2)}) collective-permute-start(f32[8,512]{1,0:T(8,128)} %pad_maximum_fusion.79), channel_id=1, source_target_pairs={{2,0},{3,1},{0,2},{1,3},{6,4},{7,5},{4,6},{5,7},{10,8},{11,9},{8,1... | collective-permute-start | bytes 49160 | tf_op jit(solution)/shard_map/ppermute | solution.py:276
  234.7 103.2 %collective-permute-start.5 = (bf16[2,2,256,256]{3,2,1,0:T(8,128)(2,1)S(1)}, bf16[2,2,256,256]{3,2,1,0:T(8,128)(2,1)}, u32[]{:S(2)}, u32[]{:S(2)}) collective-permute-start(bf16[2,2,256,256]{3,2,1,0:T(8,128)(2,1)S(1)} %get-tuple-element.115), channel_id=1, source_target_pairs={{2,0},{3,1},{0,2},{1,3},{6,4},{7,5},{4,6},{5,7},{10,8},{11,9},{8,1... | collective-permute-start | bytes 1572872 | tf_op jit(solution)/shard_map/ppermute | solution.py:276
  239.1 189.2 %collective-permute-start.15 = (bf16[192,1152]{1,0:T(8,128)(2,1)}, bf16[192,1152]{1,0:T(8,128)(2,1)}, u32[]{:S(2)}, u32[]{:S(2)}) collective-permute-start(bf16[192,1152]{1,0:T(8,128)(2,1)} %pad_maximum_fusion.45), channel_id=1, source_target_pairs={{2,0},{3,1},{0,2},{1,3},{6,4},{7,5},{4,6},{5,7},{10,8},{11,9},{8,1... | collective-permute-start | bytes 1327112 | tf_op jit(solution)/shard_map/ppermute | solution.py:276
  290.4 311.0 %all-to-all-start.3 = ((bf16[4,256,384]{2,1,0:T(8,128)(2,1)}), bf16[4,256,384]{2,1,0:T(8,128)(2,1)}, u32[]{:S(2)}, u32[]{:S(2)}) async-start(bf16[4,256,384]{2,1,0:T(8,128)(2,1)} %bitcast.677), calls=%async_computation.3 | async-start | bytes 1572864 | tf_op jit(solution)/shard_map/all_to_all | solution.py:307
  294.6 377.6 %all-gather.23.cloned.1.call-start = ((), (), s32[]{:S(2)}) async-start(), calls=%async_computation.12 | async-start | bytes 7962624 | tf_op jit(solution)/shard_map/all_gather | solution.py:562
  299.1 207.7 %collective-permute-start.20 = (bf16[192,512]{1,0:T(8,128)(2,1)}, bf16[192,512]{1,0:T(8,128)(2,1)}, u32[]{:S(2)}, u32[]{:S(2)}) collective-permute-start(bf16[192,512]{1,0:T(8,128)(2,1)} %pad_maximum_fusion.58), channel_id=1, source_target_pairs={{2,0},{3,1},{0,2},{1,3},{6,4},{7,5},{4,6},{5,7},{10,8},{11,9},{8,1... | collective-permute-start | bytes 589832 | tf_op jit(solution)/shard_map/ppermute | solution.py:276
  301.6 196.8 %collective-permute-start.22 = (f32[8,512]{1,0:T(8,128)}, f32[8,512]{1,0:T(8,128)}, u32[]{:S(2)}, u32[]{:S(2)}) collective-permute-start(f32[8,512]{1,0:T(8,128)} %pad_maximum_fusion.80), channel_id=1, source_target_pairs={{2,0},{3,1},{0,2},{1,3},{6,4},{7,5},{4,6},{5,7},{10,8},{11,9},{8,1... | collective-permute-start | bytes 49160 | tf_op jit(solution)/shard_map/ppermute | solution.py:276
  329.5 209.3 %collective-permute-start.23 = (bf16[2,2,256,256]{3,2,1,0:T(8,128)(2,1)}, bf16[2,2,256,256]{3,2,1,0:T(8,128)(2,1)}, u32[]{:S(2)}, u32[]{:S(2)}) collective-permute-start(bf16[2,2,256,256]{3,2,1,0:T(8,128)(2,1)} %get-tuple-element.114), channel_id=1, source_target_pairs={{2,0},{3,1},{0,2},{1,3},{6,4},{7,5},{4,6},{5,7},{10,8},{11,9},{8,1... | collective-permute-start | bytes 1572872 | tf_op jit(solution)/shard_map/ppermute | solution.py:276
  428.3 171.9 %collective-permute-start.33 = (bf16[192,1152]{1,0:T(8,128)(2,1)}, bf16[192,1152]{1,0:T(8,128)(2,1)}, u32[]{:S(2)}, u32[]{:S(2)}) collective-permute-start(bf16[192,1152]{1,0:T(8,128)(2,1)} %pad_maximum_fusion.46), channel_id=1, source_target_pairs={{2,0},{3,1},{0,2},{1,3},{6,4},{7,5},{4,6},{5,7},{10,8},{11,9},{8,1... | collective-permute-start | bytes 1327112 | tf_op jit(solution)/shard_map/ppermute | solution.py:276
  709.6 80.6 %collective-permute-start.59 = (bf16[192,1152]{1,0:T(8,128)(2,1)}, bf16[192,1152]{1,0:T(8,128)(2,1)}, u32[]{:S(2)}, u32[]{:S(2)}) collective-permute-start(bf16[192,1152]{1,0:T(8,128)(2,1)} %slice.1225), channel_id=1, source_target_pairs={{0,2},{1,3},{2,0},{3,1},{4,6},{5,7},{6,4},{7,5},{8,10},{9,11},{10,... | collective-permute-start | bytes 1327112 | tf_op jit(solution)/shard_map/ppermute | solution.py:281
  799.3 181.9 %all-to-all-start.2 = ((bf16[256,4,384]{2,0,1:T(8,128)(2,1)}), bf16[256,4,384]{2,0,1:T(8,128)(2,1)}, u32[]{:S(2)}, u32[]{:S(2)}) async-start(bf16[256,4,384]{2,0,1:T(8,128)(2,1)} %bitcast.653), calls=%async_computation.2 | async-start | bytes 1572864 | tf_op jit(solution)/shard_map/all_to_all | solution.py:311
  985.4 134.8 %all-reduce.7.cloned.1.call-start = ((), (), s32[]{:S(2)}) async-start(), calls=%async_computation.14 | async-start | bytes 2555904 | tf_op jit(solution)/shard_map/psum | solution.py:630
  1060.3 201.9 %all-reduce.5.cloned.1.call-start = ((), (), s32[]{:S(2)}) async-start(), calls=%async_computation.13 | async-start | bytes 4718592 | tf_op jit(solution)/shard_map/psum | solution.py:629
  1086.5 186.4 %all-to-all-start.4 = ((f32[256,4,384]{2,0,1:T(8,128)}), f32[256,4,384]{2,0,1:T(8,128)S(1)}, u32[]{:S(2)}, u32[]{:S(2)}) async-start(f32[256,4,384]{2,0,1:T(8,128)} %bitcast.609), calls=%async_computation.4 | async-start | bytes 3145728 | tf_op jit(solution)/shard_map/all_to_all | solution.py:311
  (324 other events, 4846.6 us)
Sparse Core Ops, SparseCore 0:
  35.4 46.7 all-gather.8
  84.1 32.3 all-gather.10
  118.3 78.7 all-gather.12
  199.5 48.8 all-gather.14
  250.1 45.5 all-gather.16
  297.4 32.3 all-gather.18
  331.6 78.7 all-gather.20
  522.5 52.6 all-gather.22
  1060.4 59.7 all-reduce.6
  1127.3 134.9 all-reduce.4

commit v2 on v1

v2 whole, which is shorter than its diff:
```python
from functools import partial

import jax
import jax.numpy as jnp
from jax import lax
from jax.experimental import pallas as pl
from jax.experimental.pallas import tpu as pltpu
from jax.sharding import PartitionSpec as P

HS = 256
CONV = 4
LAYERS = 2
SEGS = 8

EPSILON = 1e-06
FLOAT = jnp.float32
BRAIN = jnp.bfloat16
VMEM_BYTES = 48 * 1024 * 1024
CURVE = 0.7978845608028654
CUBIC = 0.044715
LANES = 128
SLABS = HS // LANES
MESH = pl.DeviceIdType.MESH


def nn(left, right):
    return lax.dot_general(left, right, (((1,), (0,)), ((), ())), preferred_element_type=FLOAT)


def nt(left, right):
    return lax.dot_general(left, right, (((1,), (1,)), ((), ())), preferred_element_type=FLOAT)


def tn(left, right):
    return lax.dot_general(left, right, (((0,), (0,)), ((), ())), preferred_element_type=FLOAT)


def gelu_tanh(value):
    return 0.5 * value * (1.0 + jnp.tanh(CURVE * (value + CUBIC * value * value * value)))


def gelu_pair(value):
    square = value * value
    bend = jnp.tanh(CURVE * value * (1.0 + CUBIC * square))
    half = 0.5 * (1.0 + bend)
    slope = half + 0.5 * value * (1.0 - bend * bend) * CURVE * (1.0 + 3.0 * CUBIC * square)
    return value * half, slope


def one_less_square(twice, square):
    series = -twice * (
        1.0 + twice * (0.5 + twice * (1.0 / 6.0 + twice * (1.0 / 24.0 + twice * (1.0 / 120.0))))
    )
    return jnp.where(twice > -0.1, series, 1.0 - square)


def gate_values(conv, gate_w, gate_b, soft):
    rate = jax.nn.sigmoid(nn(conv, gate_w[0]) + gate_b[0:1])
    inward = jax.nn.sigmoid(nn(conv, gate_w[1]) + gate_b[1:2])
    log_decay = (-8.0 * soft) * rate
    raw = jnp.exp(log_decay)
    gap = one_less_square(2.0 * log_decay, raw * raw)
    return rate, inward, raw, gap


def chain(axis_row="row", axis_col="col"):
    blocks_in_row = lax.axis_size(axis_col) // 2
    blocks = lax.axis_size(axis_row) * blocks_in_row
    col = lax.axis_index(axis_col)
    side = col % 2
    here = lax.axis_index(axis_row) * blocks_in_row + col // 2

    def device(by):
        block = (here + by + blocks) % blocks
        return (block // blocks_in_row, (block % blocks_in_row) * 2 + side)

    return blocks, blocks_in_row, here, side, device


def greet(blocks, device):
    barrier = pltpu.get_barrier_semaphore()
    for by in range(1, blocks):
        pl.semaphore_signal(barrier, inc=1, device_id=device(by), device_id_type=MESH)
    pl.semaphore_wait(barrier, blocks - 1)


def share_totals(blocks, device, direction, totals, inbox, send_sems, recv_sems):
    copies = [
        pltpu.make_async_remote_copy(
            src_ref=totals,
            dst_ref=inbox.at[by - 1],
            send_sem=send_sems.at[by - 1],
            recv_sem=recv_sems.at[by - 1],
            device_id=device(direction * by),
            device_id_type=MESH,
        )
        for by in range(1, blocks)
    ]
    for copy in copies:
        copy.start()
    for copy in copies:
        copy.wait()


def folded(blocks, shards, ahead, direction, inbox):
    slabs = inbox.shape[1] // 2
    piece = slabs // shards
    state = jnp.zeros((slabs, LANES), FLOAT)
    for by in reversed(range(1, blocks)):
        turn = (direction * by) % shards * piece
        cum, add = (
            jnp.concatenate([part[turn:], part[:turn]], axis=0) if turn else part
            for part in (inbox[by - 1, 0:slabs], inbox[by - 1, slabs : 2 * slabs])
        )
        state = jnp.where(ahead >= by, cum * state + add, state)
    return state


def forward_kernel(
    lead, gate, offset, conv_w, conv_b, gate_w, gate_b, soft,
    conv_out, decay_out, hidden_out, mixed_out, carry_out,
    ext, drive, state_all, cum_all, seg, totals, halo, inbox,
    halo_sems, send_sems, recv_sems,
):
    rows, width = lead.shape
    heads = width // HS
    half = rows // 2
    span = rows // SEGS
    slabs = width // LANES
    blocks, shards, here, side, device = chain()
    start = pl.multiple_of(side * half, half)
    other = pl.multiple_of(half - side * half, half)
    greet(blocks, device)
    rim = pltpu.make_async_remote_copy(
        src_ref=lead.at[pl.ds(pl.multiple_of(other + half - 8, 8), 8)],
        dst_ref=halo,
        send_sem=halo_sems.at[0],
        recv_sem=halo_sems.at[1],
        device_id=device(1),
        device_id_type=MESH,
    )
    rim.start()
    rim.wait()

    def run_head(head, nothing):
        at = pl.ds(pl.multiple_of(head * HS, HS), HS)
        there = (head + heads // shards) % heads
        ext[0:8] = halo[:, pl.ds(pl.multiple_of(there * HS, HS), HS)]
        ext[8 : 8 + half] = lead[pl.ds(start, half), at]
        ext[8 + half : 8 + rows] = lead[pl.ds(other, half), at]
        place = offset[...]
        total = conv_b[:, at] + conv_w[0:1, at] * ext[8 : 8 + rows]
        for step in range(1, CONV):
            valid = (place >= step).astype(FLOAT)
            total = total + conv_w[step : step + 1, at] * ext[8 - step : 8 - step + rows] * valid
        conv = total.astype(BRAIN)
        conv_out[:, at] = conv
        rate, inward, raw, gap = gate_values(
            conv, (gate_w[0, head], gate_w[1, head]), gate_b[:, at], soft[:, at]
        )
        first = (place == 0).astype(FLOAT)
        keep = 1.0 - first
        decay = raw * keep
        pushed = (keep * jnp.sqrt(gap) + first) * inward * conv.astype(FLOAT)
        for slab in range(SLABS):
            decay_out[head * SLABS + slab] = decay[:, slab * LANES : (slab + 1) * LANES]
            drive[slab] = pushed[:, slab * LANES : (slab + 1) * LANES]

        def advance(step, carried):
            where = pl.ds(step, SEGS, stride=span)
            after = []
            for slab, (state, cum) in enumerate(carried):
                rates = decay_out[head * SLABS + slab, where, :]
                state = rates * state + drive[slab, where, :]
                cum = rates * cum
                state_all[head * SLABS + slab, where, :] = state
                cum_all[head * SLABS + slab, where, :] = cum
                after.append((state, cum))
            return tuple(after)

        fresh = (jnp.zeros((SEGS, LANES), FLOAT), jnp.ones((SEGS, LANES), FLOAT))
        ends = lax.fori_loop(0, span, advance, (fresh,) * SLABS, unroll=8)
        for slab, (state, cum) in enumerate(ends):
            run_state = jnp.zeros((1, LANES), FLOAT)
            run_cum = jnp.ones((1, LANES), FLOAT)
            at_slab = head * SLABS + slab
            for part in range(SEGS):
                seg[at_slab, part : part + 1] = run_state
                seg[at_slab, SEGS + part : SEGS + part + 1] = run_cum
                run_state = cum[part : part + 1] * run_state + state[part : part + 1]
                run_cum = cum[part : part + 1] * run_cum
            totals[pl.ds(at_slab, 1)] = run_cum
            totals[pl.ds(slabs + at_slab, 1)] = run_state
        return nothing

    lax.fori_loop(0, heads, run_head, 0)
    share_totals(blocks, device, 1, totals, inbox, send_sems, recv_sems)
    carry_out[...] = folded(blocks, shards, here, 1, inbox)

    def mix_slab(slab, nothing):
        at = pl.ds(pl.multiple_of(slab * LANES, LANES), LANES)
        entering = seg[slab, 0:SEGS] + seg[slab, SEGS : 2 * SEGS] * carry_out[pl.ds(slab, 1)]
        for part in range(SEGS):
            lines = slice(part * span, (part + 1) * span)
            hidden_out[slab, lines] = (
                state_all[slab, lines] + cum_all[slab, lines] * entering[part : part + 1]
            )
        for place, lines in ((start, slice(0, half)), (other, slice(half, rows))):
            mixed_out[pl.ds(place, half), at] = (
                hidden_out[slab, lines] * gelu_tanh(gate[pl.ds(place, half), at])
            ).astype(BRAIN)
        return nothing

    lax.fori_loop(0, slabs, mix_slab, 0)


def backward_kernel(
    grad, gate, hidden, decay, carry, conv, offset, conv_w, gate_w, gate_b, soft,
    branch_grad,
    ext, prior, grads, chain_decay, local_all, reach_all, seg, totals, arriving, heads_out,
    heads_in, tails, inbox, halo_sems, send_sems, recv_sems,
):
    rows, width = grad.shape
    heads = width // HS
    half = rows // 2
    span = rows // SEGS
    slabs = width // LANES
    blocks, shards, here, side, device = chain()
    start = pl.multiple_of(side * half, half)
    other = pl.multiple_of(half - side * half, half)
    greet(blocks, device)

    def run_slab(slab, nothing):
        at = pl.ds(pl.multiple_of(slab * LANES, LANES), LANES)
        gate_at = pl.ds(pl.multiple_of(width + slab * LANES, LANES), LANES)
        for place, lines in ((start, slice(0, half)), (other, slice(half, rows))):
            value, slope = gelu_pair(gate[pl.ds(place, half), at])
            coming = grad[pl.ds(place, half), at]
            grads[lines] = coming * value
            branch_grad[pl.ds(place, half), gate_at] = (
                coming * hidden[slab, lines] * slope
            ).astype(BRAIN)
        chain_decay[0:rows] = decay[slab]
        chain_decay[rows : rows + 8] = jnp.ones((8, LANES), FLOAT)

        def retreat(turn, carried):
            state, cum = carried
            step = span - 1 - turn
            where = pl.ds(step, SEGS, stride=span)
            rates = chain_decay[pl.ds(step + 1, SEGS, stride=span), :]
            state = rates * state + grads[where, :]
            cum = rates * cum
            local_all[slab, where, :] = state
            reach_all[slab, where, :] = cum
            return state, cum

        fresh = (jnp.zeros((SEGS, LANES), FLOAT), jnp.ones((SEGS, LANES), FLOAT))
        state, cum = lax.fori_loop(0, span, retreat, fresh, unroll=8)
        run_state = jnp.zeros((1, LANES), FLOAT)
        run_cum = jnp.ones((1, LANES), FLOAT)
        for part in reversed(range(SEGS)):
            seg[slab, part : part + 1] = run_state
            seg[slab, SEGS + part : SEGS + part + 1] = run_cum
            run_state = cum[part : part + 1] * run_state + state[part : part + 1]
            run_cum = cum[part : part + 1] * run_cum
        opening = chain_decay[0:1]
        totals[pl.ds(slab, 1)] = run_cum * opening
        totals[pl.ds(slabs + slab, 1)] = run_state * opening
        return nothing

    lax.fori_loop(0, slabs, run_slab, 0)
    share_totals(blocks, device, -1, totals, inbox, send_sems, recv_sems)
    arriving[...] = folded(blocks, shards, blocks - 1 - here, -1, inbox)

    def run_head(head, nothing):
        at = pl.ds(pl.multiple_of(head * HS, HS), HS)
        for slab in range(SLABS):
            slot = head * SLABS + slab
            lanes = slice(slab * LANES, (slab + 1) * LANES)
            entering = seg[slot, 0:SEGS] + seg[slot, SEGS : 2 * SEGS] * arriving[pl.ds(slot, 1)]
            for part in range(SEGS):
                lines = slice(part * span, (part + 1) * span)
                ext[lines, lanes] = (
                    local_all[slot, lines] + reach_all[slot, lines] * entering[part : part + 1]
                )
            prior[7:8, lanes] = carry[pl.ds(slot, 1)]
            prior[8 : 8 + rows, lanes] = hidden[slot]
        carried = ext[0:rows]
        before = prior[7 : 7 + rows]
        low = conv[:, at]
        value = low.astype(FLOAT)
        place = offset[...]
        first = (place == 0).astype(FLOAT)
        keep = 1.0 - first
        softness = soft[:, at]
        weights = (gate_w[0, head], gate_w[1, head])
        rate, inward, raw, gap = gate_values(low, weights, gate_b[:, at], softness)
        root = jnp.sqrt(gap)
        scale = keep * root + first
        pushed = carried * inward
        log_grad = keep * raw * (carried * before - pushed * value * (raw / root))
        rate_grad = ((-8.0 * softness) * log_grad * rate * (1.0 - rate)).astype(BRAIN)
        scaled = carried * scale
        input_grad = (scaled * value * inward * (1.0 - inward)).astype(BRAIN)
        conv_grad = scaled * inward + nt(rate_grad, weights[0]) + nt(input_grad, weights[1])
        ext[rows : rows + 8] = jnp.zeros((8, HS), FLOAT)
        total = conv_w[0:1, at] * conv_grad
        head_sum = jnp.zeros((8, HS), FLOAT)
        lines = lax.broadcasted_iota(jnp.int32, (8, 1), 0)
        for step in range(1, CONV):
            term = conv_w[step : step + 1, at] * conv_grad * (place >= step).astype(FLOAT)
            ext[0:rows] = term
            total = total + ext[step : step + rows]
            moved = pltpu.roll(term[0:8], 8 - step, 0)
            head_sum = head_sum + jnp.where(lines >= 8 - step, moved, 0.0)
        heads_out[:, at] = head_sum
        tails[:, at] = total[rows - 8 : rows]
        branch_grad[pl.ds(start, half), at] = total[0:half].astype(BRAIN)
        branch_grad[pl.ds(other, half), at] = total[half:rows].astype(BRAIN)
        return nothing

    lax.fori_loop(0, heads, run_head, 0)
    rim = pltpu.make_async_remote_copy(
        src_ref=heads_out,
        dst_ref=heads_in,
        send_sem=halo_sems.at[0],
        recv_sem=halo_sems.at[1],
        device_id=device(-1),
        device_id_type=MESH,
    )
    rim.start()
    rim.wait()
    followed = jnp.where(here < blocks - 1, 1.0, 0.0)
    for head in range(heads):
        at = slice(head * HS, (head + 1) * HS)
        there = (head - heads // shards) % heads
        whole = tails[:, at] + heads_in[:, there * HS : (there + 1) * HS] * followed
        kept = branch_grad[pl.ds(pl.multiple_of(other + half - 16, 16), 16), at]
        tails_pair = jnp.concatenate([kept[0:8], whole.astype(BRAIN)], axis=0)
        branch_grad[pl.ds(pl.multiple_of(other + half - 16, 16), 16), at] = tails_pair


def block_call(kernel, ident, operands, outs, scratch):
    whole = pl.BlockSpec(memory_space=pltpu.VMEM)
    return pl.pallas_call(
        kernel,
        out_shape=[jax.ShapeDtypeStruct(*out) for out in outs],
        in_specs=[whole] * len(operands),
        out_specs=[whole] * len(outs),
        scratch_shapes=scratch,
        compiler_params=pltpu.CompilerParams(
            vmem_limit_bytes=VMEM_BYTES, collective_id=ident, has_side_effects=True
        ),
    )(*operands)


def message_scratch(width):
    others = lax.axis_size("row") * lax.axis_size("col") // 2 - 1
    slabs = width // LANES
    return [
        pltpu.VMEM((others, 2 * slabs, LANES), FLOAT),
        pltpu.SemaphoreType.DMA((2,)),
        pltpu.SemaphoreType.DMA((others,)),
        pltpu.SemaphoreType.DMA((others,)),
    ]


def recur_forward(lead, gate, offset, small):
    rows, width = lead.shape
    slabs = width // LANES
    stack = (slabs, rows, LANES)
    return block_call(
        forward_kernel,
        0,
        [lead, gate, offset, small["conv_weight"], small["conv_bias"], small["gate_weight"],
         small["gate_bias"], small["soft"]],
        [((rows, width), BRAIN), (stack, FLOAT), (stack, FLOAT), ((rows, width), BRAIN),
         ((slabs, LANES), FLOAT)],
        [
            pltpu.VMEM((rows + 8, HS), FLOAT),
            pltpu.VMEM((SLABS, rows, LANES), FLOAT),
            pltpu.VMEM(stack, FLOAT),
            pltpu.VMEM(stack, FLOAT),
            pltpu.VMEM((slabs, 2 * SEGS, LANES), FLOAT),
            pltpu.VMEM((2 * slabs, LANES), FLOAT),
            pltpu.VMEM((8, width), FLOAT),
        ]
        + message_scratch(width),
    )


def recur_backward(grad, kept, offset, small):
    rows, width = grad.shape
    slabs = width // LANES
    stack = (slabs, rows, LANES)
    return block_call(
        backward_kernel,
        1,
        [grad, kept["gate"], kept["hidden"], kept["decay"], kept["state_in"], kept["conv"], offset,
         small["conv_weight"], small["gate_weight"], small["gate_bias"], small["soft"]],
        [((rows, 2 * width), BRAIN)],
        [
            pltpu.VMEM((rows + 8, HS), FLOAT),
            pltpu.VMEM((rows + 8, HS), FLOAT),
            pltpu.VMEM((rows, LANES), FLOAT),
            pltpu.VMEM((rows + 8, LANES), FLOAT),
            pltpu.VMEM(stack, FLOAT),
            pltpu.VMEM(stack, FLOAT),
            pltpu.VMEM((slabs, 2 * SEGS, LANES), FLOAT),
            pltpu.VMEM((2 * slabs, LANES), FLOAT),
            pltpu.VMEM((slabs, LANES), FLOAT),
            pltpu.VMEM((8, width), FLOAT),
            pltpu.VMEM((8, width), FLOAT),
            pltpu.VMEM((8, width), FLOAT),
        ]
        + message_scratch(width),
    )[0]


def partner(value):
    peers = lax.axis_size("col")
    return lax.ppermute(value, "col", [(at, at ^ 1) for at in range(peers)])


def from_shard(value, turn):
    peers = lax.axis_size("col")
    return lax.ppermute(value, "col", [((at + 2 * turn) % peers, at) for at in range(peers)])


def to_shard(value, turn):
    peers = lax.axis_size("col")
    return lax.ppermute(value, "col", [(at, (at + 2 * turn) % peers) for at in range(peers)])


def all_shards(value):
    return [value] + [from_shard(value, turn) for turn in range(1, lax.axis_size("col") // 2)]


def after(value, anchor):
    return value if anchor is None else lax.optimization_barrier((value, anchor))[0]


def whole_width(value):
    peers = lax.axis_size("col")
    parts = [value] + [
        lax.ppermute(value, "col", [((at + turn) % peers, at) for at in range(peers)])
        for turn in range(1, peers)
    ]
    stacked = jnp.roll(jnp.stack(parts), lax.axis_index("col"), axis=0)
    return jnp.moveaxis(stacked, 0, -2).reshape(value.shape[:-1] + (-1,))


def to_sequence(value):
    return lax.all_to_all(value, "col", split_axis=0, concat_axis=1, tiled=True)


def from_sequence(value):
    return lax.all_to_all(value, "col", split_axis=1, concat_axis=0, tiled=True)


def both_halves(value):
    return jnp.concatenate([value, partner(value)], axis=0)


def half_share(own, other):
    return own + partner(other.astype(BRAIN)).astype(FLOAT)


def norm_forward(stream, gain):
    scale = lax.rsqrt(jnp.mean(stream * stream, axis=1, keepdims=True) + EPSILON)
    return scale, (stream * scale * gain[None, :]).astype(BRAIN)


def norm_backward(stream, scale, gain, d_normed):
    gained = d_normed * gain[None, :]
    total = jnp.mean(gained * stream, axis=1, keepdims=True)
    return scale * gained - stream * (scale * scale * scale * total)


def masked(value, pick):
    return (value * pick).astype(BRAIN)


def recur_part(stream, wide, small, gains, ctx):
    inlet, outlet = wide
    pick, offset = ctx["pick"], ctx["offset"]
    ranks = pick.shape[1]
    own = stream.shape[0]
    rows = 2 * own
    width = outlet.shape[1]

    scale_one, normed = norm_forward(stream, gains[0])
    normed_full = both_halves(normed)
    low = nt(normed_full, small["inlet_lower"])
    inner = [masked(low[:, b * ranks : (b + 1) * ranks], pick) for b in range(2)]
    branch = nn(normed_full, inlet)
    lead = branch[:, :width] + nn(inner[0], small["inlet_upper"][0])
    gate = branch[:, width:] + nn(inner[1], small["inlet_upper"][1])
    conv, decay, hidden, mixed, state_in = recur_forward(lead, gate, offset, small)
    lowrank = masked(nt(mixed, small["outlet_lower"]), pick)

    def outward(part):
        return nt(mixed[part], outlet) + nn(lowrank[part], small["outlet_upper"])

    middle = stream + half_share(outward(slice(0, own)), outward(slice(own, rows)))
    kept = dict(
        stream=stream, scale_one=scale_one, normed_full=normed_full, inner=inner, lead=lead,
        gate=gate, conv=conv, decay=decay, hidden=hidden, state_in=state_in, mixed=mixed,
        lowrank=lowrank, middle=middle,
    )
    return middle, kept


def hidden_part(middle, wide, small, gains, ctx):
    expand, shrink = wide
    pick = ctx["pick"]
    ranks = pick.shape[1]
    own = middle.shape[0]
    rows = 2 * own
    spread = shrink.shape[1]
    scale_two, normed_two = norm_forward(middle, gains[1])
    normed_two_full = both_halves(normed_two)
    low_two = nt(normed_two_full, small["expand_lower"])
    inner_two = [masked(low_two[:, b * ranks : (b + 1) * ranks], pick) for b in range(2)]
    branch_two = nn(normed_two_full, expand)
    up_gate = branch_two[:, :spread] + nn(inner_two[0], small["expand_upper"][0])
    up_value = branch_two[:, spread:] + nn(inner_two[1], small["expand_upper"][1])
    product = (gelu_tanh(up_gate) * up_value).astype(BRAIN)
    lowrank_two = masked(nt(product, small["shrink_lower"]), pick)

    def downward(part):
        return nt(product[part], shrink) + nn(lowrank_two[part], small["shrink_upper"])

    result = middle + half_share(downward(slice(0, own)), downward(slice(own, rows)))
    kept = dict(
        scale_two=scale_two, normed_two_full=normed_two_full, inner_two=inner_two,
        up_gate=up_gate, up_value=up_value, product=product, lowrank_two=lowrank_two,
    )
    return result, kept


def layer_backward(d_stream, wide, small, gains, kept, ctx):
    inlet, outlet, expand, shrink = wide
    pick, offset = ctx["pick"], ctx["offset"]
    own = d_stream.shape[0]
    rows = 2 * own
    width = outlet.shape[1]
    spread = shrink.shape[1]

    d_out = both_halves(d_stream.astype(BRAIN))
    d_low_two = masked(nt(d_out, small["shrink_upper"]), pick)
    d_product = nn(d_out, shrink) + nn(d_low_two, small["shrink_lower"])
    shrink_upper_grad = tn(kept["lowrank_two"], d_out)
    shrink_lower_grad = tn(d_low_two, kept["product"])
    value, slope = gelu_pair(kept["up_gate"])
    d_branch_two = jnp.concatenate(
        [(slope * kept["up_value"] * d_product).astype(BRAIN), (value * d_product).astype(BRAIN)],
        axis=1,
    )
    d_inner_two = jnp.concatenate(
        [
            masked(nt(d_branch_two[:, b * spread : (b + 1) * spread], small["expand_upper"][b]), pick)
            for b in range(2)
        ],
        axis=1,
    )

    def inward_two(part):
        return nt(d_branch_two[part], expand) + nn(d_inner_two[part], small["expand_lower"])

    d_normed_two = half_share(inward_two(slice(0, own)), inward_two(slice(own, rows)))
    expand_lower_grad = tn(d_inner_two, kept["normed_two_full"])
    expand_upper_grad = jnp.concatenate(
        [
            tn(kept["inner_two"][b], d_branch_two[:, b * spread : (b + 1) * spread])
            for b in range(2)
        ],
        axis=0,
    )
    d_middle = d_stream + norm_backward(kept["middle"], kept["scale_two"], gains[1], d_normed_two)

    d_mid = both_halves(d_middle.astype(BRAIN))
    d_low = masked(nt(d_mid, small["outlet_upper"]), pick)
    d_mixed = nn(d_mid, outlet) + nn(d_low, small["outlet_lower"])
    outlet_upper_grad = tn(kept["lowrank"], d_mid)
    outlet_lower_grad = tn(d_low, kept["mixed"])
    d_branch = recur_backward(d_mixed, kept, offset, small)
    d_inner = jnp.concatenate(
        [
            masked(nt(d_branch[:, b * width : (b + 1) * width], small["inlet_upper"][b]), pick)
            for b in range(2)
        ],
        axis=1,
    )

    def inward(part):
        return nt(d_branch[part], inlet) + nn(d_inner[part], small["inlet_lower"])

    d_normed = half_share(inward(slice(0, own)), inward(slice(own, rows)))
    inlet_lower_grad = tn(d_inner, kept["normed_full"])
    inlet_upper_grad = jnp.concatenate(
        [tn(kept["inner"][b], d_branch[:, b * width : (b + 1) * width]) for b in range(2)], axis=0
    )
    d_input = d_middle + norm_backward(kept["stream"], kept["scale_one"], gains[0], d_normed)
    shared = jnp.concatenate(
        [inlet_lower_grad, outlet_upper_grad, expand_lower_grad, shrink_upper_grad], axis=0
    )
    split = (
        jnp.concatenate([inlet_upper_grad, outlet_lower_grad], axis=0),
        jnp.concatenate([expand_upper_grad, shrink_lower_grad], axis=0),
    )
    return d_input, shared, split


def owned(grad, shards):
    piece = grad.shape[1] // shards
    parts = [grad[:, turn * piece : (turn + 1) * piece].astype(BRAIN) for turn in range(shards)]
    total = parts[0].astype(FLOAT)
    for turn in range(1, shards):
        total = total + to_shard(parts[turn], turn).astype(FLOAT)
    return total.astype(BRAIN)


def local(
    tokens, cotangent, adapter_ids, doc_lengths, norm_gain, inlet_weight, inlet_lower, inlet_upper,
    conv_weight, conv_bias, gate_weight, gate_bias, decay_param, outlet_weight, outlet_lower,
    outlet_upper, expand_weight, expand_lower, expand_upper, shrink_weight, shrink_lower,
    shrink_upper,
):
    row_at, col_at = lax.axis_index("row"), lax.axis_index("col")
    cols = lax.axis_size("col")
    shards = cols // 2
    rows = tokens.shape[0]
    own = rows // cols
    block = 2 * own
    docs = adapter_ids.shape[0]
    adapters, rank = inlet_lower.shape[3:]
    part_width, part_spread = inlet_weight.shape[3], expand_weight.shape[3]
    d_model = inlet_lower.shape[1]

    parity = (col_at % 2).astype(jnp.int32)
    ends = jnp.cumsum(doc_lengths)
    starts = ends - doc_lengths
    ordered = row_at * rows + (col_at // 2) * block + jnp.arange(block, dtype=jnp.int32)
    inside = (ordered[:, None] >= starts[None, :]) & (ordered[:, None] < ends[None, :])
    offset = (ordered - jnp.sum(jnp.where(inside, starts[None, :], 0), axis=1))[:, None]
    halves = (parity * own, own - parity * own)
    at_home = jnp.concatenate(
        [ordered[0] + begin + jnp.arange(own, dtype=jnp.int32) for begin in halves]
    )
    within = (at_home[:, None] >= starts[None, :]) & (at_home[:, None] < ends[None, :])
    pick = jnp.repeat(within.astype(FLOAT), rank, axis=1)
    ctx = dict(pick=pick, offset=offset)

    stream = to_sequence(tokens).astype(FLOAT)
    gains = whole_width(norm_gain)

    def by_doc(factor, axis):
        return jnp.concatenate(
            [lax.dynamic_slice_in_dim(factor, adapter_ids[at], 1, axis) for at in range(docs)], axis
        )

    def lower_t(factor):
        return by_doc(jnp.moveaxis(factor, 1, -1), factor.ndim - 3)

    def upper_t(factor):
        return by_doc(factor, factor.ndim - 3)

    ranks = docs * rank
    lows = dict(
        inlet_lower=lower_t(inlet_lower).reshape(LAYERS, 2 * ranks, d_model),
        outlet_upper=upper_t(outlet_upper).reshape(LAYERS, ranks, d_model),
        expand_lower=lower_t(expand_lower).reshape(LAYERS, 2 * ranks, d_model),
        shrink_upper=upper_t(shrink_upper).reshape(LAYERS, ranks, d_model),
    )
    narrow_own = jnp.concatenate(
        [
            upper_t(inlet_upper).reshape(LAYERS, 2 * ranks, part_width),
            lower_t(outlet_lower).reshape(LAYERS, ranks, part_width),
        ],
        axis=1,
    )
    broad_own = jnp.concatenate(
        [
            upper_t(expand_upper).reshape(LAYERS, 2 * ranks, part_spread),
            lower_t(shrink_lower).reshape(LAYERS, ranks, part_spread),
        ],
        axis=1,
    )
    vectors_own = jnp.concatenate(
        [conv_weight, gate_bias, conv_bias[:, None], decay_param[:, None]], axis=1
    )

    def fetch(pair, single, anchor):
        piece = single.shape[1]
        pack = jnp.concatenate([pair[:, 0], pair[:, 1], single], axis=1)
        parts = all_shards(after(pack, anchor))
        columns = [part[:, at * piece : (at + 1) * piece] for at in range(3) for part in parts]
        whole = lax.all_gather(jnp.concatenate(columns, axis=1), "row", axis=0, tiled=True)
        cut = 2 * shards * piece
        return (whole[:, :cut], whole[:, cut:]), parts[-1]

    def recur_weights(layer, anchor):
        wide, last = fetch(inlet_weight[layer], outlet_weight[layer], anchor)
        narrow, vectors, gates = (
            jnp.concatenate(all_shards(after(value, last)), axis=1)
            for value in (narrow_own[layer], vectors_own[layer], gate_weight[layer])
        )
        small = dict(
            inlet_lower=lows["inlet_lower"][layer],
            inlet_upper=narrow[: 2 * ranks].reshape(2, ranks, -1),
            outlet_lower=narrow[2 * ranks :],
            outlet_upper=lows["outlet_upper"][layer],
            conv_weight=vectors[:CONV],
            gate_bias=vectors[CONV : CONV + 2],
            conv_bias=vectors[CONV + 2 : CONV + 3],
            soft=jax.nn.softplus(vectors[CONV + 3 : CONV + 4]),
            gate_weight=gates,
        )
        return wide, small, last

    def hidden_weights(layer, anchor):
        wide, last = fetch(expand_weight[layer], shrink_weight[layer], anchor)
        broad = jnp.concatenate(all_shards(after(broad_own[layer], last)), axis=1)
        small = dict(
            expand_lower=lows["expand_lower"][layer],
            expand_upper=broad[: 2 * ranks].reshape(2, ranks, -1),
            shrink_lower=broad[2 * ranks :],
            shrink_upper=lows["shrink_upper"][layer],
        )
        return wide, small, last

    outputs, saved, wides, smalls = [], [], [], []
    anchor_one = anchor_two = None
    for layer in range(LAYERS):
        wide_one, small_one, last = recur_weights(layer, anchor_one)
        wide_two, small_two, _ = hidden_weights(layer, last if layer == 0 else anchor_two)
        middle, kept = recur_part(stream, wide_one, small_one, gains[layer], ctx)
        stream, more = hidden_part(middle, wide_two, small_two, gains[layer], ctx)
        anchor_one, anchor_two = kept["lead"], middle
        outputs.append(from_sequence(stream.astype(BRAIN)))
        saved.append({**kept, **more})
        wides.append(wide_one + wide_two)
        smalls.append({**small_one, **small_two})
    d_stream = to_sequence(cotangent).astype(FLOAT)
    shared, narrow, broad = [None] * LAYERS, [None] * LAYERS, [None] * LAYERS
    for layer in reversed(range(LAYERS)):
        d_stream, everywhere, split = layer_backward(
            d_stream, wides[layer], smalls[layer], gains[layer], saved[layer], ctx
        )
        shared[layer] = lax.psum(everywhere.astype(BRAIN), ("row", "col")).astype(FLOAT)
        narrow[layer] = lax.psum(owned(split[0], shards), "row").astype(FLOAT)
        broad[layer] = lax.psum(owned(split[1], shards), "row").astype(FLOAT)
    shared, narrow, broad = jnp.stack(shared), jnp.stack(narrow), jnp.stack(broad)
    spread_out = (adapter_ids[None, :] == jnp.arange(adapters, dtype=jnp.int32)[:, None])

    def by_adapter(grad, count):
        grad = grad.reshape(LAYERS, count, docs, rank, -1)
        total = 0.0
        for doc in range(docs):
            total = total + jnp.where(
                spread_out[None, None, :, doc, None, None], grad[:, :, doc][:, :, None], 0.0
            )
        return total

    def lower_out(grad, count):
        grad = by_adapter(grad, count)
        if count == 1:
            grad = grad[:, 0]
        return jnp.moveaxis(grad, -1, 1)

    return (
        jnp.stack(outputs, axis=0),
        from_sequence(d_stream),
        lower_out(shared[:, : 2 * ranks], 2),
        by_adapter(narrow[:, : 2 * ranks], 2),
        lower_out(narrow[:, 2 * ranks :], 1),
        by_adapter(shared[:, 2 * ranks : 3 * ranks], 1)[:, 0],
        lower_out(shared[:, 3 * ranks : 5 * ranks], 2),
        by_adapter(broad[:, : 2 * ranks], 2),
        lower_out(broad[:, 2 * ranks :], 1),
        by_adapter(shared[:, 5 * ranks :], 1)[:, 0],
    )


def solution(mesh):
    return jax.shard_map(
        local,
        mesh=mesh,
        in_specs=(
            P("row", "col"),
            P("row", "col"),
            P(),
            P(),
            P(None, None, "col"),
            P(None, "row", None, "col"),
            P(),
            P(None, None, None, None, "col"),
            P(None, None, "col"),
            P(None, "col"),
            P(None, None, "col", None, None),
            P(None, None, "col"),
            P(None, "col"),
            P(None, "row", "col"),
            P(None, "col", None, None),
            P(),
            P(None, "row", None, "col"),
            P(),
            P(None, None, None, None, "col"),
            P(None, "row", "col"),
            P(None, "col", None, None),
            P(),
        ),
        out_specs=(
            P(None, "row", "col"),
            P("row", "col"),
            P(),
            P(None, None, None, None, "col"),
            P(None, "col", None, None),
            P(),
            P(),
            P(None, None, None, None, "col"),
            P(None, "col", None, None),
            P(),
        ),
        check_vma=False,
    )
```

time: 1290 us -> 1190 us (0.922)
  starting transfers between devices: 162 us -> 72.9 us
  Pallas kernels: 68.8 us -> 114 us
  blocking collectives: 38.4 us -> 0 us
  local copies, waits for them, and re-layouts: 74.8 us -> 51.5 us
  other arithmetic: 66.5 us -> 46.4 us
  waiting for transfers between devices: 604 us -> 621 us
    ppermute x24 -> x3, starting transfers between devices: 83.9 us -> 2.08 us  [whole_width(): lax.ppermute(value, 'col', [((at + turn) % peers, at) for at in range(pee...]
    ppermute x16 -> x12, waiting for transfers between devices: 178 us -> 246 us  [from_shard(): lax.ppermute(value, 'col', [((at + 2 * turn) % peers, at) for at in range...]
    ppermute x24 -> x3, waiting for transfers between devices: 57.4 us -> 0.01 us  [whole_width(): lax.ppermute(value, 'col', [((at + turn) % peers, at) for at in range(pee...]
    pallas_call x8 -> x4, Pallas kernels: 68.8 us -> 114 us  [block_call(): pl.pallas_call(kernel, out_shape=[jax.ShapeDtypeStruct(*out) for out in o...]
    all_gather x1 -> x0, blocking collectives: 38.4 us -> none  [local(): gains = lax.all_gather(norm_gain, 'col', axis=2, tiled=True)]
    concatenate x24 -> x5, other arithmetic: 18.9 us -> 1.11 us  [the longest x4 1.09 us: fetch(): pack = jnp.concatenate([pair[:, 0], pair[:, 1], single], axis=1)]
    dot_general x36, matrix products: 103 us -> 116 us  [nt(): lax.dot_general(left, right, (((1,), (1,)), ((), ())), preferred_element_...]
  transfers between devices with their start and end apart: 75 -> 46, of which waited for: 47 -> 29; matrix products, arithmetic and copies ran while one was open for 24% -> 23% of each run, Pallas kernels for 5% -> 7%
where the time goes in v2:
time: 1190 us; the launch traced here: 1180 us
  waiting for transfers between devices  621 us (52%)
  matrix products  249 us (21%)
  Pallas kernels  114 us (10%)
  starting transfers between devices  72.9 us (6%)
  local copies, waits for them, and re-layouts  51.5 us (4%)
  other arithmetic  46.4 us (4%)
  between operations  26.5 us (2%)
    ppermute x12, waiting for transfers between devices, from_shard(): lax.ppermute(value, 'col', [((at + 2 * turn) % peers, at) for at in range...  246 us
    ppermute x16, waiting for transfers between devices, partner(): return lax.ppermute(value, 'col', [(at, at ^ 1) for at in range(peers)])  183 us
    psum x1, waiting for transfers between devices, local(): lax.psum(everywhere.astype(BRAIN), ('row', 'col')).astype(FLOAT)  133 us
    dot_general x36, matrix products, nt(): lax.dot_general(left, right, (((1,), (1,)), ((), ())), preferred_element_...  116 us
    dot_general x36, matrix products, nn(): lax.dot_general(left, right, (((1,), (0,)), ((), ())), preferred_element_...  116 us
    pallas_call x4, Pallas kernels, block_call(): pl.pallas_call(kernel, out_shape=[jax.ShapeDtypeStruct(*out) for out in o...  114 us
  transfers between devices with their start and end apart: 46, of which 29 were waited for; matrix products, arithmetic and copies ran while one was open for 23% of the time, Pallas kernels for 7%

profile of v2, /device:TPU:0, one launch (start us, length us, event | category | flops | bytes accessed | tf_op | source)
XLA Modules:
  0.0 1181.5 jit_solution(6714497479161281601)
XLA Ops:
  13.3 25.9 %collective-permute-done.4 = bf16[192,1536]{1,0:T(8,128)(2,1)S(1)} collective-permute-done((bf16[192,1536]{1,0:T(8,128)(2,1)S(1)}, bf16[192,1536]{1,0:T(8,128)(2,1)S(1)}, u32[]{:S(2)}, u32[]{:S(2)}) %collective-permute-start.4) | collective-permute-done | bytes 589856 | tf_op jit(solution)/shard_map/ppermute | solution.py:427
  44.0 59.6 %collective-permute-done.10 = bf16[192,3456]{1,0:T(8,128)(2,1)S(1)} collective-permute-done((bf16[192,3456]{1,0:T(8,128)(2,1)S(1)}, bf16[192,3456]{1,0:T(8,128)(2,1)S(1)}, u32[]{:S(2)}, u32[]{:S(2)}) %collective-permute-start.10) | collective-permute-done | bytes 1327136 | tf_op jit(solution)/shard_map/ppermute | solution.py:427
  135.5 17.4 %collective-permute-done.5 = bf16[192,512]{1,0:T(8,128)(2,1)S(1)} collective-permute-done((bf16[192,512]{1,0:T(8,128)(2,1)S(1)}, bf16[192,512]{1,0:T(8,128)(2,1)S(1)}, u32[]{:S(2)}, u32[]{:S(2)}) %collective-permute-start.5) | collective-permute-done | bytes 196640 | tf_op jit(solution)/shard_map/ppermute | solution.py:427
  166.9 25.0 %collective-permute-done.14 = bf16[192,1536]{1,0:T(8,128)(2,1)S(1)} collective-permute-done((bf16[192,1536]{1,0:T(8,128)(2,1)S(1)}, bf16[192,1536]{1,0:T(8,128)(2,1)S(1)}, u32[]{:S(2)}, u32[]{:S(2)}) %collective-permute-start.14) | collective-permute-done | bytes 589856 | tf_op jit(solution)/shard_map/ppermute | solution.py:427
  227.8 25.2 %shard_map.285 = (bf16[512,1024]{1,0:T(8,128)(2,1)S(1)}, f32[8,512,128]{2,1,0:T(8,128)S(1)}, f32[8,512,128]{2,1,0:T(8,128)}, bf16[512,1024]{1,0:T(8,128)(2,1)S(1)}, f32[8,128]{1,0:T(8,128)S(1)}) custom-call(f32[512,1024]{1,0:T(8,128)} %slice_add_fusion.7.lead, f32[512,1024]{1,0:T(8,128)} %slice_add_fusion.6.gate, s32[512,1]{1,0:T(8,128)S(1)} %add_subtract_fusion.offset, ...), custom_call_target="tpu_custom_call" | custom-call | tf_op jit(solution)/shard_map/pallas_call | solution.py:345
  259.2 18.7 %collective-permute-done.8 = bf16[256,1536]{1,0:T(8,128)(2,1)S(1)} collective-permute-done((bf16[256,1536]{1,0:T(8,128)(2,1)S(1)}, bf16[256,1536]{1,0:T(8,128)(2,1)S(1)}, u32[]{:S(2)}, u32[]{:S(2)}) %collective-permute-start.8) | collective-permute-done | bytes 786464 | tf_op jit(solution)/shard_map/ppermute | solution.py:422
  284.9 56.9 %collective-permute-done.20 = bf16[192,3456]{1,0:T(8,128)(2,1)S(1)} collective-permute-done((bf16[192,3456]{1,0:T(8,128)(2,1)S(1)}, bf16[192,3456]{1,0:T(8,128)(2,1)S(1)}, u32[]{:S(2)}, u32[]{:S(2)}) %collective-permute-start.20) | collective-permute-done | bytes 1327136 | tf_op jit(solution)/shard_map/ppermute | solution.py:427
  360.4 29.5 %collective-permute-done.11 = bf16[192,1152]{1,0:T(8,128)(2,1)S(1)} collective-permute-done((bf16[192,1152]{1,0:T(8,128)(2,1)}, bf16[192,1152]{1,0:T(8,128)(2,1)S(1)}, u32[]{:S(2)}, u32[]{:S(2)}) %collective-permute-start.11) | collective-permute-done | bytes 442400 | tf_op jit(solution)/shard_map/ppermute | solution.py:427
  431.2 24.8 %collective-permute-done.12 = bf16[256,1536]{1,0:T(8,128)(2,1)} collective-permute-done((bf16[256,1536]{1,0:T(8,128)(2,1)}, bf16[256,1536]{1,0:T(8,128)(2,1)}, u32[]{:S(2)}, u32[]{:S(2)}) %collective-permute-start.12) | collective-permute-done | bytes 786464 | tf_op jit(solution)/shard_map/ppermute | solution.py:422
  472.0 17.1 %collective-permute-done.13 = bf16[256,1536]{1,0:T(8,128)(2,1)S(1)} collective-permute-done((bf16[256,1536]{1,0:T(8,128)(2,1)S(1)}, bf16[256,1536]{1,0:T(8,128)(2,1)S(1)}, u32[]{:S(2)}, u32[]{:S(2)}) %collective-permute-start.13) | collective-permute-done | bytes 786464 | tf_op jit(solution)/shard_map/ppermute | solution.py:422
  499.6 27.1 %shard_map.286 = (bf16[512,1024]{1,0:T(8,128)(2,1)S(1)}, f32[8,512,128]{2,1,0:T(8,128)S(1)}, f32[8,512,128]{2,1,0:T(8,128)}, bf16[512,1024]{1,0:T(8,128)(2,1)S(1)}, f32[8,128]{1,0:T(8,128)S(1)}) custom-call(f32[512,1024]{1,0:T(8,128)} %slice_add_fusion.5.lead, f32[512,1024]{1,0:T(8,128)} %slice_add_fusion.4.gate, s32[512,1]{1,0:T(8,128)S(1)} %add_subtract_fusion.offset, ...), custom_call_target="tpu_custom_call" | custom-call | tf_op jit(solution)/shard_map/pallas_call | solution.py:345
  540.2 21.7 %collective-permute-done.18 = bf16[256,1536]{1,0:T(8,128)(2,1)} collective-permute-done((bf16[256,1536]{1,0:T(8,128)(2,1)}, bf16[256,1536]{1,0:T(8,128)(2,1)}, u32[]{:S(2)}, u32[]{:S(2)}) %collective-permute-start.18) | collective-permute-done | bytes 786464 | tf_op jit(solution)/shard_map/ppermute | solution.py:422
  568.8 15.5 %collective-permute-done.19 = bf16[256,1536]{1,0:T(8,128)(2,1)S(1)} collective-permute-done((bf16[256,1536]{1,0:T(8,128)(2,1)S(1)}, bf16[256,1536]{1,0:T(8,128)(2,1)S(1)}, u32[]{:S(2)}, u32[]{:S(2)}) %collective-permute-start.19) | collective-permute-done | bytes 786464 | tf_op jit(solution)/shard_map/ppermute | solution.py:422
  589.2 13.3 %fusion.4 = f32[512,4608]{1,0:T(8,128)} fusion(bf16[1536,6912]{1,0:T(8,128)(2,1)} %all-gather.11.cloned.1.call-done, bf16[256,1536]{1,0:T(8,128)(2,1)} %copy-done.177, bf16[256,1536]{1,0:T(8,128)(2,1)} %copy-done.103), kind=kOutput, calls=%fused_computation.4 | convolution fusion | flops 7250903040 | bytes 25165824 | tf_op jit(solution)/shard_map/dot_general | solution.py:27
  607.9 13.4 %multiply_convert_fusion.3 = (bf16[512,2304]{1,0:T(8,128)(2,1)S(1)}, bf16[512,2304]{1,0:T(8,128)(2,1)S(1)}, bf16[512,2304]{1,0:T(8,128)(2,1)S(1)}) fusion(f32[512,2304]{1,0:T(8,128)} %slice_add_fusion.1, f32[512,2304]{1,0:T(8,128)} %fusion.227, f32[512,4608]{1,0:T(8,128)} %fusion.4, f32[512,2304]{1,0:T(8,128)} %fusion.223, ...), kind=kOutput, calls=%fused_computation.65 | convolution fusion | flops 3662807040 | bytes 34603008 | tf_op jit(solution)/shard_map/dot_general | solution.py:27
  657.8 13.9 %collective-permute-done.34 = bf16[192,1152]{1,0:T(8,128)(2,1)S(1)} collective-permute-done((bf16[192,1152]{1,0:T(8,128)(2,1)S(1)}, bf16[192,1152]{1,0:T(8,128)(2,1)S(1)}, u32[]{:S(2)}, u32[]{:S(2)}) %collective-permute-start.34) | collective-permute-done | bytes 442400 | tf_op jit(solution)/shard_map/ppermute | solution.py:432
  722.5 30.4 %shard_map.287 = bf16[512,2048]{1,0:T(8,128)(2,1)S(1)} custom-call(f32[512,1024]{1,0:T(8,128)} %fusion.171.grad, f32[512,1024]{1,0:T(8,128)} %slice_add_fusion.4.gate, f32[8,512,128]{2,1,0:T(8,128)} %get-tuple-element.44.hidden, f32[8,512,128]{2,1,0:T(8,128)} %copy-done.5, f32[8,128]{1,0:T(8,128)S(1)} %get-tuple-element.46.carry, ...), custom_call_target="tpu_custom_call" | custom-call | tf_op jit(solution)/shard_map/pallas_call | solution.py:345
  759.4 19.8 %collective-permute-done.26 = bf16[256,1536]{1,0:T(8,128)(2,1)S(1)} collective-permute-done((bf16[256,1536]{1,0:T(8,128)(2,1)S(1)}, bf16[256,1536]{1,0:T(8,128)(2,1)S(1)}, u32[]{:S(2)}, u32[]{:S(2)}) %collective-permute-start.26) | collective-permute-done | bytes 786464 | tf_op jit(solution)/shard_map/ppermute | solution.py:422
  790.0 12.1 %collective-permute-done.27 = bf16[256,1536]{1,0:T(8,128)(2,1)S(1)} collective-permute-done((bf16[256,1536]{1,0:T(8,128)(2,1)S(1)}, bf16[256,1536]{1,0:T(8,128)(2,1)S(1)}, u32[]{:S(2)}, u32[]{:S(2)}) %collective-permute-start.27) | collective-permute-done | bytes 786464 | tf_op jit(solution)/shard_map/ppermute | solution.py:422
  841.7 16.3 %collective-permute-done.28 = bf16[256,1536]{1,0:T(8,128)(2,1)} collective-permute-done((bf16[256,1536]{1,0:T(8,128)(2,1)}, bf16[256,1536]{1,0:T(8,128)(2,1)}, u32[]{:S(2)}, u32[]{:S(2)}) %collective-permute-start.28) | collective-permute-done | bytes 786464 | tf_op jit(solution)/shard_map/ppermute | solution.py:422
  917.7 31.3 %shard_map.288 = bf16[512,2048]{1,0:T(8,128)(2,1)S(1)} custom-call(f32[512,1024]{1,0:T(8,128)} %fusion.168.grad, f32[512,1024]{1,0:T(8,128)} %slice_add_fusion.6.gate, f32[8,512,128]{2,1,0:T(8,128)} %get-tuple-element.48.hidden, f32[8,512,128]{2,1,0:T(8,128)} %copy-done.4, f32[8,128]{1,0:T(8,128)S(1)} %get-tuple-element.50.carry, ...), custom_call_target="tpu_custom_call" | custom-call | tf_op jit(solution)/shard_map/pallas_call | solution.py:345
  973.1 14.7 %collective-permute-done.30 = bf16[256,1536]{1,0:T(8,128)(2,1)} collective-permute-done((bf16[256,1536]{1,0:T(8,128)(2,1)}, bf16[256,1536]{1,0:T(8,128)(2,1)}, u32[]{:S(2)}, u32[]{:S(2)}) %collective-permute-start.30) | collective-permute-done | bytes 786464 | tf_op jit(solution)/shard_map/ppermute | solution.py:422
  998.4 21.4 %all-reduce.7.cloned.1.call-done = (bf16[1,192,512]{2,1,0:T(8,128)(2,1)}, bf16[1,192,512]{2,1,0:T(8,128)(2,1)}, bf16[1,192,1152]{2,1,0:T(8,128)(2,1)}, bf16[1,192,1152]{2,1,0:T(8,128)(2,1)}) async-done(((bf16[1,192,512]{2,1,0:T(8,128)(2,1)}, bf16[1,192,512]{2,1,0:T(8,128)(2,1)}, bf16[1,192,1152]{2,1,0:T(8,128)(2,1)}, bf16[1,192,1152]{2,1,0:T(8,128)(2,1)}), (bf16[1,192,512]{2,1,0:T(8,128)(2,1)}, ...) | async-done | bytes 1277968 | tf_op jit(solution)/shard_map/psum | solution.py:752
  1029.1 133.4 %all-reduce.5.cloned.1.call-done = (bf16[1,384,1536]{2,1,0:T(8,128)(2,1)}, bf16[1,384,1536]{2,1,0:T(8,128)(2,1)}) async-done(((bf16[1,384,1536]{2,1,0:T(8,128)(2,1)}, bf16[1,384,1536]{2,1,0:T(8,128)(2,1)}), (bf16[1,384,1536]{2,1,0:T(8,128)(2,1)}, bf16[1,384,1536]{2,1,0:T(8,128)(2,1)})) %all-reduce.5.cloned.1.call-update) | async-done | bytes 2359312 | tf_op jit(solution)/shard_map/psum | solution.py:751
  (729 shorter events, 470.4 us)
Async XLA Ops:
  7.2 148.9 %all-gather.5.cloned.1.call-start = ((), (), s32[]{:S(2)}) async-start(), calls=%async_computation.5 | async-start | bytes 10616832 | tf_op jit(solution)/shard_map/all_gather | solution.py:699
  9.2 30.1 %collective-permute-start.4 = (bf16[192,1536]{1,0:T(8,128)(2,1)S(1)}, bf16[192,1536]{1,0:T(8,128)(2,1)S(1)}, u32[]{:S(2)}, u32[]{:S(2)}) collective-permute-start(bf16[192,1536]{1,0:T(8,128)(2,1)S(1)} %pad_maximum_fusion.16), channel_id=1, source_target_pairs={{2,0},{3,1},{0,2},{1,3},{6,4},{7,5},{4,6},{5,7},{10,8},{11,9},{8,1... | collective-permute-start | bytes 1769480 | tf_op jit(solution)/shard_map/ppermute | solution.py:427
  40.4 355.9 %all-gather.7.cloned.1.call-start = ((), (), s32[]{:S(2)}) async-start(), calls=%async_computation.6 | async-start | bytes 23887872 | tf_op jit(solution)/shard_map/all_gather | solution.py:699
  43.9 59.7 %collective-permute-start.10 = (bf16[192,3456]{1,0:T(8,128)(2,1)S(1)}, bf16[192,3456]{1,0:T(8,128)(2,1)S(1)}, u32[]{:S(2)}, u32[]{:S(2)}) collective-permute-start(bf16[192,3456]{1,0:T(8,128)(2,1)S(1)} %pad_maximum_fusion.12), channel_id=1, source_target_pairs={{2,0},{3,1},{0,2},{1,3},{6,4},{7,5},{4,6},{5,7},{10,8},{11,9},{8,1... | collective-permute-start | bytes 3981320 | tf_op jit(solution)/shard_map/ppermute | solution.py:427
  111.8 378.3 %all-gather.9.cloned.1.call-start = ((), (), s32[]{:S(2)}) async-start(), calls=%async_computation.7 | async-start | bytes 10616832 | tf_op jit(solution)/shard_map/all_gather | solution.py:699
  195.4 393.7 %all-gather.11.cloned.1.call-start = ((), (), s32[]{:S(2)}) async-start(), calls=%async_computation.8 | async-start | bytes 23887872 | tf_op jit(solution)/shard_map/all_gather | solution.py:699
  282.3 59.5 %collective-permute-start.20 = (bf16[192,3456]{1,0:T(8,128)(2,1)S(1)}, bf16[192,3456]{1,0:T(8,128)(2,1)S(1)}, u32[]{:S(2)}, u32[]{:S(2)}) collective-permute-start(bf16[192,3456]{1,0:T(8,128)(2,1)S(1)} %pad_maximum_fusion.13), channel_id=1, source_target_pairs={{2,0},{3,1},{0,2},{1,3},{6,4},{7,5},{4,6},{5,7},{10,8},{11,9},{8,1... | collective-permute-start | bytes 3981320 | tf_op jit(solution)/shard_map/ppermute | solution.py:427
  345.8 75.3 %all-to-all-start.3 = ((bf16[4,256,384]{2,1,0:T(8,128)(2,1)}), bf16[4,256,384]{2,1,0:T(8,128)(2,1)}, u32[]{:S(2)}, u32[]{:S(2)}) async-start(bf16[4,256,384]{2,1,0:T(8,128)(2,1)} %bitcast.470), calls=%async_computation.3 | async-start | bytes 1572864 | tf_op jit(solution)/shard_map/all_to_all | solution.py:454
  354.9 35.0 %collective-permute-start.11 = (bf16[192,1152]{1,0:T(8,128)(2,1)}, bf16[192,1152]{1,0:T(8,128)(2,1)S(1)}, u32[]{:S(2)}, u32[]{:S(2)}) collective-permute-start(bf16[192,1152]{1,0:T(8,128)(2,1)} %get-tuple-element.36), channel_id=1, source_target_pairs={{2,0},{3,1},{0,2},{1,3},{6,4},{7,5},{4,6},{5,7},{10,8},{11,9},{8,1... | collective-permute-start | bytes 1327112 | tf_op jit(solution)/shard_map/ppermute | solution.py:427
  358.1 34.0 %collective-permute-start.9 = (bf16[256,1536]{1,0:T(8,128)(2,1)S(1)}, bf16[256,1536]{1,0:T(8,128)(2,1)S(1)}, u32[]{:S(2)}, u32[]{:S(2)}) collective-permute-start(bf16[256,1536]{1,0:T(8,128)(2,1)S(1)} %multiply_convert_fusion.6), channel_id=1, source_target_pairs={{0,1},{1,0},{2,3},{3,2},{4,5},{5,4},{6,7},{7,6},{8,9},{9,8},{10,11... | collective-permute-start | bytes 2359304 | tf_op jit(solution)/shard_map/ppermute | solution.py:422
  419.6 36.5 %collective-permute-start.12 = (bf16[256,1536]{1,0:T(8,128)(2,1)}, bf16[256,1536]{1,0:T(8,128)(2,1)}, u32[]{:S(2)}, u32[]{:S(2)}) collective-permute-start(bf16[256,1536]{1,0:T(8,128)(2,1)} %fusion.150), channel_id=1, source_target_pairs={{0,1},{1,0},{2,3},{3,2},{4,5},{5,4},{6,7},{7,6},{8,9},{9,8},{10,11... | collective-permute-start | bytes 2359304 | tf_op jit(solution)/shard_map/ppermute | solution.py:422
  423.4 112.9 %collective-permute-start.23 = (bf16[256,1536]{1,0:T(8,128)(2,1)}, bf16[256,1536]{1,0:T(8,128)(2,1)}, u32[]{:S(2)}, u32[]{:S(2)}) collective-permute-start(bf16[256,1536]{1,0:T(8,128)(2,1)} %bitcast.170), channel_id=1, source_target_pairs={{0,1},{1,0},{2,3},{3,2},{4,5},{5,4},{6,7},{7,6},{8,9},{9,8},{10,11... | collective-permute-start | bytes 2359304 | tf_op jit(solution)/shard_map/ppermute | solution.py:422
  424.0 47.9 %collective-permute-start.15 = (bf16[192,512]{1,0:T(8,128)(2,1)}, bf16[192,512]{1,0:T(8,128)(2,1)S(1)}, u32[]{:S(2)}, u32[]{:S(2)}) collective-permute-start(bf16[192,512]{1,0:T(8,128)(2,1)} %get-tuple-element.38), channel_id=1, source_target_pairs={{2,0},{3,1},{0,2},{1,3},{6,4},{7,5},{4,6},{5,7},{10,8},{11,9},{8,1... | collective-permute-start | bytes 589832 | tf_op jit(solution)/shard_map/ppermute | solution.py:427
  426.8 45.1 %collective-permute-start.17 = (bf16[2,2,256,256]{3,2,1,0:T(8,128)(2,1)}, bf16[2,2,256,256]{3,2,1,0:T(8,128)(2,1)S(1)}, u32[]{:S(2)}, u32[]{:S(2)}) collective-permute-start(bf16[2,2,256,256]{3,2,1,0:T(8,128)(2,1)} %get-tuple-element.40), channel_id=1, source_target_pairs={{2,0},{3,1},{0,2},{1,3},{6,4},{7,5},{4,6},{5,7},{10,8},{11,9},{8,1... | collective-permute-start | bytes 1572872 | tf_op jit(solution)/shard_map/ppermute | solution.py:427
  426.9 44.9 %collective-permute-start.16 = (f32[8,512]{1,0:T(8,128)S(1)}, f32[8,512]{1,0:T(8,128)S(1)}, u32[]{:S(2)}, u32[]{:S(2)}) collective-permute-start(f32[8,512]{1,0:T(8,128)S(1)} %copy-done.143), channel_id=1, source_target_pairs={{2,0},{3,1},{0,2},{1,3},{6,4},{7,5},{4,6},{5,7},{10,8},{11,9},{8,1... | collective-permute-start | bytes 49160 | tf_op jit(solution)/shard_map/ppermute | solution.py:427
  532.4 29.5 %collective-permute-start.18 = (bf16[256,1536]{1,0:T(8,128)(2,1)}, bf16[256,1536]{1,0:T(8,128)(2,1)}, u32[]{:S(2)}, u32[]{:S(2)}) collective-permute-start(bf16[256,1536]{1,0:T(8,128)(2,1)} %fusion.140), channel_id=1, source_target_pairs={{0,1},{1,0},{2,3},{3,2},{4,5},{5,4},{6,7},{7,6},{8,9},{9,8},{10,11... | collective-permute-start | bytes 2359304 | tf_op jit(solution)/shard_map/ppermute | solution.py:422
  643.7 30.2 %collective-permute-start.24 = (bf16[256,1536]{1,0:T(8,128)(2,1)}, bf16[256,1536]{1,0:T(8,128)(2,1)}, u32[]{:S(2)}, u32[]{:S(2)}) collective-permute-start(bf16[256,1536]{1,0:T(8,128)(2,1)} %fusion.133), channel_id=1, source_target_pairs={{0,1},{1,0},{2,3},{3,2},{4,5},{5,4},{6,7},{7,6},{8,9},{9,8},{10,11... | collective-permute-start | bytes 2359304 | tf_op jit(solution)/shard_map/ppermute | solution.py:422
  654.7 37.1 %collective-permute-start.22 = (bf16[256,1536]{1,0:T(8,128)(2,1)}, bf16[256,1536]{1,0:T(8,128)(2,1)}, u32[]{:S(2)}, u32[]{:S(2)}) collective-permute-start(bf16[256,1536]{1,0:T(8,128)(2,1)} %fusion.147), channel_id=1, source_target_pairs={{0,1},{1,0},{2,3},{3,2},{4,5},{5,4},{6,7},{7,6},{8,9},{9,8},{10,11... | collective-permute-start | bytes 2359304 | tf_op jit(solution)/shard_map/ppermute | solution.py:422
  698.9 170.6 %all-to-all-start.2 = ((bf16[256,4,384]{2,0,1:T(8,128)(2,1)}), bf16[256,4,384]{2,0,1:T(8,128)(2,1)}, u32[]{:S(2)}, u32[]{:S(2)}) async-start(bf16[256,4,384]{2,0,1:T(8,128)(2,1)} %bitcast.455), calls=%async_computation.2 | async-start | bytes 1572864 | tf_op jit(solution)/shard_map/all_to_all | solution.py:458
  758.5 29.8 %collective-permute-start.32 = (bf16[192,512]{1,0:T(8,128)(2,1)S(1)}, bf16[192,512]{1,0:T(8,128)(2,1)S(1)}, u32[]{:S(2)}, u32[]{:S(2)}) collective-permute-start(bf16[192,512]{1,0:T(8,128)(2,1)S(1)} %slice.1023), channel_id=1, source_target_pairs={{0,2},{1,3},{2,0},{3,1},{4,6},{5,7},{6,4},{7,5},{8,10},{9,11},{10,... | collective-permute-start | bytes 589832 | tf_op jit(solution)/shard_map/ppermute | solution.py:432
  835.0 64.9 %collective-permute-start.33 = (bf16[192,1152]{1,0:T(8,128)(2,1)}, bf16[192,1152]{1,0:T(8,128)(2,1)}, u32[]{:S(2)}, u32[]{:S(2)}) collective-permute-start(bf16[192,1152]{1,0:T(8,128)(2,1)} %slice.1043), channel_id=1, source_target_pairs={{0,2},{1,3},{2,0},{3,1},{4,6},{5,7},{6,4},{7,5},{8,10},{9,11},{10,... | collective-permute-start | bytes 1327112 | tf_op jit(solution)/shard_map/ppermute | solution.py:432
  878.1 141.7 %all-reduce.7.cloned.1.call-start = ((), (), s32[]{:S(2)}) async-start(), calls=%async_computation.10 | async-start | bytes 2555904 | tf_op jit(solution)/shard_map/psum | solution.py:752
  962.6 199.9 %all-reduce.5.cloned.1.call-start = ((), (), s32[]{:S(2)}) async-start(), calls=%async_computation.9 | async-start | bytes 4718592 | tf_op jit(solution)/shard_map/psum | solution.py:751
  994.6 178.7 %all-to-all-start.4 = ((f32[256,4,384]{2,0,1:T(8,128)}), f32[256,4,384]{2,0,1:T(8,128)S(1)}, u32[]{:S(2)}, u32[]{:S(2)}) async-start(f32[256,4,384]{2,0,1:T(8,128)} %bitcast.416), calls=%async_computation.4 | async-start | bytes 3145728 | tf_op jit(solution)/shard_map/all_to_all | solution.py:458
  (210 other events, 3360.0 us)
Sparse Core Ops, SparseCore 0:
  40.5 60.0 all-gather.4
  105.5 107.2 all-gather.6
  215.3 60.2 all-gather.8
  345.9 107.5 all-gather.10
  962.8 56.9 all-reduce.6
  1027.4 135.0 all-reduce.4

commit v3 on v2

--- a/solution.py
+++ b/solution.py
@@ -417,6 +417,232 @@
     )[0]
 
 
+def line_plan(pieces, unit):
+    plan, line = [], 0
+    for at, (rows, columns) in enumerate(pieces):
+        for begin in range(0, columns, LANES):
+            done = 0
+            while done < rows:
+                index, inner = divmod(line, unit)
+                count = min(rows - done, unit - inner)
+                plan.append(
+                    (at, slice(done, done + count), slice(begin, begin + LANES), index,
+                     slice(inner, inner + count))
+                )
+                done += count
+                line += count
+    return plan
+
+
+def closing_sizes(shared, split, peers, cols, shards):
+    shared_lines = sum(rows * columns for rows, columns in shared) // LANES
+    split_lines = sum(rows * columns for rows, columns in split) // LANES // shards
+    unit = -(-shared_lines // (peers * cols * 16)) * 16
+    part = -(-split_lines // (peers * 16)) * 16
+    return unit, part
+
+
+def remote(source, target, sems, slot, device):
+    return pltpu.make_async_remote_copy(
+        src_ref=source,
+        dst_ref=target,
+        send_sem=sems.at[0, slot],
+        recv_sem=sems.at[1, slot],
+        device_id=device,
+        device_id_type=MESH,
+    )
+
+
+def closing_kernel(
+    own_part, other_part, stream, d_middle, gain,
+    shared_a, shared_b, shared_c, shared_d, split_a, split_b, split_c, split_d,
+    tokens_out, shared_out_a, shared_out_b, shared_out_c, shared_out_d,
+    split_out_a, split_out_b, split_out_c, split_out_d,
+    received, outgoing, flat, inbox, red, red_split, zbox, sbox, zfull, sfull, shared_all,
+    split_all, pair_sems, row_sems, col_sems, turn_sems, spread_sems, shared_sems, split_sems,
+    token_sems,
+):
+    shared = (shared_a, shared_b, shared_c, shared_d)
+    split = (split_a, split_b, split_c, split_d)
+    shared_out = (shared_out_a, shared_out_b, shared_out_c, shared_out_d)
+    split_out = (split_out_a, split_out_b, split_out_c, split_out_d)
+    peers, cols = lax.axis_size("row"), lax.axis_size("col")
+    shards = cols // 2
+    row, col = lax.axis_index("row"), lax.axis_index("col")
+    own, d_model = stream.shape
+    piece = d_model // cols
+    unit, part = zbox.shape[1], sbox.shape[1]
+    shared_lines = cols * unit
+
+    barrier = pltpu.get_barrier_semaphore()
+    for by in range(1, peers):
+        pl.semaphore_signal(
+            barrier, inc=1, device_id=((row + by) % peers, col), device_id_type=MESH
+        )
+    for by in range(1, cols):
+        pl.semaphore_signal(barrier, inc=1, device_id=(row, (col + by) % cols), device_id_type=MESH)
+
+    sizes = [value.shape for value in shared]
+    shared_plan = line_plan(sizes, unit)
+    thin = [(value.shape[0], value.shape[1] // shards) for value in split]
+    split_plan = line_plan(thin, part)
+    flat[...] = jnp.zeros(flat.shape, BRAIN)
+    for at, rows, lanes, index, lines in shared_plan:
+        begin = index % cols * unit
+        flat[index // cols, begin + lines.start : begin + lines.stop] = shared[at][
+            rows, lanes
+        ].astype(BRAIN)
+    for turn in range(shards):
+        for at, rows, lanes, index, lines in split_plan:
+            begin = shared_lines + turn * part
+            skip = turn * thin[at][1]
+            flat[index, begin + lines.start : begin + lines.stop] = split[at][
+                rows, skip + lanes.start : skip + lanes.stop
+            ].astype(BRAIN)
+    pl.semaphore_wait(barrier, peers + cols - 2)
+
+    pair = remote(other_part, received, pair_sems, 0, (row, col + 1 - 2 * (col % 2)))
+    pair.start()
+    scattered = []
+    for by in range(1, peers):
+        to = (row + by) % peers
+        copy = remote(flat.at[to], inbox.at[by - 1], row_sems, by - 1, (to, col))
+        copy.start()
+        scattered.append(copy)
+
+    pair.wait()
+
+    def norm_rows(at, nothing):
+        lines = pl.ds(pl.multiple_of(at * 16, 16), 16)
+        value = stream[lines]
+        scale = lax.rsqrt(jnp.mean(value * value, axis=1, keepdims=True) + EPSILON)
+        gained = (own_part[lines] + received[lines].astype(FLOAT)) * gain[...]
+        total = jnp.mean(gained * value, axis=1, keepdims=True)
+        result = d_middle[lines] + scale * gained - value * (scale * scale * scale * total)
+        for to in range(cols):
+            outgoing[to, lines] = result[:, to * piece : (to + 1) * piece]
+        return nothing
+
+    lax.fori_loop(0, own // 16, norm_rows, 0)
+    mine = pl.ds(pl.multiple_of(col * own, own), own)
+    returned = []
+    for by in range(1, cols):
+        to = (col + by) % cols
+        copy = remote(outgoing.at[to], tokens_out.at[mine], token_sems, by - 1, (row, to))
+        copy.start()
+        returned.append(copy)
+    tokens_out[mine] = outgoing[col]
+
+    for copy in scattered:
+        copy.wait()
+    total = flat[row].astype(FLOAT)
+    for by in range(1, peers):
+        total = total + inbox[by - 1].astype(FLOAT)
+    for at in range(cols):
+        red[at] = total[at * unit : (at + 1) * unit].astype(BRAIN)
+    for turn in range(shards):
+        begin = shared_lines + turn * part
+        red_split[turn] = total[begin : begin + part].astype(BRAIN)
+
+    copies = []
+    for by in range(1, cols):
+        to = (col + by) % cols
+        copies.append(remote(red.at[to], zbox.at[by - 1], col_sems, by - 1, (row, to)))
+    for turn in range(1, shards):
+        to = (col + 2 * turn) % cols
+        copies.append(remote(red_split.at[turn], sbox.at[turn - 1], turn_sems, turn - 1, (row, to)))
+    for copy in copies:
+        copy.start()
+    for copy in copies:
+        copy.wait()
+    total = red[col].astype(FLOAT)
+    for by in range(1, cols):
+        total = total + zbox[by - 1].astype(FLOAT)
+    zfull[col] = total.astype(BRAIN)
+    total = red_split[0].astype(FLOAT)
+    for turn in range(1, shards):
+        total = total + sbox[turn - 1].astype(FLOAT)
+    sfull[...] = total.astype(BRAIN)
+
+    spread = []
+    for by in range(1, cols):
+        to = (col + by) % cols
+        copy = remote(zfull.at[col], zfull.at[col], spread_sems, by - 1, (row, to))
+        copy.start()
+        spread.append(copy)
+    last = []
+    for by in range(1, peers):
+        to = (row + by) % peers
+        copy = remote(sfull, split_all.at[row], split_sems, by - 1, (to, col))
+        copy.start()
+        last.append(copy)
+    split_all[row] = sfull[...]
+    for copy in spread:
+        copy.wait()
+    for by in range(1, peers):
+        to = (row + by) % peers
+        copy = remote(zfull, shared_all.at[row], shared_sems, by - 1, (to, col))
+        copy.start()
+        last.append(copy)
+    shared_all[row] = zfull[...]
+    for copy in last:
+        copy.wait()
+    for at, rows, lanes, index, lines in shared_plan:
+        shared_out[at][rows, lanes] = shared_all[index // cols, index % cols, lines].astype(FLOAT)
+    for at, rows, lanes, index, lines in split_plan:
+        split_out[at][rows, lanes] = split_all[index, lines].astype(FLOAT)
+    for copy in returned:
+        copy.wait()
+
+
+def close(own_part, other_part, stream, d_middle, gain, shared, split):
+    peers, cols = lax.axis_size("row"), lax.axis_size("col")
+    shards = cols // 2
+    own, d_model = stream.shape
+    pieces = [value.shape[1] // shards for value in split]
+
+    def widened(value):
+        cut = value.reshape(value.shape[0], shards, -1)
+        short = -cut.shape[2] % LANES
+        return jnp.pad(cut, ((0, 0), (0, 0), (0, short))).reshape(value.shape[0], -1)
+
+    split = [widened(value) if piece % LANES else value for value, piece in zip(split, pieces)]
+    shared_sizes = [value.shape for value in shared]
+    split_sizes = [value.shape for value in split]
+    unit, part = closing_sizes(shared_sizes, split_sizes, peers, cols, shards)
+    lines = cols * unit + shards * part
+    sems = [
+        pltpu.SemaphoreType.DMA((2, count))
+        for count in (1, peers - 1, cols - 1, max(shards - 1, 1), cols - 1, peers - 1, peers - 1,
+                      cols - 1)
+    ]
+    result = block_call(
+        closing_kernel,
+        2,
+        [own_part, other_part, stream, d_middle, gain, *shared, *split],
+        [((own * cols, d_model // cols), FLOAT)]
+        + [(size, FLOAT) for size in shared_sizes]
+        + [((rows, columns // shards), FLOAT) for rows, columns in split_sizes],
+        [
+            pltpu.VMEM((own, d_model), BRAIN),
+            pltpu.VMEM((cols, own, d_model // cols), FLOAT),
+            pltpu.VMEM((peers, lines, LANES), BRAIN),
+            pltpu.VMEM((peers - 1, lines, LANES), BRAIN),
+            pltpu.VMEM((cols, unit, LANES), BRAIN),
+            pltpu.VMEM((shards, part, LANES), BRAIN),
+            pltpu.VMEM((cols - 1, unit, LANES), BRAIN),
+            pltpu.VMEM((max(shards - 1, 1), part, LANES), BRAIN),
+            pltpu.VMEM((cols, unit, LANES), BRAIN),
+            pltpu.VMEM((part, LANES), BRAIN),
+            pltpu.VMEM((peers, cols, unit, LANES), BRAIN),
+            pltpu.VMEM((peers, part, LANES), BRAIN),
+        ]
+        + sems,
+    )
+    split = [value[:, :piece] for value, piece in zip(result[5:9], pieces)]
+    return result[0], result[1:5], split
+
+
 def partner(value):
     peers = lax.axis_size("col")
     return lax.ppermute(value, "col", [(at, at ^ 1) for at in range(peers)])
@@ -481,21 +707,27 @@
     return (value * pick).astype(BRAIN)
 
 
-def recur_part(stream, wide, small, gains, ctx):
-    inlet, outlet = wide
-    pick, offset = ctx["pick"], ctx["offset"]
+def entry(stream, gain):
+    scale, normed = norm_forward(stream, gain)
+    return scale, both_halves(normed)
+
+
+def recur_branch(normed_full, inlet, small, ctx):
+    pick = ctx["pick"]
     ranks = pick.shape[1]
-    own = stream.shape[0]
-    rows = 2 * own
-    width = outlet.shape[1]
-
-    scale_one, normed = norm_forward(stream, gains[0])
-    normed_full = both_halves(normed)
+    width = inlet.shape[1] // 2
     low = nt(normed_full, small["inlet_lower"])
     inner = [masked(low[:, b * ranks : (b + 1) * ranks], pick) for b in range(2)]
     branch = nn(normed_full, inlet)
     lead = branch[:, :width] + nn(inner[0], small["inlet_upper"][0])
     gate = branch[:, width:] + nn(inner[1], small["inlet_upper"][1])
+    return lead, gate, inner
+
+
+def recur_part(stream, lead, gate, outlet, small, ctx):
+    pick, offset = ctx["pick"], ctx["offset"]
+    own = stream.shape[0]
+    rows = 2 * own
     conv, decay, hidden, mixed, state_in = recur_forward(lead, gate, offset, small)
     lowrank = masked(nt(mixed, small["outlet_lower"]), pick)
 
@@ -504,22 +736,19 @@
 
     middle = stream + half_share(outward(slice(0, own)), outward(slice(own, rows)))
     kept = dict(
-        stream=stream, scale_one=scale_one, normed_full=normed_full, inner=inner, lead=lead,
-        gate=gate, conv=conv, decay=decay, hidden=hidden, state_in=state_in, mixed=mixed,
-        lowrank=lowrank, middle=middle,
+        conv=conv, decay=decay, hidden=hidden, state_in=state_in, mixed=mixed, lowrank=lowrank,
+        middle=middle,
     )
     return middle, kept
 
 
-def hidden_part(middle, wide, small, gains, ctx):
+def hidden_part(middle, normed_two_full, wide, small, ctx):
     expand, shrink = wide
     pick = ctx["pick"]
     ranks = pick.shape[1]
     own = middle.shape[0]
     rows = 2 * own
     spread = shrink.shape[1]
-    scale_two, normed_two = norm_forward(middle, gains[1])
-    normed_two_full = both_halves(normed_two)
     low_two = nt(normed_two_full, small["expand_lower"])
     inner_two = [masked(low_two[:, b * ranks : (b + 1) * ranks], pick) for b in range(2)]
     branch_two = nn(normed_two_full, expand)
@@ -533,7 +762,7 @@
 
     result = middle + half_share(downward(slice(0, own)), downward(slice(own, rows)))
     kept = dict(
-        scale_two=scale_two, normed_two_full=normed_two_full, inner_two=inner_two,
+        inner_two=inner_two,
         up_gate=up_gate, up_value=up_value, product=product, lowrank_two=lowrank_two,
     )
     return result, kept
@@ -596,29 +825,38 @@
     def inward(part):
         return nt(d_branch[part], inlet) + nn(d_inner[part], small["inlet_lower"])
 
-    d_normed = half_share(inward(slice(0, own)), inward(slice(own, rows)))
     inlet_lower_grad = tn(d_inner, kept["normed_full"])
     inlet_upper_grad = jnp.concatenate(
         [tn(kept["inner"][b], d_branch[:, b * width : (b + 1) * width]) for b in range(2)], axis=0
     )
-    d_input = d_middle + norm_backward(kept["stream"], kept["scale_one"], gains[0], d_normed)
-    shared = jnp.concatenate(
-        [inlet_lower_grad, outlet_upper_grad, expand_lower_grad, shrink_upper_grad], axis=0
-    )
-    split = (
-        jnp.concatenate([inlet_upper_grad, outlet_lower_grad], axis=0),
-        jnp.concatenate([expand_upper_grad, shrink_lower_grad], axis=0),
-    )
-    return d_input, shared, split
-
-
-def owned(grad, shards):
-    piece = grad.shape[1] // shards
-    parts = [grad[:, turn * piece : (turn + 1) * piece].astype(BRAIN) for turn in range(shards)]
-    total = parts[0].astype(FLOAT)
-    for turn in range(1, shards):
-        total = total + to_shard(parts[turn], turn).astype(FLOAT)
-    return total.astype(BRAIN)
+    shared = (inlet_lower_grad, outlet_upper_grad, expand_lower_grad, shrink_upper_grad)
+    split = (inlet_upper_grad, outlet_lower_grad, expand_upper_grad, shrink_lower_grad)
+    partial_sums = (inward(slice(0, own)), inward(slice(own, rows)))
+    return d_middle, partial_sums, shared, split
+
+
+def start_sums(shared, split):
+    return (
+        lax.psum(jnp.concatenate(shared, axis=0).astype(BRAIN), ("row", "col")),
+        [
+            lax.psum(jnp.concatenate(pair, axis=0).astype(BRAIN), "row")
+            for pair in (split[:2], split[2:])
+        ],
+    )
+
+
+def end_sums(shared, split, shards, anchor):
+    shared = after(shared, anchor).astype(FLOAT)
+    totals = []
+    for whole in split:
+        whole = after(whole, anchor)
+        piece = whole.shape[1] // shards
+        parts = [whole[:, turn * piece : (turn + 1) * piece] for turn in range(shards)]
+        total = parts[0].astype(FLOAT)
+        for turn in range(1, shards):
+            total = total + to_shard(parts[turn], turn).astype(FLOAT)
+        totals.append(total)
+    return shared, totals
 
 
 def local(
@@ -691,22 +929,29 @@
         [conv_weight, gate_bias, conv_bias[:, None], decay_param[:, None]], axis=1
     )
 
-    def fetch(pair, single, anchor):
-        piece = single.shape[1]
-        pack = jnp.concatenate([pair[:, 0], pair[:, 1], single], axis=1)
-        parts = all_shards(after(pack, anchor))
+    def start(pair, single, anchor):
+        return all_shards(after(jnp.concatenate([pair[:, 0], pair[:, 1], single], axis=1), anchor))
+
+    def gathered(parts, anchor):
+        piece = parts[0].shape[1] // 3
+        parts = [parts[0]] + [after(part, anchor) for part in parts[1:]]
         columns = [part[:, at * piece : (at + 1) * piece] for at in range(3) for part in parts]
         whole = lax.all_gather(jnp.concatenate(columns, axis=1), "row", axis=0, tiled=True)
         cut = 2 * shards * piece
-        return (whole[:, :cut], whole[:, cut:]), parts[-1]
-
-    def recur_weights(layer, anchor):
-        wide, last = fetch(inlet_weight[layer], outlet_weight[layer], anchor)
-        narrow, vectors, gates = (
-            jnp.concatenate(all_shards(after(value, last)), axis=1)
+        return whole[:, :cut], whole[:, cut:]
+
+    def joined(parts, anchor):
+        return jnp.concatenate([parts[0]] + [after(part, anchor) for part in parts[1:]], axis=1)
+
+    def start_recur_small(layer, anchor):
+        return [
+            all_shards(after(value, anchor))
             for value in (narrow_own[layer], vectors_own[layer], gate_weight[layer])
-        )
-        small = dict(
+        ]
+
+    def recur_small(layer, parts, anchor):
+        narrow, vectors, gates = (joined(part, anchor) for part in parts)
+        return dict(
             inlet_lower=lows["inlet_lower"][layer],
             inlet_upper=narrow[: 2 * ranks].reshape(2, ranks, -1),
             outlet_lower=narrow[2 * ranks :],
@@ -717,40 +962,75 @@
             soft=jax.nn.softplus(vectors[CONV + 3 : CONV + 4]),
             gate_weight=gates,
         )
-        return wide, small, last
-
-    def hidden_weights(layer, anchor):
-        wide, last = fetch(expand_weight[layer], shrink_weight[layer], anchor)
-        broad = jnp.concatenate(all_shards(after(broad_own[layer], last)), axis=1)
-        small = dict(
+
+    def hidden_small(layer, parts, anchor):
+        broad = joined(parts, anchor)
+        return dict(
             expand_lower=lows["expand_lower"][layer],
             expand_upper=broad[: 2 * ranks].reshape(2, ranks, -1),
             shrink_lower=broad[2 * ranks :],
             shrink_upper=lows["shrink_upper"][layer],
         )
-        return wide, small, last
 
     outputs, saved, wides, smalls = [], [], [], []
-    anchor_one = anchor_two = None
+    recur_pack = start(inlet_weight[0], outlet_weight[0], None)
+    recur_bits = start_recur_small(0, recur_pack[-1])
+    hidden_pack = start(expand_weight[0], shrink_weight[0], recur_pack[-1])
+    wide_one = gathered(recur_pack, None)
     for layer in range(LAYERS):
-        wide_one, small_one, last = recur_weights(layer, anchor_one)
-        wide_two, small_two, _ = hidden_weights(layer, last if layer == 0 else anchor_two)
-        middle, kept = recur_part(stream, wide_one, small_one, gains[layer], ctx)
-        stream, more = hidden_part(middle, wide_two, small_two, gains[layer], ctx)
-        anchor_one, anchor_two = kept["lead"], middle
+        more_layers = layer + 1 < LAYERS
+        scale_one, normed_full = entry(stream, gains[layer][0])
+        small_one = recur_small(layer, recur_bits, normed_full)
+        lead, gate, inner = recur_branch(normed_full, wide_one[0], small_one, ctx)
+        if layer == 0:
+            wide_two = gathered(hidden_pack, lead)
+        hidden_bits = all_shards(after(broad_own[layer], lead))
+        if more_layers:
+            recur_pack = start(inlet_weight[layer + 1], outlet_weight[layer + 1], lead)
+        middle, kept = recur_part(stream, lead, gate, wide_one[1], small_one, ctx)
+        kept.update(
+            stream=stream, scale_one=scale_one, normed_full=normed_full, inner=inner, gate=gate
+        )
+        if more_layers:
+            wide_next = gathered(recur_pack, middle)
+            recur_bits = start_recur_small(layer + 1, middle)
+            hidden_pack = start(expand_weight[layer + 1], shrink_weight[layer + 1], middle)
+        scale_two, normed_two_full = entry(middle, gains[layer][1])
+        small_two = hidden_small(layer, hidden_bits, normed_two_full)
+        stream, more = hidden_part(middle, normed_two_full, wide_two, small_two, ctx)
+        more.update(scale_two=scale_two, normed_two_full=normed_two_full)
+        if more_layers:
+            wide_two_next = gathered(hidden_pack, more["product"])
         outputs.append(from_sequence(stream.astype(BRAIN)))
         saved.append({**kept, **more})
         wides.append(wide_one + wide_two)
         smalls.append({**small_one, **small_two})
+        if more_layers:
+            wide_one, wide_two = wide_next, wide_two_next
     d_stream = to_sequence(cotangent).astype(FLOAT)
     shared, narrow, broad = [None] * LAYERS, [None] * LAYERS, [None] * LAYERS
+    started = {}
     for layer in reversed(range(LAYERS)):
-        d_stream, everywhere, split = layer_backward(
-            d_stream, wides[layer], smalls[layer], gains[layer], saved[layer], ctx
+        kept = saved[layer]
+        d_middle, parts, shared_parts, split_parts = layer_backward(
+            d_stream, wides[layer], smalls[layer], gains[layer], kept, ctx
         )
-        shared[layer] = lax.psum(everywhere.astype(BRAIN), ("row", "col")).astype(FLOAT)
-        narrow[layer] = lax.psum(owned(split[0], shards), "row").astype(FLOAT)
-        broad[layer] = lax.psum(owned(split[1], shards), "row").astype(FLOAT)
+        if layer:
+            d_normed = half_share(*parts)
+            d_stream = d_middle + norm_backward(
+                kept["stream"], kept["scale_one"], gains[layer][0], d_normed
+            )
+            started[layer] = start_sums(shared_parts, split_parts)
+        else:
+            tokens_grad, shared_parts, split_parts = close(
+                parts[0], parts[1].astype(BRAIN), kept["stream"], d_middle, gains[layer][:1],
+                shared_parts, split_parts,
+            )
+            shared[layer] = jnp.concatenate(shared_parts, axis=0)
+            narrow[layer] = jnp.concatenate(split_parts[:2], axis=0)
+            broad[layer] = jnp.concatenate(split_parts[2:], axis=0)
+    for layer, (whole, pairs) in started.items():
+        shared[layer], (narrow[layer], broad[layer]) = end_sums(whole, pairs, shards, tokens_grad)
     shared, narrow, broad = jnp.stack(shared), jnp.stack(narrow), jnp.stack(broad)
     spread_out = (adapter_ids[None, :] == jnp.arange(adapters, dtype=jnp.int32)[:, None])
 
@@ -771,7 +1051,7 @@
 
     return (
         jnp.stack(outputs, axis=0),
-        from_sequence(d_stream),
+        tokens_grad,
         lower_out(shared[:, : 2 * ranks], 2),
         by_adapter(narrow[:, : 2 * ranks], 2),
         lower_out(narrow[:, 2 * ranks :], 1),

time: 1190 us -> 1040 us (0.87)
  waiting for transfers between devices: 621 us -> 368 us
  Pallas kernels: 114 us -> 205 us
  local copies, waits for them, and re-layouts: 51.5 us -> 77.1 us
    psum x2, waiting for transfers between devices: 155 us -> 0.01 us  [the longest x1 0.01 us: start_sums(): lax.psum(jnp.concatenate(shared, axis=0).astype(BRAIN), ('row', 'col'))]
    ppermute x12, waiting for transfers between devices: 246 us -> 129 us  [from_shard(): lax.ppermute(value, 'col', [((at + 2 * turn) % peers, at) for at in range...]
    pallas_call x4 -> x5, Pallas kernels: 114 us -> 205 us  [block_call(): pl.pallas_call(kernel, out_shape=[jax.ShapeDtypeStruct(*out) for out in o...]
    ppermute x16 -> x15, waiting for transfers between devices: 183 us -> 211 us  [partner(): return lax.ppermute(value, 'col', [(at, at ^ 1) for at in range(peers)])]
    unnamed x413 -> x403, local copies, waits for them, and re-layouts: 22.8 us -> 42.9 us
  transfers between devices with their start and end apart: 46 -> 42, of which waited for: 29 -> 21; matrix products, arithmetic and copies ran while one was open for 23% -> 28% of each run, Pallas kernels for 7% -> 20%
where the time goes in v3:
time: 1040 us
  waiting for transfers between devices  368 us (35%)
  matrix products  253 us (24%)
  Pallas kernels  205 us (20%)
  local copies, waits for them, and re-layouts  77.1 us (7%)
  starting transfers between devices  62.7 us (6%)
  other arithmetic  44.6 us (4%)
  between operations  26.4 us (3%)
    ppermute x15, waiting for transfers between devices, partner(): return lax.ppermute(value, 'col', [(at, at ^ 1) for at in range(peers)])  211 us
    pallas_call x5, Pallas kernels, block_call(): pl.pallas_call(kernel, out_shape=[jax.ShapeDtypeStruct(*out) for out in o...  205 us
    ppermute x12, waiting for transfers between devices, from_shard(): lax.ppermute(value, 'col', [((at + 2 * turn) % peers, at) for at in range...  129 us
    dot_general x36, matrix products, nn(): lax.dot_general(left, right, (((1,), (0,)), ((), ())), preferred_element_...  116 us
    dot_general x36, matrix products, nt(): lax.dot_general(left, right, (((1,), (1,)), ((), ())), preferred_element_...  112 us
    unnamed x403, local copies, waits for them, and re-layouts  42.9 us
    dot_general x20, matrix products, tn(): lax.dot_general(left, right, (((0,), (0,)), ((), ())), preferred_element_...  24.7 us
  transfers between devices with their start and end apart: 42, of which 21 were waited for; matrix products, arithmetic and copies ran while one was open for 28% of the time, Pallas kernels for 20%

profile of v3, /device:TPU:0, one launch (start us, length us, event | category | flops | bytes accessed | tf_op | source)
XLA Modules:
  0.0 1036.8 jit_solution(3354909399444736801)
XLA Ops:
  14.7 25.9 %collective-permute-done.4 = bf16[192,1536]{1,0:T(8,128)(2,1)S(1)} collective-permute-done((bf16[192,1536]{1,0:T(8,128)(2,1)S(1)}, bf16[192,1536]{1,0:T(8,128)(2,1)S(1)}, u32[]{:S(2)}, u32[]{:S(2)}) %collective-permute-start.4) | collective-permute-done | bytes 589856 | tf_op jit(solution)/shard_map/ppermute | solution.py:653
  78.5 28.3 %collective-permute-done.3 = bf16[256,1536]{1,0:T(8,128)(2,1)S(1)} collective-permute-done((bf16[256,1536]{1,0:T(8,128)(2,1)S(1)}, bf16[256,1536]{1,0:T(8,128)(2,1)S(1)}, u32[]{:S(2)}, u32[]{:S(2)}) %collective-permute-start.3) | collective-permute-done | bytes 786464 | tf_op jit(solution)/shard_map/ppermute | solution.py:648
  116.3 25.2 %collective-permute-done.10 = bf16[192,3456]{1,0:T(8,128)(2,1)} collective-permute-done((bf16[192,3456]{1,0:T(8,128)(2,1)}, bf16[192,3456]{1,0:T(8,128)(2,1)}, u32[]{:S(2)}, u32[]{:S(2)}) %collective-permute-start.10) | collective-permute-done | bytes 1327136 | tf_op jit(solution)/shard_map/ppermute | solution.py:653
  159.8 20.4 %collective-permute-done.6 = f32[8,512]{1,0:T(8,128)S(1)} collective-permute-done((f32[8,512]{1,0:T(8,128)S(1)}, f32[8,512]{1,0:T(8,128)S(1)}, u32[]{:S(2)}, u32[]{:S(2)}) %collective-permute-start.6) | collective-permute-done | bytes 16416 | tf_op jit(solution)/shard_map/ppermute | solution.py:653
  182.1 26.4 %shard_map.285 = (bf16[512,1024]{1,0:T(8,128)(2,1)S(1)}, f32[8,512,128]{2,1,0:T(8,128)S(1)}, f32[8,512,128]{2,1,0:T(8,128)}, bf16[512,1024]{1,0:T(8,128)(2,1)S(1)}, f32[8,128]{1,0:T(8,128)S(1)}) custom-call(f32[512,1024]{1,0:T(8,128)} %slice_add_fusion.7.lead, f32[512,1024]{1,0:T(8,128)} %slice_add_fusion.6.gate, s32[512,1]{1,0:T(8,128)S(1)} %add_subtract_fusion.offset, ...), custom_call_target="tpu_custom_call" | custom-call | tf_op jit(solution)/shard_map/pallas_call | solution.py:345
  215.9 29.2 %collective-permute-done.8 = bf16[256,1536]{1,0:T(8,128)(2,1)S(1)} collective-permute-done((bf16[256,1536]{1,0:T(8,128)(2,1)S(1)}, bf16[256,1536]{1,0:T(8,128)(2,1)S(1)}, u32[]{:S(2)}, u32[]{:S(2)}) %collective-permute-start.8) | collective-permute-done | bytes 786464 | tf_op jit(solution)/shard_map/ppermute | solution.py:648
  261.7 18.2 %collective-permute-done.11 = bf16[192,1152]{1,0:T(8,128)(2,1)S(1)} collective-permute-done((bf16[192,1152]{1,0:T(8,128)(2,1)}, bf16[192,1152]{1,0:T(8,128)(2,1)S(1)}, u32[]{:S(2)}, u32[]{:S(2)}) %collective-permute-start.11) | collective-permute-done | bytes 442400 | tf_op jit(solution)/shard_map/ppermute | solution.py:653
  295.0 10.8 %fusion.10 = f32[512,4608]{1,0:T(8,128)S(1)} fusion(bf16[1536,6912]{1,0:T(8,128)(2,1)} %all-gather.7.cloned.1.call-done, bf16[256,1536]{1,0:T(8,128)(2,1)} %copy-done.172, bf16[256,1536]{1,0:T(8,128)(2,1)} %copy-done.98), kind=kOutput, calls=%fused_computation.10 | convolution fusion | flops 7250903040 | bytes 25165824 | tf_op jit(solution)/shard_map/dot_general | solution.py:27
  311.6 29.1 %collective-permute-done.20 = bf16[192,3456]{1,0:T(8,128)(2,1)} collective-permute-done((bf16[192,3456]{1,0:T(8,128)(2,1)}, bf16[192,3456]{1,0:T(8,128)(2,1)}, u32[]{:S(2)}, u32[]{:S(2)}) %collective-permute-start.20) | collective-permute-done | bytes 1327136 | tf_op jit(solution)/shard_map/ppermute | solution.py:653
  371.2 18.8 %collective-permute-done.12 = bf16[256,1536]{1,0:T(8,128)(2,1)} collective-permute-done((bf16[256,1536]{1,0:T(8,128)(2,1)S(1)}, bf16[256,1536]{1,0:T(8,128)(2,1)}, u32[]{:S(2)}, u32[]{:S(2)}) %collective-permute-start.12) | collective-permute-done | bytes 786464 | tf_op jit(solution)/shard_map/ppermute | solution.py:648
  402.7 26.8 %collective-permute-done.13 = bf16[256,1536]{1,0:T(8,128)(2,1)} collective-permute-done((bf16[256,1536]{1,0:T(8,128)(2,1)}, bf16[256,1536]{1,0:T(8,128)(2,1)}, u32[]{:S(2)}, u32[]{:S(2)}) %collective-permute-start.13) | collective-permute-done | bytes 786464 | tf_op jit(solution)/shard_map/ppermute | solution.py:648
  452.2 27.6 %shard_map.286 = (bf16[512,1024]{1,0:T(8,128)(2,1)S(1)}, f32[8,512,128]{2,1,0:T(8,128)S(1)}, f32[8,512,128]{2,1,0:T(8,128)}, bf16[512,1024]{1,0:T(8,128)(2,1)S(1)}, f32[8,128]{1,0:T(8,128)S(1)}) custom-call(f32[512,1024]{1,0:T(8,128)} %slice_add_fusion.5.lead, f32[512,1024]{1,0:T(8,128)} %slice_add_fusion.4.gate, s32[512,1]{1,0:T(8,128)S(1)} %add_subtract_fusion.offset, ...), custom_call_target="tpu_custom_call" | custom-call | tf_op jit(solution)/shard_map/pallas_call | solution.py:345
  490.2 22.8 %collective-permute-done.18 = bf16[256,1536]{1,0:T(8,128)(2,1)} collective-permute-done((bf16[256,1536]{1,0:T(8,128)(2,1)S(1)}, bf16[256,1536]{1,0:T(8,128)(2,1)}, u32[]{:S(2)}, u32[]{:S(2)}) %collective-permute-start.18) | collective-permute-done | bytes 786464 | tf_op jit(solution)/shard_map/ppermute | solution.py:648
  519.9 15.5 %collective-permute-done.19 = bf16[256,1536]{1,0:T(8,128)(2,1)S(1)} collective-permute-done((bf16[256,1536]{1,0:T(8,128)(2,1)S(1)}, bf16[256,1536]{1,0:T(8,128)(2,1)S(1)}, u32[]{:S(2)}, u32[]{:S(2)}) %collective-permute-start.19) | collective-permute-done | bytes 786464 | tf_op jit(solution)/shard_map/ppermute | solution.py:648
  558.8 13.7 %multiply_convert_fusion.3 = (bf16[512,2304]{1,0:T(8,128)(2,1)S(1)}, bf16[512,2304]{1,0:T(8,128)(2,1)S(1)}, bf16[512,2304]{1,0:T(8,128)(2,1)}) fusion(f32[512,2304]{1,0:T(8,128)} %slice_add_fusion.1, f32[512,2304]{1,0:T(8,128)S(1)} %copy-done.48, f32[512,4608]{1,0:T(8,128)} %copy-done.76, f32[512,2304]{1,0:T(8,128)} %fusion.145, ...), kind=kOutput, calls=%fused_computation.71 | convolution fusion | flops 3662807040 | bytes 34603008 | tf_op jit(solution)/shard_map/dot_general | solution.py:27
  603.7 10.7 %fusion.2 = f32[256,1536]{1,0:T(8,128)} fusion(bf16[1536,6912]{1,0:T(8,128)(2,1)} %all-gather.11.cloned.1.call-done, bf16[512,2304]{1,0:T(8,128)(2,1)} %copy-done.39, bf16[512,2304]{1,0:T(8,128)(2,1)} %get-tuple-element.114), kind=kOutput, calls=%fused_computation.2 | convolution fusion | flops 3628597248 | bytes 20447232 | tf_op jit(solution)/shard_map/dot_general | solution.py:31
  639.2 17.5 %collective-permute-done.25 = bf16[256,1536]{1,0:T(8,128)(2,1)} collective-permute-done((bf16[256,1536]{1,0:T(8,128)(2,1)}, bf16[256,1536]{1,0:T(8,128)(2,1)}, u32[]{:S(2)}, u32[]{:S(2)}) %collective-permute-start.25) | collective-permute-done | bytes 786464 | tf_op jit(solution)/shard_map/ppermute | solution.py:648
  665.7 29.2 %shard_map.287 = bf16[512,2048]{1,0:T(8,128)(2,1)S(1)} custom-call(f32[512,1024]{1,0:T(8,128)} %fusion.92.grad, f32[512,1024]{1,0:T(8,128)} %slice_add_fusion.4.gate, f32[8,512,128]{2,1,0:T(8,128)} %get-tuple-element.78.hidden, f32[8,512,128]{2,1,0:T(8,128)} %copy-done.7, f32[8,128]{1,0:T(8,128)S(1)} %get-tuple-element.80.carry, ...), custom_call_target="tpu_custom_call" | custom-call | tf_op jit(solution)/shard_map/pallas_call | solution.py:345
  729.8 15.4 %collective-permute-done.27 = bf16[256,1536]{1,0:T(8,128)(2,1)} collective-permute-done((bf16[256,1536]{1,0:T(8,128)(2,1)}, bf16[256,1536]{1,0:T(8,128)(2,1)}, u32[]{:S(2)}, u32[]{:S(2)}) %collective-permute-start.27) | collective-permute-done | bytes 786464 | tf_op jit(solution)/shard_map/ppermute | solution.py:648
  747.9 11.6 %multiply_convert_fusion = (bf16[512,2304]{1,0:T(8,128)(2,1)S(1)}, bf16[512,2304]{1,0:T(8,128)(2,1)S(1)}) fusion(f32[512,2304]{1,0:T(8,128)} %get-tuple-element.244, f32[512,2304]{1,0:T(8,128)} %fusion.160, f32[512,4608]{1,0:T(8,128)} %copy-done.77, f32[512,2304]{1,0:T(8,128)S(1)} %fusion.156, bf16[1536,6912]{1,0:T(8,128)(2,1)} %all-gather.7.cloned.1.call-done, ...), kind=kOutput, calls=%fused_computation.66 | convolution fusion | flops 3655335936 | bytes 32243712 | tf_op jit(solution)/shard_map/dot_general | solution.py:27
  825.5 12.8 %collective-permute-done.29 = bf16[256,1536]{1,0:T(8,128)(2,1)} collective-permute-done((bf16[256,1536]{1,0:T(8,128)(2,1)S(1)}, bf16[256,1536]{1,0:T(8,128)(2,1)}, u32[]{:S(2)}, u32[]{:S(2)}) %collective-permute-start.29) | collective-permute-done | bytes 786464 | tf_op jit(solution)/shard_map/ppermute | solution.py:648
  846.3 33.3 %shard_map.288 = bf16[512,2048]{1,0:T(8,128)(2,1)S(1)} custom-call(f32[512,1024]{1,0:T(8,128)} %fusion.89.grad, f32[512,1024]{1,0:T(8,128)} %slice_add_fusion.6.gate, f32[8,512,128]{2,1,0:T(8,128)} %get-tuple-element.82.hidden, f32[8,512,128]{2,1,0:T(8,128)} %copy-done.6, f32[8,128]{1,0:T(8,128)S(1)} %get-tuple-element.84.carry, ...), custom_call_target="tpu_custom_call" | custom-call | tf_op jit(solution)/shard_map/pallas_call | solution.py:345
  893.8 88.8 %shard_map.289 = (f32[1024,384]{1,0:T(8,128)}, f32[128,1536]{1,0:T(8,128)S(1)}, f32[64,1536]{1,0:T(8,128)S(1)}, f32[128,1536]{1,0:T(8,128)S(1)}, f32[64,1536]{1,...) custom-call(f32[256,1536]{1,0:T(8,128)} %fusion.54.own_part, ...), custom_call_target="tpu_custom_call" | custom-call | tf_op jit(solution)/shard_map/pallas_call | solution.py:345
  1003.6 18.1 %collective-permute-done.30 = bf16[192,512]{1,0:T(8,128)(2,1)S(1)} collective-permute-done((bf16[192,512]{1,0:T(8,128)(2,1)S(1)}, bf16[192,512]{1,0:T(8,128)(2,1)S(1)}, u32[]{:S(2)}, u32[]{:S(2)}) %collective-permute-start.30) | collective-permute-done | bytes 196640 | tf_op jit(solution)/shard_map/ppermute | solution.py:658
  (704 shorter events, 434.4 us)
Async XLA Ops:
  7.2 100.6 %all-gather.5.cloned.1.call-start = ((), (), s32[]{:S(2)}) async-start(), calls=%async_computation.4 | async-start | bytes 10616832 | tf_op jit(solution)/shard_map/all_gather | solution.py:939
  50.5 244.5 %all-gather.7.cloned.1.call-start = ((), (), s32[]{:S(2)}) async-start(), calls=%async_computation.5 | async-start | bytes 23887872 | tf_op jit(solution)/shard_map/all_gather | solution.py:939
  71.6 35.2 %collective-permute-start.3 = (bf16[256,1536]{1,0:T(8,128)(2,1)S(1)}, bf16[256,1536]{1,0:T(8,128)(2,1)S(1)}, u32[]{:S(2)}, u32[]{:S(2)}) collective-permute-start(bf16[256,1536]{1,0:T(8,128)(2,1)S(1)} %multiply_convert_fusion.7), channel_id=1, source_target_pairs={{0,1},{1,0},{2,3},{3,2},{4,5},{5,4},{6,7},{7,6},{8,9},{9,8},{10,11... | collective-permute-start | bytes 2359304 | tf_op jit(solution)/shard_map/ppermute | solution.py:648
  73.7 33.7 %collective-permute-start.5 = (bf16[192,512]{1,0:T(8,128)(2,1)S(1)}, bf16[192,512]{1,0:T(8,128)(2,1)S(1)}, u32[]{:S(2)}, u32[]{:S(2)}) collective-permute-start(bf16[192,512]{1,0:T(8,128)(2,1)S(1)} %get-tuple-element.54), channel_id=1, source_target_pairs={{2,0},{3,1},{0,2},{1,3},{6,4},{7,5},{4,6},{5,7},{10,8},{11,9},{8,1... | collective-permute-start | bytes 589832 | tf_op jit(solution)/shard_map/ppermute | solution.py:653
  76.1 65.4 %collective-permute-start.10 = (bf16[192,3456]{1,0:T(8,128)(2,1)}, bf16[192,3456]{1,0:T(8,128)(2,1)}, u32[]{:S(2)}, u32[]{:S(2)}) collective-permute-start(bf16[192,3456]{1,0:T(8,128)(2,1)} %pad_maximum_fusion.12), channel_id=1, source_target_pairs={{2,0},{3,1},{0,2},{1,3},{6,4},{7,5},{4,6},{5,7},{10,8},{11,9},{8,1... | collective-permute-start | bytes 3981320 | tf_op jit(solution)/shard_map/ppermute | solution.py:653
  150.7 291.6 %all-gather.9.cloned.1.call-start = ((), (), s32[]{:S(2)}) async-start(), calls=%async_computation.6 | async-start | bytes 10616832 | tf_op jit(solution)/shard_map/all_gather | solution.py:939
  213.1 32.1 %collective-permute-start.8 = (bf16[256,1536]{1,0:T(8,128)(2,1)S(1)}, bf16[256,1536]{1,0:T(8,128)(2,1)S(1)}, u32[]{:S(2)}, u32[]{:S(2)}) collective-permute-start(bf16[256,1536]{1,0:T(8,128)(2,1)S(1)} %fusion.62), channel_id=1, source_target_pairs={{0,1},{1,0},{2,3},{3,2},{4,5},{5,4},{6,7},{7,6},{8,9},{9,8},{10,11... | collective-permute-start | bytes 2359304 | tf_op jit(solution)/shard_map/ppermute | solution.py:648
  213.6 34.8 %collective-permute-start.14 = (bf16[192,1536]{1,0:T(8,128)(2,1)S(1)}, bf16[192,1536]{1,0:T(8,128)(2,1)S(1)}, u32[]{:S(2)}, u32[]{:S(2)}) collective-permute-start(bf16[192,1536]{1,0:T(8,128)(2,1)S(1)} %pad_maximum_fusion.23), channel_id=1, source_target_pairs={{2,0},{3,1},{0,2},{1,3},{6,4},{7,5},{4,6},{5,7},{10,8},{11,9},{8,1... | collective-permute-start | bytes 1769480 | tf_op jit(solution)/shard_map/ppermute | solution.py:653
  251.9 288.0 %all-gather.11.cloned.1.call-start = ((), (), s32[]{:S(2)}) async-start(), calls=%async_computation.7 | async-start | bytes 23887872 | tf_op jit(solution)/shard_map/all_gather | solution.py:939
  258.4 32.7 %collective-permute-start.9 = (bf16[256,1536]{1,0:T(8,128)(2,1)S(1)}, bf16[256,1536]{1,0:T(8,128)(2,1)S(1)}, u32[]{:S(2)}, u32[]{:S(2)}) collective-permute-start(bf16[256,1536]{1,0:T(8,128)(2,1)S(1)} %multiply_convert_fusion.6), channel_id=1, source_target_pairs={{0,1},{1,0},{2,3},{3,2},{4,5},{5,4},{6,7},{7,6},{8,9},{9,8},{10,11... | collective-permute-start | bytes 2359304 | tf_op jit(solution)/shard_map/ppermute | solution.py:648
  279.9 60.8 %collective-permute-start.20 = (bf16[192,3456]{1,0:T(8,128)(2,1)}, bf16[192,3456]{1,0:T(8,128)(2,1)}, u32[]{:S(2)}, u32[]{:S(2)}) collective-permute-start(bf16[192,3456]{1,0:T(8,128)(2,1)} %pad_maximum_fusion.13), channel_id=1, source_target_pairs={{2,0},{3,1},{0,2},{1,3},{6,4},{7,5},{4,6},{5,7},{10,8},{11,9},{8,1... | collective-permute-start | bytes 3981320 | tf_op jit(solution)/shard_map/ppermute | solution.py:653
  361.1 32.4 %all-to-all-start.3 = ((bf16[4,256,384]{2,1,0:T(8,128)(2,1)}), bf16[4,256,384]{2,1,0:T(8,128)(2,1)}, u32[]{:S(2)}, u32[]{:S(2)}) async-start(bf16[4,256,384]{2,1,0:T(8,128)(2,1)} %bitcast.72), calls=%async_computation.3 | async-start | bytes 1572864 | tf_op jit(solution)/shard_map/all_to_all | solution.py:680
  392.9 36.6 %collective-permute-start.13 = (bf16[256,1536]{1,0:T(8,128)(2,1)}, bf16[256,1536]{1,0:T(8,128)(2,1)}, u32[]{:S(2)}, u32[]{:S(2)}) collective-permute-start(bf16[256,1536]{1,0:T(8,128)(2,1)} %multiply_convert_fusion.5), channel_id=1, source_target_pairs={{0,1},{1,0},{2,3},{3,2},{4,5},{5,4},{6,7},{7,6},{8,9},{9,8},{10,11... | collective-permute-start | bytes 2359304 | tf_op jit(solution)/shard_map/ppermute | solution.py:648
  395.6 90.1 %collective-permute-start.23 = (bf16[256,1536]{1,0:T(8,128)(2,1)}, bf16[256,1536]{1,0:T(8,128)(2,1)}, u32[]{:S(2)}, u32[]{:S(2)}) collective-permute-start(bf16[256,1536]{1,0:T(8,128)(2,1)} %bitcast.167), channel_id=1, source_target_pairs={{0,1},{1,0},{2,3},{3,2},{4,5},{5,4},{6,7},{7,6},{8,9},{9,8},{10,11... | collective-permute-start | bytes 2359304 | tf_op jit(solution)/shard_map/ppermute | solution.py:648
  397.7 41.7 %collective-permute-start.15 = (bf16[192,512]{1,0:T(8,128)(2,1)}, bf16[192,512]{1,0:T(8,128)(2,1)S(1)}, u32[]{:S(2)}, u32[]{:S(2)}) collective-permute-start(bf16[192,512]{1,0:T(8,128)(2,1)} %get-tuple-element.67), channel_id=1, source_target_pairs={{2,0},{3,1},{0,2},{1,3},{6,4},{7,5},{4,6},{5,7},{10,8},{11,9},{8,1... | collective-permute-start | bytes 589832 | tf_op jit(solution)/shard_map/ppermute | solution.py:653
  397.7 43.8 %collective-permute-start.17 = (bf16[2,2,256,256]{3,2,1,0:T(8,128)(2,1)}, bf16[2,2,256,256]{3,2,1,0:T(8,128)(2,1)S(1)}, u32[]{:S(2)}, u32[]{:S(2)}) collective-permute-start(bf16[2,2,256,256]{3,2,1,0:T(8,128)(2,1)} %get-tuple-element.71), channel_id=1, source_target_pairs={{2,0},{3,1},{0,2},{1,3},{6,4},{7,5},{4,6},{5,7},{10,8},{11,9},{8,1... | collective-permute-start | bytes 1572872 | tf_op jit(solution)/shard_map/ppermute | solution.py:653
  400.6 38.7 %collective-permute-start.16 = (f32[8,512]{1,0:T(8,128)S(1)}, f32[8,512]{1,0:T(8,128)S(1)}, u32[]{:S(2)}, u32[]{:S(2)}) collective-permute-start(f32[8,512]{1,0:T(8,128)S(1)} %copy-done.143), channel_id=1, source_target_pairs={{2,0},{3,1},{0,2},{1,3},{6,4},{7,5},{4,6},{5,7},{10,8},{11,9},{8,1... | collective-permute-start | bytes 49160 | tf_op jit(solution)/shard_map/ppermute | solution.py:653
  624.8 31.8 %collective-permute-start.25 = (bf16[256,1536]{1,0:T(8,128)(2,1)}, bf16[256,1536]{1,0:T(8,128)(2,1)}, u32[]{:S(2)}, u32[]{:S(2)}) collective-permute-start(bf16[256,1536]{1,0:T(8,128)(2,1)} %get-tuple-element.108), channel_id=1, source_target_pairs={{0,1},{1,0},{2,3},{3,2},{4,5},{5,4},{6,7},{7,6},{8,9},{9,8},{10,11... | collective-permute-start | bytes 2359304 | tf_op jit(solution)/shard_map/ppermute | solution.py:648
  634.5 159.9 %all-to-all-start.2 = ((bf16[256,4,384]{2,0,1:T(8,128)(2,1)}), bf16[256,4,384]{2,0,1:T(8,128)(2,1)}, u32[]{:S(2)}, u32[]{:S(2)}) async-start(bf16[256,4,384]{2,0,1:T(8,128)(2,1)} %bitcast.412), calls=%async_computation.2 | async-start | bytes 1572864 | tf_op jit(solution)/shard_map/all_to_all | solution.py:684
  638.7 346.1 %all-reduce.4.cloned.1.call-start = ((), (), s32[]{:S(2)}) async-start(), calls=%async_computation.8 | async-start | bytes 2359296 | tf_op jit(solution)/shard_map/psum | solution.py:840
  705.7 283.2 %all-reduce.6.cloned.1.call-start = ((), (), s32[]{:S(2)}) async-start(), calls=%async_computation.9 | async-start | bytes 2555904 | tf_op jit(solution)/shard_map/psum | solution.py:842
  806.2 32.1 %collective-permute-start.29 = (bf16[256,1536]{1,0:T(8,128)(2,1)S(1)}, bf16[256,1536]{1,0:T(8,128)(2,1)}, u32[]{:S(2)}, u32[]{:S(2)}) collective-permute-start(bf16[256,1536]{1,0:T(8,128)(2,1)S(1)} %get-tuple-element.104), channel_id=1, source_target_pairs={{0,1},{1,0},{2,3},{3,2},{4,5},{5,4},{6,7},{7,6},{8,9},{9,8},{10,11... | collective-permute-start | bytes 2359304 | tf_op jit(solution)/shard_map/ppermute | solution.py:648
  990.1 34.2 %collective-permute-start.31 = (bf16[192,1152]{1,0:T(8,128)(2,1)S(1)}, bf16[192,1152]{1,0:T(8,128)(2,1)S(1)}, u32[]{:S(2)}, u32[]{:S(2)}) collective-permute-start(bf16[192,1152]{1,0:T(8,128)(2,1)S(1)} %slice.866), channel_id=1, source_target_pairs={{0,2},{1,3},{2,0},{3,1},{4,6},{5,7},{6,4},{7,5},{8,10},{9,11},{10,... | collective-permute-start | bytes 1327112 | tf_op jit(solution)/shard_map/ppermute | solution.py:658
  991.6 30.1 %collective-permute-start.30 = (bf16[192,512]{1,0:T(8,128)(2,1)S(1)}, bf16[192,512]{1,0:T(8,128)(2,1)S(1)}, u32[]{:S(2)}, u32[]{:S(2)}) collective-permute-start(bf16[192,512]{1,0:T(8,128)(2,1)S(1)} %slice.844), channel_id=1, source_target_pairs={{0,2},{1,3},{2,0},{3,1},{4,6},{5,7},{6,4},{7,5},{8,10},{9,11},{10,... | collective-permute-start | bytes 589832 | tf_op jit(solution)/shard_map/ppermute | solution.py:658
  (201 other events, 2665.7 us)
Sparse Core Ops, SparseCore 0:
  41.9 60.0 all-gather.4
  150.8 109.9 all-gather.6
  263.3 58.8 all-gather.8
  349.9 107.0 all-gather.10
  705.8 133.9 all-reduce.3
  843.3 58.2 all-reduce.5

commit v4 on v3

--- a/solution.py
+++ b/solution.py
@@ -340,14 +340,21 @@
         branch_grad[pl.ds(pl.multiple_of(other + half - 16, 16), 16), at] = tails_pair
 
 
-def block_call(kernel, ident, operands, outs, scratch):
-    whole = pl.BlockSpec(memory_space=pltpu.VMEM)
+def lasting(microseconds):
+    return pl.CostEstimate(
+        flops=int(microseconds * 1.1e9), bytes_accessed=int(microseconds * 3e6), transcendentals=0
+    )
+
+
+def block_call(kernel, ident, operands, outs, scratch, microseconds, anywhere=0):
+    whole, open_place = pl.BlockSpec(memory_space=pltpu.VMEM), pl.BlockSpec(memory_space=pl.ANY)
     return pl.pallas_call(
         kernel,
         out_shape=[jax.ShapeDtypeStruct(*out) for out in outs],
-        in_specs=[whole] * len(operands),
-        out_specs=[whole] * len(outs),
+        in_specs=[whole] * (len(operands) - anywhere) + [open_place] * anywhere,
+        out_specs=[whole] * (len(outs) - anywhere) + [open_place] * anywhere,
         scratch_shapes=scratch,
+        cost_estimate=lasting(microseconds),
         compiler_params=pltpu.CompilerParams(
             vmem_limit_bytes=VMEM_BYTES, collective_id=ident, has_side_effects=True
         ),
@@ -386,6 +393,7 @@
             pltpu.VMEM((8, width), FLOAT),
         ]
         + message_scratch(width),
+        27,
     )
 
 
@@ -414,6 +422,7 @@
             pltpu.VMEM((8, width), FLOAT),
         ]
         + message_scratch(width),
+        30,
     )[0]
 
 
@@ -453,19 +462,16 @@
     )
 
 
-def closing_kernel(
-    own_part, other_part, stream, d_middle, gain,
-    shared_a, shared_b, shared_c, shared_d, split_a, split_b, split_c, split_d,
-    tokens_out, shared_out_a, shared_out_b, shared_out_c, shared_out_d,
-    split_out_a, split_out_b, split_out_c, split_out_d,
-    received, outgoing, flat, inbox, red, red_split, zbox, sbox, zfull, sfull, shared_all,
-    split_all, pair_sems, row_sems, col_sems, turn_sems, spread_sems, shared_sems, split_sems,
-    token_sems,
-):
-    shared = (shared_a, shared_b, shared_c, shared_d)
-    split = (split_a, split_b, split_c, split_d)
-    shared_out = (shared_out_a, shared_out_b, shared_out_c, shared_out_d)
-    split_out = (split_out_a, split_out_b, split_out_c, split_out_d)
+def closing_kernel(count, *refs):
+    own_part, other_part, stream, d_middle, gain = refs[:5]
+    shared, split = refs[5 : 5 + count], refs[5 + count : 5 + 2 * count]
+    tokens_out, *refs = refs[5 + 2 * count :]
+    shared_out, split_out = refs[:count], refs[count : 2 * count]
+    (
+        received, outgoing, homing, flat, beside_in, both, inbox, red, red_split, zbox, sbox, zfull,
+        sfull, shared_all, split_all, pair_sems, beside_sems, row_sems, col_sems, turn_sems,
+        spread_sems, shared_sems, split_sems, token_sems,
+    ) = refs[2 * count :]
     peers, cols = lax.axis_size("row"), lax.axis_size("col")
     shards = cols // 2
     row, col = lax.axis_index("row"), lax.axis_index("col")
@@ -474,13 +480,18 @@
     unit, part = zbox.shape[1], sbox.shape[1]
     shared_lines = cols * unit
 
+    side, place, places = row % 2, row // 2, peers // 2
+    beside = (row + 1 - 2 * side, col)
+
+    def along(by):
+        return (((place + by) % places) * 2 + side, col)
+
     barrier = pltpu.get_barrier_semaphore()
-    for by in range(1, peers):
-        pl.semaphore_signal(
-            barrier, inc=1, device_id=((row + by) % peers, col), device_id_type=MESH
-        )
-    for by in range(1, cols):
-        pl.semaphore_signal(barrier, inc=1, device_id=(row, (col + by) % cols), device_id_type=MESH)
+    greeted = [beside]
+    greeted += [along(by) for by in range(1, places)]
+    greeted += [(row, (col + by) % cols) for by in range(1, cols)]
+    for to in greeted:
+        pl.semaphore_signal(barrier, inc=1, device_id=to, device_id_type=MESH)
 
     sizes = [value.shape for value in shared]
     shared_plan = line_plan(sizes, unit)
@@ -488,28 +499,36 @@
     split_plan = line_plan(thin, part)
     flat[...] = jnp.zeros(flat.shape, BRAIN)
     for at, rows, lanes, index, lines in shared_plan:
-        begin = index % cols * unit
-        flat[index // cols, begin + lines.start : begin + lines.stop] = shared[at][
+        begin, owner = index % cols * unit, index // cols
+        flat[owner % 2, owner // 2, begin + lines.start : begin + lines.stop] = shared[at][
             rows, lanes
         ].astype(BRAIN)
     for turn in range(shards):
         for at, rows, lanes, index, lines in split_plan:
             begin = shared_lines + turn * part
             skip = turn * thin[at][1]
-            flat[index, begin + lines.start : begin + lines.stop] = split[at][
+            flat[index % 2, index // 2, begin + lines.start : begin + lines.stop] = split[at][
                 rows, skip + lanes.start : skip + lanes.stop
             ].astype(BRAIN)
-    pl.semaphore_wait(barrier, peers + cols - 2)
-
+    pl.semaphore_wait(barrier, len(greeted))
+
+    paired = remote(flat.at[1 - side], beside_in, beside_sems, 0, beside)
+    paired.start()
     pair = remote(other_part, received, pair_sems, 0, (row, col + 1 - 2 * (col % 2)))
     pair.start()
+    paired.wait()
+
+    def add_pair(at, nothing):
+        both[at] = (flat[side, at].astype(FLOAT) + beside_in[at].astype(FLOAT)).astype(BRAIN)
+        return nothing
+
+    lax.fori_loop(0, places, add_pair, 0)
     scattered = []
-    for by in range(1, peers):
-        to = (row + by) % peers
-        copy = remote(flat.at[to], inbox.at[by - 1], row_sems, by - 1, (to, col))
+    for by in range(1, places):
+        to = (place + by) % places
+        copy = remote(both.at[to], inbox.at[by - 1], row_sems, by - 1, along(by))
         copy.start()
         scattered.append(copy)
-
     pair.wait()
 
     def norm_rows(at, nothing):
@@ -520,23 +539,14 @@
         total = jnp.mean(gained * value, axis=1, keepdims=True)
         result = d_middle[lines] + scale * gained - value * (scale * scale * scale * total)
         for to in range(cols):
-            outgoing[to, lines] = result[:, to * piece : (to + 1) * piece]
+            outgoing[to, lines] = result[:, to * piece : (to + 1) * piece].astype(BRAIN)
         return nothing
 
     lax.fori_loop(0, own // 16, norm_rows, 0)
-    mine = pl.ds(pl.multiple_of(col * own, own), own)
-    returned = []
-    for by in range(1, cols):
-        to = (col + by) % cols
-        copy = remote(outgoing.at[to], tokens_out.at[mine], token_sems, by - 1, (row, to))
-        copy.start()
-        returned.append(copy)
-    tokens_out[mine] = outgoing[col]
-
     for copy in scattered:
         copy.wait()
-    total = flat[row].astype(FLOAT)
-    for by in range(1, peers):
+    total = both[place].astype(FLOAT)
+    for by in range(1, places):
         total = total + inbox[by - 1].astype(FLOAT)
     for at in range(cols):
         red[at] = total[at * unit : (at + 1) * unit].astype(BRAIN)
@@ -571,28 +581,46 @@
         copy.start()
         spread.append(copy)
     last = []
-    for by in range(1, peers):
-        to = (row + by) % peers
-        copy = remote(sfull, split_all.at[row], split_sems, by - 1, (to, col))
+    for by in range(1, places):
+        copy = remote(sfull, split_all.at[side, place], split_sems, by - 1, along(by))
         copy.start()
         last.append(copy)
-    split_all[row] = sfull[...]
+    split_all[side, place] = sfull[...]
     for copy in spread:
         copy.wait()
-    for by in range(1, peers):
-        to = (row + by) % peers
-        copy = remote(zfull, shared_all.at[row], shared_sems, by - 1, (to, col))
+    for by in range(1, places):
+        copy = remote(zfull, shared_all.at[side, place], shared_sems, by - 1, along(by))
         copy.start()
         last.append(copy)
-    shared_all[row] = zfull[...]
+    shared_all[side, place] = zfull[...]
+    returned = []
+    for by in range(1, cols):
+        to = (col + by) % cols
+        copy = remote(outgoing.at[to], homing.at[col], token_sems, by - 1, (row, to))
+        copy.start()
+        returned.append(copy)
+    homing[col] = outgoing[col]
     for copy in last:
         copy.wait()
+    lanes_over = [
+        remote(split_all.at[side], split_all.at[side], beside_sems, 1, beside),
+        remote(shared_all.at[side], shared_all.at[side], beside_sems, 2, beside),
+    ]
+    for copy in lanes_over:
+        copy.start()
+    for copy in lanes_over:
+        copy.wait()
     for at, rows, lanes, index, lines in shared_plan:
-        shared_out[at][rows, lanes] = shared_all[index // cols, index % cols, lines].astype(FLOAT)
+        owner = index // cols
+        shared_out[at][rows, lanes] = shared_all[
+            owner % 2, owner // 2, index % cols, lines
+        ].astype(FLOAT)
     for at, rows, lanes, index, lines in split_plan:
-        split_out[at][rows, lanes] = split_all[index, lines].astype(FLOAT)
+        split_out[at][rows, lanes] = split_all[index % 2, index // 2, lines].astype(FLOAT)
     for copy in returned:
         copy.wait()
+    for at in range(cols):
+        tokens_out[at * own : (at + 1) * own] = homing[at].astype(FLOAT)
 
 
 def close(own_part, other_part, stream, d_middle, gain, shared, split):
@@ -609,15 +637,16 @@
     split = [widened(value) if piece % LANES else value for value, piece in zip(split, pieces)]
     shared_sizes = [value.shape for value in shared]
     split_sizes = [value.shape for value in split]
+    places = peers // 2
     unit, part = closing_sizes(shared_sizes, split_sizes, peers, cols, shards)
     lines = cols * unit + shards * part
     sems = [
         pltpu.SemaphoreType.DMA((2, count))
-        for count in (1, peers - 1, cols - 1, max(shards - 1, 1), cols - 1, peers - 1, peers - 1,
-                      cols - 1)
+        for count in (1, 3, places - 1, cols - 1, max(shards - 1, 1), cols - 1, places - 1,
+                      places - 1, cols - 1)
     ]
     result = block_call(
-        closing_kernel,
+        partial(closing_kernel, len(shared)),
         2,
         [own_part, other_part, stream, d_middle, gain, *shared, *split],
         [((own * cols, d_model // cols), FLOAT)]
@@ -625,22 +654,327 @@
         + [((rows, columns // shards), FLOAT) for rows, columns in split_sizes],
         [
             pltpu.VMEM((own, d_model), BRAIN),
-            pltpu.VMEM((cols, own, d_model // cols), FLOAT),
-            pltpu.VMEM((peers, lines, LANES), BRAIN),
-            pltpu.VMEM((peers - 1, lines, LANES), BRAIN),
+            pltpu.VMEM((cols, own, d_model // cols), BRAIN),
+            pltpu.VMEM((cols, own, d_model // cols), BRAIN),
+            pltpu.VMEM((2, places, lines, LANES), BRAIN),
+            pltpu.VMEM((places, lines, LANES), BRAIN),
+            pltpu.VMEM((places, lines, LANES), BRAIN),
+            pltpu.VMEM((places - 1, lines, LANES), BRAIN),
             pltpu.VMEM((cols, unit, LANES), BRAIN),
             pltpu.VMEM((shards, part, LANES), BRAIN),
             pltpu.VMEM((cols - 1, unit, LANES), BRAIN),
             pltpu.VMEM((max(shards - 1, 1), part, LANES), BRAIN),
             pltpu.VMEM((cols, unit, LANES), BRAIN),
             pltpu.VMEM((part, LANES), BRAIN),
-            pltpu.VMEM((peers, cols, unit, LANES), BRAIN),
-            pltpu.VMEM((peers, part, LANES), BRAIN),
+            pltpu.VMEM((2, places, cols, unit, LANES), BRAIN),
+            pltpu.VMEM((2, places, part, LANES), BRAIN),
         ]
         + sems,
-    )
-    split = [value[:, :piece] for value, piece in zip(result[5:9], pieces)]
-    return result[0], result[1:5], split
+        80,
+    )
+    count = len(shared)
+    split = [value[:, :piece] for value, piece in zip(result[1 + count :], pieces)]
+    return result[0], result[1 : 1 + count], split
+
+
+def opening_kernel(count, routes, *refs):
+    small, refs = refs[:count], refs[count:]
+    tokens, gains, vectors, pack, *refs = refs
+    small_out, refs = refs[:count], refs[count:]
+    tokens_out, gains_out, vectors_out, packs_out, *refs = refs
+    flat, got, others, across_sems, spread_sems, *refs = refs
+    peers, cols = lax.axis_size("row"), lax.axis_size("col")
+    shards = cols // 2
+    row, col = lax.axis_index("row"), lax.axis_index("col")
+    plan = line_plan([value.shape for value in small], flat.shape[1])
+    barrier = pltpu.get_barrier_semaphore()
+    signals = [(row, (col + by) % cols) for by in range(1, cols)]
+    signals += [((row + by) % peers, col) for by in range(1, peers)]
+    for to in signals:
+        pl.semaphore_signal(barrier, inc=1, device_id=to, device_id_type=MESH)
+    flat[...] = jnp.zeros(flat.shape, BRAIN)
+    for at, rows, lanes, index, lines in plan:
+        flat[index, lines] = small[at][rows, lanes]
+    pl.semaphore_wait(barrier, len(signals))
+
+    across, copies = [], []
+    for turn in range(1, shards):
+        to = (row, (col + cols - 2 * turn) % cols)
+        across.append(remote(flat.at[row], got.at[turn - 1], across_sems, turn - 1, to))
+    for copy in across:
+        copy.start()
+    token_got, vector_got, token_sems, gain_sems, vector_sems, pack_sems = refs
+    own, piece = tokens_out.shape[0], tokens.shape[1]
+    for turn in range(1, shards):
+        to = (row, (col + cols - 2 * turn) % cols)
+        copies.append(remote(vectors, vector_got.at[turn - 1], vector_sems, turn - 1, to))
+    copies += shipped(routes, [pack], [packs_out], pack_sems)
+    for by in range(1, cols):
+        to = (col + by) % cols
+        there = pl.ds(pl.multiple_of(to * own, own), own)
+        copies.append(remote(tokens.at[there], token_got.at[col], token_sems, by - 1, (row, to)))
+        copies.append(remote(gains, gains_out.at[col], gain_sems, by - 1, (row, to)))
+    for copy in copies:
+        copy.start()
+    token_got[col] = tokens[pl.ds(pl.multiple_of(col * own, own), own)]
+    gains_out[col] = gains[...]
+    spread = []
+    for turn in range(1, shards):
+        across[turn - 1].wait()
+        for by in range(1, peers):
+            to = ((row + by) % peers, col)
+            slot = (turn - 1) * (peers - 1) + by - 1
+            copy = remote(got.at[turn - 1], others.at[turn - 1, row], spread_sems, slot, to)
+            copy.start()
+            spread.append(copy)
+        others[turn - 1, row] = got[turn - 1]
+    for at in range(count):
+        small_out[at][0] = small[at][...]
+    for copy in copies:
+        copy.wait()
+    for at in range(cols):
+        tokens_out[:, at * piece : (at + 1) * piece] = token_got[at]
+    vectors_out[0] = vectors[...]
+    for turn in range(1, shards):
+        vectors_out[turn] = vector_got[turn - 1]
+    for copy in spread:
+        copy.wait()
+    for turn in range(1, shards):
+        for at, rows, lanes, index, lines in plan:
+            small_out[at][turn, rows, lanes] = others[turn - 1, index, lines]
+
+
+def open_up(ident, small, tokens, gains, vectors, pack):
+    peers, cols = lax.axis_size("row"), lax.axis_size("col")
+    shards = cols // 2
+    rest = max(shards - 1, 1)
+    kept = [value.shape[1] for value in small]
+    small = [
+        jnp.pad(value, ((0, 0), (0, -value.shape[1] % LANES))) if value.shape[1] % LANES else value
+        for value in small
+    ]
+    lines = sum(value.shape[0] * value.shape[1] for value in small) // LANES
+    unit = -(-lines // (peers * 16)) * 16
+    rows, piece = tokens.shape
+    own = rows // cols
+    routes = routes_of(pack.shape[1], range(PARTS), 0, 0)
+    operands = [*small, tokens, gains, vectors, pack]
+    outs = [((shards,) + value.shape, BRAIN) for value in small]
+    outs += [
+        ((own, piece * cols), BRAIN),
+        ((cols,) + gains.shape, FLOAT),
+        ((shards,) + vectors.shape, FLOAT),
+        ((pack.shape[0], pack.shape[1] * shards), BRAIN),
+    ]
+    scratch = [
+        pltpu.VMEM((peers, unit, LANES), BRAIN),
+        pltpu.VMEM((rest, unit, LANES), BRAIN),
+        pltpu.VMEM((rest, peers, unit, LANES), BRAIN),
+        pltpu.SemaphoreType.DMA((2, rest)),
+        pltpu.SemaphoreType.DMA((2, rest * (peers - 1))),
+        pltpu.VMEM((cols, own, piece), BRAIN),
+        pltpu.VMEM((rest,) + vectors.shape, FLOAT),
+    ]
+    scratch += [
+        pltpu.SemaphoreType.DMA((2, size)) for size in (cols - 1, cols - 1, rest, len(routes))
+    ]
+    result = block_call(
+        partial(opening_kernel, len(small), routes), ident, operands, outs, scratch, 30,
+        anywhere=1,
+    )
+    values = [value[:, :, :size] for value, size in zip(result, kept)]
+    return values, result[len(small) :]
+
+
+PARTS = 3
+
+
+def routes_of(pack_width, parts, source, target, begin=0):
+    shards = lax.axis_size("col") // 2
+    piece = pack_width // PARTS
+    return [
+        (source, part * piece, piece, target, ((part - begin) * shards + shard) * piece, shard)
+        for part in parts
+        for shard in range(shards)
+    ]
+
+
+def shipped(routes, sources, targets, sems):
+    cols = lax.axis_size("col")
+    row, col = lax.axis_index("row"), lax.axis_index("col")
+    copies = []
+    for slot, (source, begin, width, target, place, shard) in enumerate(routes):
+        held = sources[source].at[:, pl.ds(begin, width)]
+        there = targets[target].at[:, pl.ds(place, width)]
+        if shard:
+            to = (row, (col + cols - 2 * shard) % cols)
+            copies.append(remote(held, there, sems, slot, to))
+        else:
+            copies.append(pltpu.make_async_copy(held, there, sems.at[0, slot]))
+    return copies
+
+
+TILE = 256
+LINES = 64
+
+
+def turn_kernel(backward, offset, plan, sources, counts, routes, *refs):
+    (x, wide, x2, w2, stream, gain, d_stream), refs = refs[:7], refs[7:]
+    extra, refs = refs[:sources], refs[sources:]
+    cargo, refs = refs[: counts[0]], refs[counts[0] :]
+    (new_out, full_out), refs = refs[:2], refs[2:]
+    grad_outs, refs = refs[: len(plan)], refs[len(plan) :]
+    cargo_outs, refs = refs[: counts[1]], refs[counts[1] :]
+    weights, sending, received, mine, weight_sems, share_sems, spread_sems, cargo_sems = refs
+    cols = lax.axis_size("col")
+    shards = cols // 2
+    own = stream.shape[0]
+    depth = x.shape[1]
+    tiles = sending.shape[0]
+    row, col = lax.axis_index("row"), lax.axis_index("col")
+    peer = (row, col + 1 - 2 * (col % 2))
+
+    barrier = pltpu.get_barrier_semaphore()
+    greeted = [peer]
+    if routes:
+        greeted += [(row, (col + 2 * other) % cols) for other in range(1, shards)]
+    for to in greeted:
+        pl.semaphore_signal(barrier, inc=1, device_id=to, device_id_type=MESH)
+
+    def weight_copy(tile):
+        lines = pl.ds(pl.multiple_of(tile * TILE, TILE), TILE)
+        return pltpu.make_async_copy(
+            wide.at[lines, pl.ds(offset, depth)], weights.at[tile], weight_sems.at[tile]
+        )
+
+    def share_copy(tile):
+        return remote(sending.at[tile], received.at[tile], share_sems, tile, peer)
+
+    def spread_copy(at):
+        lines = pl.multiple_of(at * LINES, LINES)
+        return pltpu.make_async_remote_copy(
+            src_ref=full_out.at[pl.ds(lines, LINES)],
+            dst_ref=full_out.at[pl.ds(pl.multiple_of(own + lines, LINES), LINES)],
+            send_sem=spread_sems.at[0, at],
+            recv_sem=spread_sems.at[1, at],
+            device_id=peer,
+            device_id_type=MESH,
+        )
+
+    def begin(tile, nothing):
+        weight_copy(tile).start()
+        return nothing
+
+    lax.fori_loop(0, tiles, begin, 0)
+    pl.semaphore_wait(barrier, len(greeted))
+    carried = shipped(routes, cargo, cargo_outs, cargo_sems)
+    for copy in carried:
+        copy.start()
+
+    def project(tile, nothing):
+        weight_copy(tile).wait()
+        at = pl.ds(pl.multiple_of(tile * TILE, TILE), TILE)
+        total = nt(x[...], weights[tile]) + nn(x2[...], w2[:, at])
+        sending[tile] = total[own:].astype(BRAIN)
+        mine[tile] = total[:own]
+        share_copy(tile).start()
+        return nothing
+
+    lax.fori_loop(0, tiles, project, 0)
+
+    def gradients(part):
+        for (left, right, lanes), out in part:
+            value = (x if right is None else extra[right])[:, lanes]
+            out[...] = tn(extra[left][...], value)
+
+    pairs = list(zip(plan, grad_outs))
+    gradients(pairs[: len(pairs) // 2])
+
+    def arrive(tile, nothing):
+        share_copy(tile).wait()
+        return nothing
+
+    lax.fori_loop(0, tiles, arrive, 0)
+
+    def finish(at, nothing):
+        lines = pl.ds(pl.multiple_of(at * LINES, LINES), LINES)
+        total = jnp.concatenate(
+            [mine[tile, lines] + received[tile, lines].astype(FLOAT) for tile in range(tiles)],
+            axis=1,
+        )
+        value = stream[lines]
+        if backward:
+            scale = lax.rsqrt(jnp.mean(value * value, axis=1, keepdims=True) + EPSILON)
+            gained = total * gain[...]
+            shift = jnp.mean(gained * value, axis=1, keepdims=True)
+            result = d_stream[lines] + scale * gained - value * (scale * scale * scale * shift)
+            new_out[lines] = result
+            full_out[lines] = result.astype(BRAIN)
+        else:
+            result = value + total
+            scale = lax.rsqrt(jnp.mean(result * result, axis=1, keepdims=True) + EPSILON)
+            new_out[lines] = result
+            full_out[lines] = (result * scale * gain[...]).astype(BRAIN)
+        spread_copy(at).start()
+        return nothing
+
+    lax.fori_loop(0, own // LINES, finish, 0)
+    gradients(pairs[len(pairs) // 2 :])
+
+    def leave(at, nothing):
+        spread_copy(at).wait()
+        return nothing
+
+    lax.fori_loop(0, own // LINES, leave, 0)
+    for copy in carried:
+        copy.wait()
+
+
+def turn(
+    ident, x, wide, offset, x2, w2, stream, gain, d_stream=None, extra=(), plan=(), cargo=(),
+    widths=(), routes=(),
+):
+    own, d_model = stream.shape
+    depth = x.shape[1]
+    tiles = d_model // TILE
+    whole = pl.BlockSpec(memory_space=pltpu.VMEM)
+    backward = d_stream is not None
+    operands = [x, wide, x2, w2, stream, gain, d_stream if backward else gain, *extra]
+    specs = [whole] * len(operands)
+    anywhere = pl.BlockSpec(memory_space=pl.ANY)
+    specs[1] = anywhere
+    operands += cargo
+    specs += [anywhere] * len(cargo)
+    plan = tuple(plan)
+    sizes = []
+    for left, right, lanes in plan:
+        wide_by = (x if right is None else extra[right]).shape[1]
+        sizes.append((extra[left].shape[1], len(range(wide_by)[lanes])))
+    return pl.pallas_call(
+        partial(turn_kernel, backward, offset, plan, len(extra), (len(cargo), len(widths)), tuple(routes)),
+        out_shape=[
+            jax.ShapeDtypeStruct((own, d_model), FLOAT),
+            jax.ShapeDtypeStruct((2 * own, d_model), BRAIN),
+        ]
+        + [jax.ShapeDtypeStruct(size, FLOAT) for size in sizes]
+        + [jax.ShapeDtypeStruct((cargo[0].shape[0], size), cargo[0].dtype) for size in widths],
+        in_specs=specs,
+        out_specs=[whole] * (2 + len(plan)) + [anywhere] * len(widths),
+        scratch_shapes=[
+            pltpu.VMEM((tiles, TILE, depth), BRAIN),
+            pltpu.VMEM((tiles, own, TILE), BRAIN),
+            pltpu.VMEM((tiles, own, TILE), BRAIN),
+            pltpu.VMEM((tiles, own, TILE), FLOAT),
+            pltpu.SemaphoreType.DMA((tiles,)),
+            pltpu.SemaphoreType.DMA((2, tiles)),
+            pltpu.SemaphoreType.DMA((2, own // LINES)),
+            pltpu.SemaphoreType.DMA((2, max(len(routes), 1))),
+        ],
+        cost_estimate=lasting(40),
+        compiler_params=pltpu.CompilerParams(
+            vmem_limit_bytes=VMEM_BYTES, collective_id=ident, has_side_effects=True
+        ),
+    )(*operands)
 
 
 def partner(value):
@@ -663,17 +997,7 @@
 
 
 def after(value, anchor):
-    return value if anchor is None else lax.optimization_barrier((value, anchor))[0]
-
-
-def whole_width(value):
-    peers = lax.axis_size("col")
-    parts = [value] + [
-        lax.ppermute(value, "col", [((at + turn) % peers, at) for at in range(peers)])
-        for turn in range(1, peers)
-    ]
-    stacked = jnp.roll(jnp.stack(parts), lax.axis_index("col"), axis=0)
-    return jnp.moveaxis(stacked, 0, -2).reshape(value.shape[:-1] + (-1,))
+    return lax.optimization_barrier((value, anchor))[0] if jax.tree.leaves(anchor) else value
 
 
 def to_sequence(value):
@@ -697,90 +1021,68 @@
     return scale, (stream * scale * gain[None, :]).astype(BRAIN)
 
 
-def norm_backward(stream, scale, gain, d_normed):
-    gained = d_normed * gain[None, :]
-    total = jnp.mean(gained * stream, axis=1, keepdims=True)
-    return scale * gained - stream * (scale * scale * scale * total)
-
-
 def masked(value, pick):
     return (value * pick).astype(BRAIN)
 
 
-def entry(stream, gain):
-    scale, normed = norm_forward(stream, gain)
-    return scale, both_halves(normed)
-
-
-def recur_branch(normed_full, inlet, small, ctx):
+def recur_branch(normed_full, wide, small, ctx):
     pick = ctx["pick"]
     ranks = pick.shape[1]
-    width = inlet.shape[1] // 2
+    width = wide.shape[1] // 3
     low = nt(normed_full, small["inlet_lower"])
     inner = [masked(low[:, b * ranks : (b + 1) * ranks], pick) for b in range(2)]
-    branch = nn(normed_full, inlet)
+    branch = nn(normed_full, wide[:, : 2 * width])
     lead = branch[:, :width] + nn(inner[0], small["inlet_upper"][0])
     gate = branch[:, width:] + nn(inner[1], small["inlet_upper"][1])
     return lead, gate, inner
 
 
-def recur_part(stream, lead, gate, outlet, small, ctx):
+def recur_part(
+    ident, stream, lead, gate, wide, small, gain, ctx, ready, cargo, widths, routes
+):
     pick, offset = ctx["pick"], ctx["offset"]
-    own = stream.shape[0]
-    rows = 2 * own
+    width = lead.shape[1]
     conv, decay, hidden, mixed, state_in = recur_forward(lead, gate, offset, small)
+    mixed = after(mixed, ready)
     lowrank = masked(nt(mixed, small["outlet_lower"]), pick)
-
-    def outward(part):
-        return nt(mixed[part], outlet) + nn(lowrank[part], small["outlet_upper"])
-
-    middle = stream + half_share(outward(slice(0, own)), outward(slice(own, rows)))
+    middle, normed_two_full, *parts = turn(
+        ident, mixed, wide, 2 * width, lowrank, small["outlet_upper"], stream, gain, cargo=cargo,
+        widths=widths, routes=routes,
+    )
     kept = dict(
         conv=conv, decay=decay, hidden=hidden, state_in=state_in, mixed=mixed, lowrank=lowrank,
-        middle=middle,
-    )
-    return middle, kept
-
-
-def hidden_part(middle, normed_two_full, wide, small, ctx):
-    expand, shrink = wide
+        middle=middle, normed_two_full=normed_two_full,
+    )
+    return middle, normed_two_full, kept, parts
+
+
+def hidden_part(normed_two_full, wide, small, ctx):
     pick = ctx["pick"]
     ranks = pick.shape[1]
-    own = middle.shape[0]
-    rows = 2 * own
-    spread = shrink.shape[1]
+    spread = wide.shape[1] // 3
     low_two = nt(normed_two_full, small["expand_lower"])
     inner_two = [masked(low_two[:, b * ranks : (b + 1) * ranks], pick) for b in range(2)]
-    branch_two = nn(normed_two_full, expand)
+    branch_two = nn(normed_two_full, wide[:, : 2 * spread])
     up_gate = branch_two[:, :spread] + nn(inner_two[0], small["expand_upper"][0])
     up_value = branch_two[:, spread:] + nn(inner_two[1], small["expand_upper"][1])
     product = (gelu_tanh(up_gate) * up_value).astype(BRAIN)
     lowrank_two = masked(nt(product, small["shrink_lower"]), pick)
-
-    def downward(part):
-        return nt(product[part], shrink) + nn(lowrank_two[part], small["shrink_upper"])
-
-    result = middle + half_share(downward(slice(0, own)), downward(slice(own, rows)))
-    kept = dict(
-        inner_two=inner_two,
-        up_gate=up_gate, up_value=up_value, product=product, lowrank_two=lowrank_two,
-    )
-    return result, kept
-
-
-def layer_backward(d_stream, wide, small, gains, kept, ctx):
-    inlet, outlet, expand, shrink = wide
+    return dict(
+        inner_two=inner_two, up_gate=up_gate, up_value=up_value, product=product,
+        lowrank_two=lowrank_two,
+    )
+
+
+def layer_backward(ident, d_stream, d_out, wide, small, gains, kept, ctx, first, pending):
+    recur_wide, hidden_wide = wide
     pick, offset = ctx["pick"], ctx["offset"]
     own = d_stream.shape[0]
     rows = 2 * own
-    width = outlet.shape[1]
-    spread = shrink.shape[1]
-
-    d_out = both_halves(d_stream.astype(BRAIN))
+    width = recur_wide.shape[1] // 3
+    spread = hidden_wide.shape[1] // 3
+
     d_low_two = masked(nt(d_out, small["shrink_upper"]), pick)
-    d_product = nn(d_out, shrink) + nn(d_low_two, small["shrink_lower"])
-    shrink_upper_grad = tn(kept["lowrank_two"], d_out)
-    shrink_lower_grad = tn(d_low_two, kept["product"])
+    d_product = nn(d_out, hidden_wide[:, 2 * spread :]) + nn(d_low_two, small["shrink_lower"])
     value, slope = gelu_pair(kept["up_gate"])
     d_branch_two = jnp.concatenate(
         [(slope * kept["up_value"] * d_product).astype(BRAIN), (value * d_product).astype(BRAIN)],
@@ -793,26 +1095,20 @@
         ],
         axis=1,
     )
-
-    def inward_two(part):
-        return nt(d_branch_two[part], expand) + nn(d_inner_two[part], small["expand_lower"])
-
-    d_normed_two = half_share(inward_two(slice(0, own)), inward_two(slice(own, rows)))
-    expand_lower_grad = tn(d_inner_two, kept["normed_two_full"])
-    expand_upper_grad = jnp.concatenate(
-        [
-            tn(kept["inner_two"][b], d_branch_two[:, b * spread : (b + 1) * spread])
-            for b in range(2)
-        ],
-        axis=0,
-    )
-    d_middle = d_stream + norm_backward(kept["middle"], kept["scale_two"], gains[1], d_normed_two)
-
-    d_mid = both_halves(d_middle.astype(BRAIN))
+    halves = (slice(0, spread), slice(spread, 2 * spread))
+    every = slice(None)
+    d_middle, d_mid, shrink_upper, shrink_lower, expand_lower, expand_a, expand_b = turn(
+        ident, d_branch_two, hidden_wide, 0, d_inner_two, small["expand_lower"], kept["middle"],
+        gains[1:2], d_stream,
+        [kept["lowrank_two"], d_out, d_low_two, kept["product"], d_inner_two,
+         kept["normed_two_full"], *kept["inner_two"]],
+        [(0, 1, every), (2, 3, every), (4, 5, every), (6, None, halves[0]), (7, None, halves[1])],
+    )
+    expand_upper = jnp.concatenate([expand_a, expand_b], axis=0)
+
+    d_mid, ctx["last"] = lax.optimization_barrier((d_mid, pending))
     d_low = masked(nt(d_mid, small["outlet_upper"]), pick)
-    d_mixed = nn(d_mid, outlet) + nn(d_low, small["outlet_lower"])
-    outlet_upper_grad = tn(kept["lowrank"], d_mid)
-    outlet_lower_grad = tn(d_low, kept["mixed"])
+    d_mixed = nn(d_mid, recur_wide[:, 2 * width :]) + nn(d_low, small["outlet_lower"])
     d_branch = recur_backward(d_mixed, kept, offset, small)
     d_inner = jnp.concatenate(
         [
@@ -821,42 +1117,30 @@
         ],
         axis=1,
     )
-
-    def inward(part):
-        return nt(d_branch[part], inlet) + nn(d_inner[part], small["inlet_lower"])
-
-    inlet_lower_grad = tn(d_inner, kept["normed_full"])
-    inlet_upper_grad = jnp.concatenate(
-        [tn(kept["inner"][b], d_branch[:, b * width : (b + 1) * width]) for b in range(2)], axis=0
-    )
-    shared = (inlet_lower_grad, outlet_upper_grad, expand_lower_grad, shrink_upper_grad)
-    split = (inlet_upper_grad, outlet_lower_grad, expand_upper_grad, shrink_lower_grad)
-    partial_sums = (inward(slice(0, own)), inward(slice(own, rows)))
-    return d_middle, partial_sums, shared, split
-
-
-def start_sums(shared, split):
-    return (
-        lax.psum(jnp.concatenate(shared, axis=0).astype(BRAIN), ("row", "col")),
-        [
-            lax.psum(jnp.concatenate(pair, axis=0).astype(BRAIN), "row")
-            for pair in (split[:2], split[2:])
-        ],
-    )
-
-
-def end_sums(shared, split, shards, anchor):
-    shared = after(shared, anchor).astype(FLOAT)
-    totals = []
-    for whole in split:
-        whole = after(whole, anchor)
-        piece = whole.shape[1] // shards
-        parts = [whole[:, turn * piece : (turn + 1) * piece] for turn in range(shards)]
-        total = parts[0].astype(FLOAT)
-        for turn in range(1, shards):
-            total = total + to_shard(parts[turn], turn).astype(FLOAT)
-        totals.append(total)
-    return shared, totals
+    halves = (slice(0, width), slice(width, 2 * width))
+    if first:
+        outlet_upper = tn(kept["lowrank"], d_mid)
+        outlet_lower = tn(d_low, kept["mixed"])
+        inlet_lower = tn(d_inner, kept["normed_full"])
+        inlet_a, inlet_b = (tn(kept["inner"][b], d_branch[:, halves[b]]) for b in range(2))
+        result = tuple(
+            nt(d_branch[part], recur_wide[:, : 2 * width]) + nn(d_inner[part], small["inlet_lower"])
+            for part in (slice(0, own), slice(own, rows))
+        )
+    else:
+        d_before, d_out_before, outlet_upper, outlet_lower, inlet_lower, inlet_a, inlet_b = turn(
+            ident + 1, d_branch, recur_wide, 0, d_inner, small["inlet_lower"], kept["stream"],
+            gains[0:1], d_middle,
+            [kept["lowrank"], d_mid, d_low, kept["mixed"], d_inner, kept["normed_full"],
+             *kept["inner"]],
+            [(0, 1, every), (2, 3, every), (4, 5, every), (6, None, halves[0]),
+             (7, None, halves[1])],
+        )
+        result = (d_before, d_out_before)
+    inlet_upper = jnp.concatenate([inlet_a, inlet_b], axis=0)
+    shared = (inlet_lower, outlet_upper, expand_lower, shrink_upper)
+    split = (inlet_upper, outlet_lower, expand_upper, shrink_lower)
+    return d_middle, result, shared, split
 
 
 def local(
@@ -888,10 +1172,8 @@
     )
     within = (at_home[:, None] >= starts[None, :]) & (at_home[:, None] < ends[None, :])
     pick = jnp.repeat(within.astype(FLOAT), rank, axis=1)
-    ctx = dict(pick=pick, offset=offset)
-
-    stream = to_sequence(tokens).astype(FLOAT)
-    gains = whole_width(norm_gain)
+    ctx = dict(pick=pick, offset=offset, pending={})
+
 
     def by_doc(factor, axis):
         return jnp.concatenate(
@@ -929,42 +1211,44 @@
         [conv_weight, gate_bias, conv_bias[:, None], decay_param[:, None]], axis=1
     )
 
-    def start(pair, single, anchor):
-        return all_shards(after(jnp.concatenate([pair[:, 0], pair[:, 1], single], axis=1), anchor))
-
-    def gathered(parts, anchor):
-        piece = parts[0].shape[1] // 3
-        parts = [parts[0]] + [after(part, anchor) for part in parts[1:]]
-        columns = [part[:, at * piece : (at + 1) * piece] for at in range(3) for part in parts]
-        whole = lax.all_gather(jnp.concatenate(columns, axis=1), "row", axis=0, tiled=True)
-        cut = 2 * shards * piece
-        return whole[:, :cut], whole[:, cut:]
-
-    def joined(parts, anchor):
-        return jnp.concatenate([parts[0]] + [after(part, anchor) for part in parts[1:]], axis=1)
-
-    def start_recur_small(layer, anchor):
-        return [
-            all_shards(after(value, anchor))
-            for value in (narrow_own[layer], vectors_own[layer], gate_weight[layer])
-        ]
-
-    def recur_small(layer, parts, anchor):
-        narrow, vectors, gates = (joined(part, anchor) for part in parts)
+    def rows_of(value):
+        return value.reshape(-1, value.shape[-1])
+
+    def packed(pair, single):
+        pack = jnp.concatenate([pair[:, 0], pair[:, 1], single], axis=1)
+        short = -single.shape[1] % LANES
+        if short:
+            pack = jnp.pad(pack.reshape(pack.shape[0], PARTS, -1), ((0, 0), (0, 0), (0, short)))
+            pack = pack.reshape(pack.shape[0], -1)
+        return pack
+
+    def side_packs(pack):
+        parts = all_shards(pack)
+        piece = pack.shape[1] // PARTS
+        columns = [part[:, at * piece : (at + 1) * piece] for at in range(PARTS) for part in parts]
+        return jnp.concatenate(columns, axis=1)
+
+    def gathered(packs, piece):
+        whole = lax.all_gather(packs, "row", axis=0, tiled=True)
+        if piece % LANES:
+            whole = whole.reshape(whole.shape[0], PARTS * shards, -1)[:, :, :piece]
+            whole = whole.reshape(whole.shape[0], -1)
+        return whole
+
+    def recur_small(layer, narrow, gates):
         return dict(
             inlet_lower=lows["inlet_lower"][layer],
             inlet_upper=narrow[: 2 * ranks].reshape(2, ranks, -1),
             outlet_lower=narrow[2 * ranks :],
             outlet_upper=lows["outlet_upper"][layer],
-            conv_weight=vectors[:CONV],
-            gate_bias=vectors[CONV : CONV + 2],
-            conv_bias=vectors[CONV + 2 : CONV + 3],
-            soft=jax.nn.softplus(vectors[CONV + 3 : CONV + 4]),
+            conv_weight=vectors_all[layer, :CONV],
+            gate_bias=vectors_all[layer, CONV : CONV + 2],
+            conv_bias=vectors_all[layer, CONV + 2 : CONV + 3],
+            soft=jax.nn.softplus(vectors_all[layer, CONV + 3 : CONV + 4]),
             gate_weight=gates,
         )
 
-    def hidden_small(layer, parts, anchor):
-        broad = joined(parts, anchor)
+    def hidden_small(layer, broad):
         return dict(
             expand_lower=lows["expand_lower"][layer],
             expand_upper=broad[: 2 * ranks].reshape(2, ranks, -1),
@@ -973,65 +1257,116 @@
         )
 
     outputs, saved, wides, smalls = [], [], [], []
-    recur_pack = start(inlet_weight[0], outlet_weight[0], None)
-    recur_bits = start_recur_small(0, recur_pack[-1])
-    hidden_pack = start(expand_weight[0], shrink_weight[0], recur_pack[-1])
-    wide_one = gathered(recur_pack, None)
+    recur_packs = [packed(inlet_weight[at], outlet_weight[at]) for at in range(LAYERS)]
+    hidden_packs = [packed(expand_weight[at], shrink_weight[at]) for at in range(LAYERS)]
+    def side_by_side(value):
+        return jnp.concatenate([value[at] for at in range(shards)], axis=1)
+
+    def heads_in_turn(value):
+        return jnp.concatenate(
+            [value[at].reshape((2, -1) + gate_weight.shape[3:]) for at in range(shards)], axis=1
+        )
+
+    (narrow, gates, broad), (stream, gains, vectors_all, recur_side) = open_up(
+        20, [narrow_own[0], rows_of(gate_weight[0]), broad_own[0]], tokens, rows_of(norm_gain),
+        rows_of(vectors_own), recur_packs[0],
+    )
+    narrow, gates, broad = side_by_side(narrow), heads_in_turn(gates), side_by_side(broad)
+    gains = jnp.moveaxis(gains, 0, 1).reshape(LAYERS, 2, d_model)
+    vectors_all = side_by_side(vectors_all).reshape(LAYERS, -1, shards * part_width)
+    wide_one = gathered(recur_side, part_width)
+    hidden_side = side_packs(after(hidden_packs[0], stream))
+    stream = stream.astype(FLOAT)
+    _, normed = norm_forward(stream, gains[0][0])
+    normed_full = both_halves(normed)
+    normed_full, hidden_side = lax.optimization_barrier((normed_full, hidden_side))
     for layer in range(LAYERS):
         more_layers = layer + 1 < LAYERS
-        scale_one, normed_full = entry(stream, gains[layer][0])
-        small_one = recur_small(layer, recur_bits, normed_full)
-        lead, gate, inner = recur_branch(normed_full, wide_one[0], small_one, ctx)
+        kept = dict(stream=stream, normed_full=normed_full)
+        small_one = recur_small(layer, narrow, gates)
+        lead, gate, inner = recur_branch(normed_full, wide_one, small_one, ctx)
+        ready, cargo, widths, routes = [], [], [], []
         if layer == 0:
-            wide_two = gathered(hidden_pack, lead)
-        hidden_bits = all_shards(after(broad_own[layer], lead))
+            wide_two = gathered(after(hidden_side, lead), part_spread)
         if more_layers:
-            recur_pack = start(inlet_weight[layer + 1], outlet_weight[layer + 1], lead)
-        middle, kept = recur_part(stream, lead, gate, wide_one[1], small_one, ctx)
-        kept.update(
-            stream=stream, scale_one=scale_one, normed_full=normed_full, inner=inner, gate=gate
+            narrow_parts, gate_parts = (
+                all_shards(after(value[layer + 1], lead)) for value in (narrow_own, gate_weight)
+            )
+            ready = [narrow_parts[1:], gate_parts[1:]]
+            cargo = [recur_packs[layer + 1], hidden_packs[layer + 1]]
+            spans = [pack.shape[1] for pack in cargo]
+            widths = [spans[0] * shards, spans[1] // PARTS * shards]
+            routes = routes_of(spans[0], range(PARTS), 0, 0) + routes_of(spans[1], [0], 1, 1)
+        elif layer:
+            ending = to_sequence(after(cotangent, lead))
+            ready = [ending]
+            cargo = [broad_own[layer]]
+            spread_piece = cargo[0].shape[1]
+            if spread_piece % LANES:
+                cargo = [jnp.pad(cargo[0], ((0, 0), (0, -spread_piece % LANES)))]
+            span = cargo[0].shape[1]
+            widths = [span * shards]
+            routes = [(0, 0, span, 0, shard * span, shard) for shard in range(shards)]
+        middle, normed_two_full, more, sides = recur_part(
+            3 + 2 * layer, stream, lead, gate, wide_one, small_one, gains[layer][1:2], ctx, ready,
+            cargo, widths, routes,
         )
+        if layer and not more_layers:
+            broad = sides[0].reshape(sides[0].shape[0], shards, -1)[:, :, :spread_piece]
+            broad = broad.reshape(broad.shape[0], -1)
+        kept.update(inner=inner, gate=gate, **more)
         if more_layers:
-            wide_next = gathered(recur_pack, middle)
-            recur_bits = start_recur_small(layer + 1, middle)
-            hidden_pack = start(expand_weight[layer + 1], shrink_weight[layer + 1], middle)
-        scale_two, normed_two_full = entry(middle, gains[layer][1])
-        small_two = hidden_small(layer, hidden_bits, normed_two_full)
-        stream, more = hidden_part(middle, normed_two_full, wide_two, small_two, ctx)
-        more.update(scale_two=scale_two, normed_two_full=normed_two_full)
+            wide_next = gathered(sides[0], part_width)
+        small_two = hidden_small(layer, broad)
+        more = hidden_part(normed_two_full, wide_two, small_two, ctx)
+        kept.update(more)
+        wides.append((wide_one, wide_two))
+        smalls.append({**small_one, **small_two})
+        saved.append(kept)
+        product, lowrank, upper = more["product"], more["lowrank_two"], small_two["shrink_upper"]
+        spread = product.shape[1]
         if more_layers:
-            wide_two_next = gathered(hidden_pack, more["product"])
+            pack = hidden_packs[layer + 1]
+            span, early = pack.shape[1], sides[1].shape[1]
+            routes = routes_of(span, range(1, PARTS), 0, 0) + [(1, 0, early, 0, 0, 0)]
+            stream, normed_full, hidden_side = turn(
+                4 + 2 * layer, product, wide_two, 2 * spread, lowrank, upper, middle,
+                gains[layer + 1][0:1], cargo=[pack, sides[1]], widths=[span * shards],
+                routes=routes,
+            )
+            wide_two_next = gathered(hidden_side, part_spread)
+            narrow, gates = (jnp.concatenate(part, axis=1) for part in (narrow_parts, gate_parts))
+            wide_one, wide_two = wide_next, wide_two_next
+        else:
+            shrink = wide_two[:, 2 * spread :]
+            parts = [
+                nt(product[part], shrink) + nn(lowrank[part], upper)
+                for part in (slice(0, own), slice(own, 2 * own))
+            ]
+            stream = middle + half_share(*parts)
+            last_stream = stream
         outputs.append(from_sequence(stream.astype(BRAIN)))
-        saved.append({**kept, **more})
-        wides.append(wide_one + wide_two)
-        smalls.append({**small_one, **small_two})
-        if more_layers:
-            wide_one, wide_two = wide_next, wide_two_next
-    d_stream = to_sequence(cotangent).astype(FLOAT)
-    shared, narrow, broad = [None] * LAYERS, [None] * LAYERS, [None] * LAYERS
-    started = {}
+    ctx["pending"] = {LAYERS - 1: last_stream, LAYERS - 2: outputs.pop()}
+    d_stream, d_out = ending.astype(FLOAT), both_halves(after(ending, normed_two_full))
+    shared_parts, split_parts = [], []
     for layer in reversed(range(LAYERS)):
         kept = saved[layer]
-        d_middle, parts, shared_parts, split_parts = layer_backward(
-            d_stream, wides[layer], smalls[layer], gains[layer], kept, ctx
+        d_middle, result, shared_more, split_more = layer_backward(
+            3 + 2 * LAYERS + 2 * layer, d_stream, d_out, wides[layer], smalls[layer], gains[layer],
+            kept, ctx, layer == 0, ctx["pending"].get(layer),
         )
+        shared_parts = [*shared_more, *shared_parts]
+        split_parts = [*split_more, *split_parts]
         if layer:
-            d_normed = half_share(*parts)
-            d_stream = d_middle + norm_backward(
-                kept["stream"], kept["scale_one"], gains[layer][0], d_normed
-            )
-            started[layer] = start_sums(shared_parts, split_parts)
-        else:
-            tokens_grad, shared_parts, split_parts = close(
-                parts[0], parts[1].astype(BRAIN), kept["stream"], d_middle, gains[layer][:1],
-                shared_parts, split_parts,
-            )
-            shared[layer] = jnp.concatenate(shared_parts, axis=0)
-            narrow[layer] = jnp.concatenate(split_parts[:2], axis=0)
-            broad[layer] = jnp.concatenate(split_parts[2:], axis=0)
-    for layer, (whole, pairs) in started.items():
-        shared[layer], (narrow[layer], broad[layer]) = end_sums(whole, pairs, shards, tokens_grad)
-    shared, narrow, broad = jnp.stack(shared), jnp.stack(narrow), jnp.stack(broad)
+            d_stream, d_out = result
+    tokens_grad, shared_parts, split_parts = close(
+        result[0], result[1].astype(BRAIN), kept["stream"], d_middle, gains[0][:1], shared_parts,
+        split_parts,
+    )
+    inlet_low, outlet_up, expand_low, shrink_up = (
+        jnp.stack(shared_parts[at::4]) for at in range(4)
+    )
+    inlet_up, outlet_low, expand_up, shrink_low = (jnp.stack(split_parts[at::4]) for at in range(4))
     spread_out = (adapter_ids[None, :] == jnp.arange(adapters, dtype=jnp.int32)[:, None])
 
     def by_adapter(grad, count):
@@ -1050,16 +1385,16 @@
         return jnp.moveaxis(grad, -1, 1)
 
     return (
-        jnp.stack(outputs, axis=0),
+        jnp.stack([*outputs, ctx["last"]], axis=0),
         tokens_grad,
-        lower_out(shared[:, : 2 * ranks], 2),
-        by_adapter(narrow[:, : 2 * ranks], 2),
-        lower_out(narrow[:, 2 * ranks :], 1),
-        by_adapter(shared[:, 2 * ranks : 3 * ranks], 1)[:, 0],
-        lower_out(shared[:, 3 * ranks : 5 * ranks], 2),
-        by_adapter(broad[:, : 2 * ranks], 2),
-        lower_out(broad[:, 2 * ranks :], 1),
-        by_adapter(shared[:, 5 * ranks :], 1)[:, 0],
+        lower_out(inlet_low, 2),
+        by_adapter(inlet_up, 2),
+        lower_out(outlet_low, 1),
+        by_adapter(outlet_up, 1)[:, 0],
+        lower_out(expand_low, 2),
+        by_adapter(expand_up, 2),
+        lower_out(shrink_low, 1),
+        by_adapter(shrink_up, 1)[:, 0],
     )
 
 

time: 1040 us -> 972 us (0.935)
  Pallas kernels: 205 us -> 603 us
  waiting for transfers between devices: 368 us -> 62.7 us
  matrix products: 253 us -> 132 us
  starting transfers between devices: 62.7 us -> 27.4 us
    pallas_call x0 -> x6, Pallas kernels: none -> 323 us  [turn(): pl.pallas_call(partial(turn_kernel, backward, offset, plan, len(extra), (...]
    ppermute x15 -> x3, waiting for transfers between devices: 211 us -> 25.4 us  [partner(): return lax.ppermute(value, 'col', [(at, at ^ 1) for at in range(peers)])]
    ppermute x12 -> x3, waiting for transfers between devices: 129 us -> 37.2 us  [from_shard(): lax.ppermute(value, 'col', [((at + 2 * turn) % peers, at) for at in range...]
    dot_general x36 -> x24, matrix products: 112 us -> 36.5 us  [nt(): lax.dot_general(left, right, (((1,), (1,)), ((), ())), preferred_element_...]
    pallas_call x5 -> x6, Pallas kernels: 205 us -> 280 us  [block_call(): pl.pallas_call(kernel, out_shape=[jax.ShapeDtypeStruct(*out) for out in o...]
    dot_general x36 -> x24, matrix products: 116 us -> 93.4 us  [nn(): lax.dot_general(left, right, (((1,), (0,)), ((), ())), preferred_element_...]
    dot_general x20 -> x5, matrix products: 24.7 us -> 2.56 us  [tn(): lax.dot_general(left, right, (((0,), (0,)), ((), ())), preferred_element_...]
    ppermute x5 -> x0, waiting for transfers between devices: 18.1 us -> none  [the longest x2 18.1 us: to_shard(): lax.ppermute(value, 'col', [(at, (at + 2 * turn) % peers) for at in range...]
  transfers between devices with their start and end apart: 42 -> 13, of which waited for: 21 -> 3; matrix products, arithmetic and copies ran while one was open for 28% -> 11% of each run, Pallas kernels for 20% -> 49%
where the time goes in v4:
time: 972 us; the launch traced here: 964 us
  Pallas kernels  603 us (62%)
  matrix products  132 us (14%)
  local copies, waits for them, and re-layouts  76 us (8%)
  waiting for transfers between devices  62.7 us (6%)
  other arithmetic  37.1 us (4%)
  starting transfers between devices  27.4 us (3%)
  between operations  26 us (3%)
    pallas_call x6, Pallas kernels, turn(): pl.pallas_call(partial(turn_kernel, backward, offset, plan, len(extra), (...  323 us
    pallas_call x6, Pallas kernels, block_call(): pl.pallas_call(kernel, out_shape=[jax.ShapeDtypeStruct(*out) for out in o...  280 us
    dot_general x24, matrix products, nn(): lax.dot_general(left, right, (((1,), (0,)), ((), ())), preferred_element_...  93.4 us
    unnamed x375, local copies, waits for them, and re-layouts  44.5 us
    ppermute x3, waiting for transfers between devices, from_shard(): lax.ppermute(value, 'col', [((at + 2 * turn) % peers, at) for at in range...  37.2 us
    dot_general x24, matrix products, nt(): lax.dot_general(left, right, (((1,), (1,)), ((), ())), preferred_element_...  36.5 us
    ppermute x3, waiting for transfers between devices, partner(): return lax.ppermute(value, 'col', [(at, at ^ 1) for at in range(peers)])  25.4 us
  transfers between devices with their start and end apart: 13, of which 3 were waited for; matrix products, arithmetic and copies ran while one was open for 11% of the time, Pallas kernels for 49%

profile of v4, /device:TPU:0, one launch (start us, length us, event | category | flops | bytes accessed | tf_op | source)
XLA Modules:
  0.0 964.2 jit_solution(11233803793487196298)
XLA Ops:
  26.9 54.7 %shard_map.285 = (bf16[2,192,512]{2,1,0:T(8,128)(2,1)S(1)}, bf16[2,1024,256]{2,1,0:T(8,128)(2,1)S(1)}, bf16[2,192,1152]{2,1,0:T(8,128)(2,1)S(1)}, bf16[256,1536]...) custom-call(bf16[192,512]{1,0:T(8,128)(2,1)S(1)} %get-tuple-element.264.refs_, ...), custom_call_target="tpu_custom_call" | custom-call | flops 32999999488 | bytes 90000000 | tf_op jit(solution)/shard_map/pallas_call | solution.py:351
  102.8 11.9 %collective-permute-done = bf16[256,1536]{1,0:T(8,128)(2,1)} collective-permute-done((bf16[256,1536]{1,0:T(8,128)(2,1)S(1)}, bf16[256,1536]{1,0:T(8,128)(2,1)}, u32[]{:S(2)}, u32[]{:S(2)}) %collective-permute-start) | collective-permute-done | bytes 786464 | tf_op jit(solution)/shard_map/ppermute | solution.py:982
  116.2 37.2 %collective-permute-done.1 = bf16[192,3456]{1,0:T(8,128)(2,1)} collective-permute-done((bf16[192,3456]{1,0:T(8,128)(2,1)}, bf16[192,3456]{1,0:T(8,128)(2,1)}, u32[]{:S(2)}, u32[]{:S(2)}) %collective-permute-start.1) | collective-permute-done | bytes 1327136 | tf_op jit(solution)/shard_map/ppermute | solution.py:987
  164.7 5.6 fusion.24
  186.6 44.9 %shard_map.286 = (bf16[512,1024]{1,0:T(8,128)(2,1)S(1)}, f32[8,512,128]{2,1,0:T(8,128)S(1)}, f32[8,512,128]{2,1,0:T(8,128)}, bf16[512,1024]{1,0:T(8,128)(2,1)S(1)}, f32[8,128]{1,0:T(8,128)S(1)}) custom-call(f32[512,1024]{1,0:T(8,128)} %slice_add_fusion.3.lead, f32[512,1024]{1,0:T(8,128)} %slice_add_fusion.2.gate, s32[512,1]{1,0:T(8,128)S(1)} %add_subtract_fusion.offset, ...), custom_call_target="tpu_custom_call" | custom-call | flops 29699999744 | bytes 81000000 | tf_op jit(solution)/shard_map/pallas_call | solution.py:351
  233.4 69.3 %shard_map.287 = (f32[256,1536]{1,0:T(8,128)}, bf16[512,1536]{1,0:T(8,128)(2,1)}, bf16[192,3072]{1,0:T(8,128)(2,1)}, bf16[192,2304]{1,0:T(8,128)(2,1)S(1)}) custom-call(bf16[512,1024]{1,0:T(8,128)(2,1)S(1)} %get-tuple-element.99.refs_0_, bf16[1536,3072]{1,0:T(8,128)(2,1)} %all-gather.5.cloned.1.call-done.refs_1_, bf16[512,64]{1,0:T(8,128)(2,1)S(1)} %fusion.47.refs_2_, ...), custom_call_target="tpu_custom_call" | custom-call | flops 44000002048 | bytes 120000000 | tf_op jit(solution)/shard_map/pallas_call | solution.py:953
  308.3 11.5 %fusion.2 = f32[512,4608]{1,0:T(8,128)S(1)} fusion(bf16[512,1536]{1,0:T(8,128)(2,1)} %get-tuple-element.100.refs_12_, bf16[1536,6912]{1,0:T(8,128)(2,1)} %all-gather.7.cloned.1.call-done.refs_1_), kind=kOutput, calls=%fused_computation.2 | convolution fusion | flops 7247757312 | bytes 25165824 | tf_op jit(solution)/shard_map/dot_general | solution.py:27
  327.8 59.0 %shard_map.288 = (f32[256,1536]{1,0:T(8,128)S(1)}, bf16[512,1536]{1,0:T(8,128)(2,1)S(1)}, bf16[192,6912]{1,0:T(8,128)(2,1)}) custom-call(bf16[512,2304]{1,0:T(8,128)(2,1)} %copy-done.95, bf16[1536,6912]{1,0:T(8,128)(2,1)} %all-gather.7.cloned.1.call-done.refs_1_, bf16[512,64]{1,0:T(8,128)(2,1)S(1)} %copy.174.refs_2_.refs_7_, bf16[64,1536]{1,0:T(8,128)(2,1)S(1)} %bitcast.360, ...), custom_call_target="tpu_custom_call" | custom-call | flops 44000002048 | bytes 120000000 | tf_op jit(solution)/shard_map/pallas_call | solution.py:953
  394.2 6.3 fusion.6
  411.2 34.4 %shard_map.289 = (bf16[512,1024]{1,0:T(8,128)(2,1)S(1)}, f32[8,512,128]{2,1,0:T(8,128)S(1)}, f32[8,512,128]{2,1,0:T(8,128)}, bf16[512,1024]{1,0:T(8,128)(2,1)S(1)}, f32[8,128]{1,0:T(8,128)S(1)}) custom-call(f32[512,1024]{1,0:T(8,128)} %slice_add_fusion.1.lead, f32[512,1024]{1,0:T(8,128)} %slice_add_fusion.gate, s32[512,1]{1,0:T(8,128)S(1)} %copy-done.38, ...), custom_call_target="tpu_custom_call" | custom-call | flops 29699999744 | bytes 81000000 | tf_op jit(solution)/shard_map/pallas_call | solution.py:351
  455.7 50.2 %shard_map.290 = (f32[256,1536]{1,0:T(8,128)S(1)}, bf16[512,1536]{1,0:T(8,128)(2,1)S(1)}, bf16[192,2304]{1,0:T(8,128)(2,1)S(1)}) custom-call(bf16[512,1024]{1,0:T(8,128)(2,1)S(1)} %get-tuple-element.111.refs_0_.refs_10_, bf16[1536,3072]{1,0:T(8,128)(2,1)} %all-gather.9.cloned.1.call-done.refs_1_, bf16[512,64]{1,0:T(8,128)(2,1)S(1)} %copy-done.45, ...), custom_call_target="tpu_custom_call" | custom-call | flops 44000002048 | bytes 120000000 | tf_op jit(solution)/shard_map/pallas_call | solution.py:953
  511.7 13.5 %collective-permute-done.4 = bf16[256,1536]{1,0:T(8,128)(2,1)S(1)} collective-permute-done((bf16[256,1536]{1,0:T(8,128)(2,1)S(1)}, bf16[256,1536]{1,0:T(8,128)(2,1)S(1)}, u32[]{:S(2)}, u32[]{:S(2)}) %collective-permute-start.4) | collective-permute-done | bytes 786464 | tf_op jit(solution)/shard_map/ppermute | solution.py:982
  529.3 10.2 %fusion = f32[512,4608]{1,0:T(8,128)S(1)} fusion(bf16[512,1536]{1,0:T(8,128)(2,1)S(1)} %copy-done.8, bf16[1536,6912]{1,0:T(8,128)(2,1)} %all-gather.11.cloned.1.call-done.refs_1_), kind=kOutput, calls=%fused_computation | convolution fusion | flops 7247757312 | bytes 25165824 | tf_op jit(solution)/shard_map/dot_general | solution.py:27
  543.3 12.4 %fusion.37 = (bf16[512,2304]{1,0:T(8,128)(2,1)}, bf16[512,2304]{1,0:T(8,128)(2,1)S(1)}, bf16[512,2304]{1,0:T(8,128)(2,1)S(1)}) fusion(f32[512,2304]{1,0:T(8,128)S(1)} %convolution_add_fusion, f32[512,2304]{1,0:T(8,128)} %convolution_add_fusion.1, f32[512,2304]{1,0:T(8,128)S(1)} %bitcast.405, bf16[512,1536]{1,0:T(8,128)(2,1)S(1)} %copy-done.114, ...), kind=kOutput, calls=%fused_computation.39 | convolution fusion | flops 3661627392 | bytes 29884416 | tf_op jit(solution)/shard_map/dot_general | solution.py:27
  570.1 52.1 %shard_map.291 = (f32[256,1536]{1,0:T(8,128)S(1)}, bf16[512,1536]{1,0:T(8,128)(2,1)}, f32[64,1536]{1,0:T(8,128)S(1)}, f32[64,2304]{1,0:T(8,128)S(1)}, f32[128,15...) custom-call(bf16[512,4608]{1,0:T(8,128)(2,1)} %pad_maximum_fusion.refs_0_, ...), custom_call_target="tpu_custom_call" | custom-call | flops 44000002048 | bytes 120000000 | tf_op jit(solution)/shard_map/pallas_call | solution.py:953
  625.5 5.1 fusion.10
  639.0 30.0 %shard_map.292.refs_0_ = bf16[512,2048]{1,0:T(8,128)(2,1)S(1)} custom-call(f32[512,1024]{1,0:T(8,128)} %convolution_add_fusion.9.grad, f32[512,1024]{1,0:T(8,128)} %slice_add_fusion.gate, f32[8,512,128]{2,1,0:T(8,128)} %get-tuple-element.119.hidden, f32[8,512,128]{2,1,0:T(8,128)} %copy-done.61, f32[8,128]{1,0:T(8,128)S(1)} %copy-done.87, ...), custom_call_target="tpu_custom_call" | custom-call | flops 32999999488 | bytes 90000000 | tf_op jit(solution)/shard_map/pallas_call | solution.py:351
  671.2 42.6 %shard_map.293 = (f32[256,1536]{1,0:T(8,128)S(1)}, bf16[512,1536]{1,0:T(8,128)(2,1)}, f32[64,1536]{1,0:T(8,128)S(1)}, f32[64,1024]{1,0:T(8,128)S(1)}, f32[128,15...) custom-call(bf16[512,2048]{1,0:T(8,128)(2,1)} %copy-done.59, ...), custom_call_target="tpu_custom_call" | custom-call | flops 44000002048 | bytes 120000000 | tf_op jit(solution)/shard_map/pallas_call | solution.py:953
  718.3 10.1 %multiply_convert_fusion.1 = (bf16[512,2304]{1,0:T(8,128)(2,1)S(1)}, bf16[512,2304]{1,0:T(8,128)(2,1)S(1)}) fusion(f32[512,2304]{1,0:T(8,128)} %get-tuple-element.307, f32[512,2304]{1,0:T(8,128)} %copy-done.92, f32[512,2304]{1,0:T(8,128)S(1)} %fusion.185, bf16[512,1536]{1,0:T(8,128)(2,1)S(1)} %copy-done.127, ...), kind=kOutput, calls=%fused_computation.43 | convolution fusion | flops 3651010560 | bytes 27525120 | tf_op jit(solution)/shard_map/dot_general | solution.py:27
  734.0 5.8 all-to-all-start.2
  740.0 49.6 %shard_map.294 = (f32[256,1536]{1,0:T(8,128)S(1)}, bf16[512,1536]{1,0:T(8,128)(2,1)}, f32[64,1536]{1,0:T(8,128)S(1)}, f32[64,2304]{1,0:T(8,128)S(1)}, f32[128,15...) custom-call(bf16[512,4608]{1,0:T(8,128)(2,1)} %pad_maximum_fusion.1.refs_0_, ...), custom_call_target="tpu_custom_call" | custom-call | flops 44000002048 | bytes 120000000 | tf_op jit(solution)/shard_map/pallas_call | solution.py:953
  792.7 5.5 all-to-all-start
  806.4 31.4 %shard_map.295 = bf16[512,2048]{1,0:T(8,128)(2,1)S(1)} custom-call(f32[512,1024]{1,0:T(8,128)} %convolution_add_fusion.8.grad, f32[512,1024]{1,0:T(8,128)} %slice_add_fusion.2.gate, f32[8,512,128]{2,1,0:T(8,128)} %get-tuple-element.129.hidden, f32[8,512,128]{2,1,0:T(8,128)} %copy-done.60, f32[8,128]{1,0:T(8,128)S(1)} %copy-done.85, ...), custom_call_target="tpu_custom_call" | custom-call | flops 32999999488 | bytes 90000000 | tf_op jit(solution)/shard_map/pallas_call | solution.py:351
  852.0 84.4 %shard_map.296 = (f32[1024,384]{1,0:T(8,128)}, f32[128,1536]{1,0:T(8,128)}, f32[64,1536]{1,0:T(8,128)S(1)}, f32[128,1536]{1,0:T(8,128)}, f32[64,1536]{1,0:T(8,12...) custom-call(f32[256,1536]{1,0:T(8,128)} %convolution_add_fusion.7.re, ...), custom_call_target="tpu_custom_call" | custom-call | flops 88000004096 | bytes 240000000 | tf_op jit(solution)/shard_map/pallas_call | solution.py:351
  (563 shorter events, 200.5 us)
Async XLA Ops:
  7.2 157.5 %all-gather.5.cloned.1.call-start = ((), (), s32[]{:S(2)}) async-start(), calls=%async_computation.3 | async-start | bytes 10616832 | tf_op jit(solution)/shard_map/all_gather | solution.py:1232
  82.6 225.7 %all-gather.7.cloned.1.call-start = ((), (), s32[]{:S(2)}) async-start(), calls=%async_computation.4 | async-start | bytes 23887872 | tf_op jit(solution)/shard_map/all_gather | solution.py:1232
  82.7 243.9 %copy-start.51 = (f32[1,4,384]{2,0,1:T(1,128)}, f32[1,4,384]{2,0,1:T(1,128)S(1)}, u32[]{:S(2)}) copy-start(f32[1,4,384]{2,0,1:T(1,128)S(1)} %get-tuple-element.292) | copy-start | bytes 18436
  83.2 31.5 %collective-permute-start = (bf16[256,1536]{1,0:T(8,128)(2,1)S(1)}, bf16[256,1536]{1,0:T(8,128)(2,1)}, u32[]{:S(2)}, u32[]{:S(2)}) collective-permute-start(bf16[256,1536]{1,0:T(8,128)(2,1)S(1)} %multiply_convert_fusion.4), channel_id=1, source_target_pairs={{0,1},{1,0},{2,3},{3,2},{4,5},{5,4},{6,7},{7,6},{8,9},{9,8},{10,11... | collective-permute-start | bytes 2359304 | tf_op jit(solution)/shard_map/ppermute | solution.py:982
  93.3 60.1 %collective-permute-start.1 = (bf16[192,3456]{1,0:T(8,128)(2,1)}, bf16[192,3456]{1,0:T(8,128)(2,1)}, u32[]{:S(2)}, u32[]{:S(2)}) collective-permute-start(bf16[192,3456]{1,0:T(8,128)(2,1)} %pad_maximum_fusion.4), channel_id=1, source_target_pairs={{2,0},{3,1},{0,2},{1,3},{6,4},{7,5},{4,6},{5,7},{10,8},{11,9},{8,1... | collective-permute-start | bytes 3981320 | tf_op jit(solution)/shard_map/ppermute | solution.py:987
  174.1 220.0 %all-gather.9.cloned.1.call-start = ((), (), s32[]{:S(2)}) async-start(), calls=%async_computation.5 | async-start | bytes 10616832 | tf_op jit(solution)/shard_map/all_gather | solution.py:1232
  176.0 148.2 %copy-start.96 = (f32[512,4,16]{0,2,1:T(8,128)}, f32[512,4,16]{0,2,1:T(8,128)S(1)}, u32[]{:S(2)}) copy-start(f32[512,4,16]{0,2,1:T(8,128)S(1)} %broadcast_in_dim.528) | copy-start | bytes 393220
  176.2 349.1 %copy-start.93 = (f32[512,64]{1,0:T(8,128)}, f32[512,64]{1,0:T(8,128)S(1)}, u32[]{:S(2)}) copy-start(f32[512,64]{1,0:T(8,128)S(1)} %copy.167) | copy-start | bytes 393220
  181.8 51.1 %collective-permute-start.2 = (bf16[192,512]{1,0:T(8,128)(2,1)S(1)}, bf16[192,512]{1,0:T(8,128)(2,1)S(1)}, u32[]{:S(2)}, u32[]{:S(2)}) collective-permute-start(bf16[192,512]{1,0:T(8,128)(2,1)S(1)} %copy-done.133), channel_id=1, source_target_pairs={{2,0},{3,1},{0,2},{1,3},{6,4},{7,5},{4,6},{5,7},{10,8},{11,9},{8,1... | collective-permute-start | bytes 589832 | tf_op jit(solution)/shard_map/ppermute | solution.py:987
  183.6 49.3 %collective-permute-start.3 = (bf16[2,2,256,256]{3,2,1,0:T(8,128)(2,1)S(1)}, bf16[2,2,256,256]{3,2,1,0:T(8,128)(2,1)S(1)}, u32[]{:S(2)}, u32[]{:S(2)}) collective-permute-start(bf16[2,2,256,256]{3,2,1,0:T(8,128)(2,1)S(1)} %copy-done.121), channel_id=1, source_target_pairs={{2,0},{3,1},{0,2},{1,3},{6,4},{7,5},{4,6},{5,7},{10,8},{11,9},{8,1... | collective-permute-start | bytes 1572872 | tf_op jit(solution)/shard_map/ppermute | solution.py:987
  232.9 69.8 %copy-start.65 = (bf16[512,1024]{1,0:T(8,128)(2,1)}, bf16[512,1024]{1,0:T(8,128)(2,1)S(1)}, u32[]{:S(2)}) copy-start(bf16[512,1024]{1,0:T(8,128)(2,1)S(1)} %get-tuple-element.132.conv) | copy-start | bytes 3145732
  232.9 69.8 %copy-start.84 = (f32[8,128]{1,0:T(8,128)}, f32[8,128]{1,0:T(8,128)S(1)}, u32[]{:S(2)}) copy-start(f32[8,128]{1,0:T(8,128)S(1)} %get-tuple-element.131.carry) | copy-start | bytes 12292
  232.9 69.8 %copy-start.158 = (bf16[192,512]{1,0:T(8,128)(2,1)}, bf16[192,512]{1,0:T(8,128)(2,1)S(1)}, u32[]{:S(2)}) copy-start(bf16[192,512]{1,0:T(8,128)(2,1)S(1)} %collective-permute-done.2) | copy-start | bytes 589828
  233.3 70.6 %copy-start.148 = (bf16[2,1,16,1536]{3,2,1,0:T(8,128)(2,1)S(1)}, bf16[2,1,16,1536]{3,2,1,0:T(8,128)(2,1)}, u32[]{:S(2)}) copy-start(bf16[2,1,16,1536]{3,2,1,0:T(8,128)(2,1)} %get-tuple-element.224) | copy-start | bytes 294916
  233.4 70.6 %copy-start.149 = (bf16[2,1,16,1536]{3,2,1,0:T(8,128)(2,1)S(1)}, bf16[2,1,16,1536]{3,2,1,0:T(8,128)(2,1)}, u32[]{:S(2)}) copy-start(bf16[2,1,16,1536]{3,2,1,0:T(8,128)(2,1)} %get-tuple-element.225) | copy-start | bytes 294916
  233.4 70.6 %copy-start.150 = (bf16[2,1,16,1536]{3,2,1,0:T(8,128)(2,1)S(1)}, bf16[2,1,16,1536]{3,2,1,0:T(8,128)(2,1)}, u32[]{:S(2)}) copy-start(bf16[2,1,16,1536]{3,2,1,0:T(8,128)(2,1)} %get-tuple-element.226) | copy-start | bytes 294916
  233.4 70.6 %copy-start.139 = (bf16[2,2,1,16,1536]{4,3,2,1,0:T(8,128)(2,1)S(1)}, bf16[2,2,1,16,1536]{4,3,2,1,0:T(8,128)(2,1)}, u32[]{:S(2)}) copy-start(bf16[2,2,1,16,1536]{4,3,2,1,0:T(8,128)(2,1)} %get-tuple-element.181) | copy-start | bytes 589828
  233.4 70.6 %copy-start.140 = (bf16[2,2,1,16,1536]{4,3,2,1,0:T(8,128)(2,1)S(1)}, bf16[2,2,1,16,1536]{4,3,2,1,0:T(8,128)(2,1)}, u32[]{:S(2)}) copy-start(bf16[2,2,1,16,1536]{4,3,2,1,0:T(8,128)(2,1)} %get-tuple-element.182) | copy-start | bytes 589828
  303.7 225.6 %all-gather.11.cloned.1.call-start = ((), (), s32[]{:S(2)}) async-start(), calls=%async_computation.6 | async-start | bytes 23887872 | tf_op jit(solution)/shard_map/all_gather | solution.py:1232
  403.3 45.2 %all-to-all-start.1 = ((bf16[4,256,384]{2,1,0:T(8,128)(2,1)}), bf16[4,256,384]{2,1,0:T(8,128)(2,1)S(1)}, u32[]{:S(2)}, u32[]{:S(2)}) async-start(bf16[4,256,384]{2,1,0:T(8,128)(2,1)} %bitcast.79), calls=%async_computation.1 | async-start | bytes 1572864 | tf_op jit(solution)/shard_map/all_to_all | solution.py:1004
  505.9 19.3 %collective-permute-start.4 = (bf16[256,1536]{1,0:T(8,128)(2,1)S(1)}, bf16[256,1536]{1,0:T(8,128)(2,1)S(1)}, u32[]{:S(2)}, u32[]{:S(2)}) collective-permute-start(bf16[256,1536]{1,0:T(8,128)(2,1)S(1)} %bitcast.398), channel_id=1, source_target_pairs={{0,1},{1,0},{2,3},{3,2},{4,5},{5,4},{6,7},{7,6},{8,9},{9,8},{10,11... | collective-permute-start | bytes 2359304 | tf_op jit(solution)/shard_map/ppermute | solution.py:982
  568.2 62.6 %collective-permute-start.5 = (bf16[256,1536]{1,0:T(8,128)(2,1)S(1)}, bf16[256,1536]{1,0:T(8,128)(2,1)S(1)}, u32[]{:S(2)}, u32[]{:S(2)}) collective-permute-start(bf16[256,1536]{1,0:T(8,128)(2,1)S(1)} %fusion.42), channel_id=1, source_target_pairs={{0,1},{1,0},{2,3},{3,2},{4,5},{5,4},{6,7},{7,6},{8,9},{9,8},{10,11... | collective-permute-start | bytes 2359304 | tf_op jit(solution)/shard_map/ppermute | solution.py:982
  734.0 58.7 %all-to-all-start.2 = ((bf16[256,4,384]{2,0,1:T(8,128)(2,1)}), bf16[256,4,384]{2,0,1:T(8,128)(2,1)}, u32[]{:S(2)}, u32[]{:S(2)}) async-start(bf16[256,4,384]{2,0,1:T(8,128)(2,1)} %bitcast.411), calls=%async_computation.2 | async-start | bytes 1572864 | tf_op jit(solution)/shard_map/all_to_all | solution.py:1008
  792.7 143.7 %all-to-all-start = ((bf16[256,4,384]{2,0,1:T(8,128)(2,1)}), bf16[256,4,384]{2,0,1:T(8,128)(2,1)}, u32[]{:S(2)}, u32[]{:S(2)}) async-start(bf16[256,4,384]{2,0,1:T(8,128)(2,1)} %bitcast.410), calls=%async_computation | async-start | bytes 1572864 | tf_op jit(solution)/shard_map/all_to_all | solution.py:1008
  (172 other events, 1228.0 us)
Sparse Core Ops, SparseCore 0:
  82.7 61.1 all-gather.4
  174.2 107.9 all-gather.6
  303.8 57.8 all-gather.8
  388.1 109.3 all-gather.10

commit v5 on v4

--- a/solution.py
+++ b/solution.py
@@ -216,7 +216,7 @@
 
 def backward_kernel(
     grad, gate, hidden, decay, carry, conv, offset, conv_w, gate_w, gate_b, soft,
-    branch_grad,
+    lead_grad, gate_grad,
     ext, prior, grads, chain_decay, local_all, reach_all, seg, totals, arriving, heads_out,
     heads_in, tails, inbox, halo_sems, send_sems, recv_sems,
 ):
@@ -232,12 +232,11 @@
 
     def run_slab(slab, nothing):
         at = pl.ds(pl.multiple_of(slab * LANES, LANES), LANES)
-        gate_at = pl.ds(pl.multiple_of(width + slab * LANES, LANES), LANES)
         for place, lines in ((start, slice(0, half)), (other, slice(half, rows))):
             value, slope = gelu_pair(gate[pl.ds(place, half), at])
             coming = grad[pl.ds(place, half), at]
             grads[lines] = coming * value
-            branch_grad[pl.ds(place, half), gate_at] = (
+            gate_grad[pl.ds(place, half), at] = (
                 coming * hidden[slab, lines] * slope
             ).astype(BRAIN)
         chain_decay[0:rows] = decay[slab]
@@ -315,8 +314,8 @@
             head_sum = head_sum + jnp.where(lines >= 8 - step, moved, 0.0)
         heads_out[:, at] = head_sum
         tails[:, at] = total[rows - 8 : rows]
-        branch_grad[pl.ds(start, half), at] = total[0:half].astype(BRAIN)
-        branch_grad[pl.ds(other, half), at] = total[half:rows].astype(BRAIN)
+        lead_grad[pl.ds(start, half), at] = total[0:half].astype(BRAIN)
+        lead_grad[pl.ds(other, half), at] = total[half:rows].astype(BRAIN)
         return nothing
 
     lax.fori_loop(0, heads, run_head, 0)
@@ -335,9 +334,9 @@
         at = slice(head * HS, (head + 1) * HS)
         there = (head - heads // shards) % heads
         whole = tails[:, at] + heads_in[:, there * HS : (there + 1) * HS] * followed
-        kept = branch_grad[pl.ds(pl.multiple_of(other + half - 16, 16), 16), at]
+        kept = lead_grad[pl.ds(pl.multiple_of(other + half - 16, 16), 16), at]
         tails_pair = jnp.concatenate([kept[0:8], whole.astype(BRAIN)], axis=0)
-        branch_grad[pl.ds(pl.multiple_of(other + half - 16, 16), 16), at] = tails_pair
+        lead_grad[pl.ds(pl.multiple_of(other + half - 16, 16), 16), at] = tails_pair
 
 
 def lasting(microseconds):
@@ -406,7 +405,7 @@
         1,
         [grad, kept["gate"], kept["hidden"], kept["decay"], kept["state_in"], kept["conv"], offset,
          small["conv_weight"], small["gate_weight"], small["gate_bias"], small["soft"]],
-        [((rows, 2 * width), BRAIN)],
+        [((rows, width), BRAIN), ((rows, width), BRAIN)],
         [
             pltpu.VMEM((rows + 8, HS), FLOAT),
             pltpu.VMEM((rows + 8, HS), FLOAT),
@@ -423,7 +422,7 @@
         ]
         + message_scratch(width),
         30,
-    )[0]
+    )
 
 
 def line_plan(pieces, unit):
@@ -462,15 +461,16 @@
     )
 
 
-def closing_kernel(count, *refs):
+def closing_kernel(count, layers, *refs):
+    streams, refs = refs[:layers], refs[layers:]
     own_part, other_part, stream, d_middle, gain = refs[:5]
     shared, split = refs[5 : 5 + count], refs[5 + count : 5 + 2 * count]
-    tokens_out, *refs = refs[5 + 2 * count :]
+    tokens_out, states_out, *refs = refs[5 + 2 * count :]
     shared_out, split_out = refs[:count], refs[count : 2 * count]
     (
         received, outgoing, homing, flat, beside_in, both, inbox, red, red_split, zbox, sbox, zfull,
         sfull, shared_all, split_all, pair_sems, beside_sems, row_sems, col_sems, turn_sems,
-        spread_sems, shared_sems, split_sems, token_sems,
+        spread_sems, shared_sems, split_sems, token_sems, leaving, state_sems,
     ) = refs[2 * count :]
     peers, cols = lax.axis_size("row"), lax.axis_size("col")
     shards = cols // 2
@@ -514,8 +514,24 @@
 
     paired = remote(flat.at[1 - side], beside_in, beside_sems, 0, beside)
     paired.start()
+    mine = pl.ds(pl.multiple_of(col * own, own), own)
+    for layer in range(layers):
+        for at in range(cols):
+            leaving[layer, at] = streams[layer][:, at * piece : (at + 1) * piece].astype(BRAIN)
+    states = []
+    for by in range(1, cols):
+        to = (col + by) % cols
+        for layer in range(layers):
+            slot = layer * (cols - 1) + by - 1
+            there = states_out.at[layer, mine]
+            copy = remote(leaving.at[layer, to], there, state_sems, slot, (row, to))
+            states.append(copy)
+    for layer in range(layers):
+        states_out[layer, mine] = leaving[layer, col]
     pair = remote(other_part, received, pair_sems, 0, (row, col + 1 - 2 * (col % 2)))
     pair.start()
+    for copy in states:
+        copy.start()
     paired.wait()
 
     def add_pair(at, nothing):
@@ -617,13 +633,13 @@
         ].astype(FLOAT)
     for at, rows, lanes, index, lines in split_plan:
         split_out[at][rows, lanes] = split_all[index % 2, index // 2, lines].astype(FLOAT)
-    for copy in returned:
+    for copy in returned + states:
         copy.wait()
     for at in range(cols):
         tokens_out[at * own : (at + 1) * own] = homing[at].astype(FLOAT)
 
 
-def close(own_part, other_part, stream, d_middle, gain, shared, split):
+def close(streams, own_part, other_part, stream, d_middle, gain, shared, split):
     peers, cols = lax.axis_size("row"), lax.axis_size("col")
     shards = cols // 2
     own, d_model = stream.shape
@@ -646,10 +662,11 @@
                       places - 1, cols - 1)
     ]
     result = block_call(
-        partial(closing_kernel, len(shared)),
+        partial(closing_kernel, len(shared), len(streams)),
         2,
-        [own_part, other_part, stream, d_middle, gain, *shared, *split],
+        [*streams, own_part, other_part, stream, d_middle, gain, *shared, *split],
         [((own * cols, d_model // cols), FLOAT)]
+        + [((len(streams), own * cols, d_model // cols), BRAIN)]
         + [(size, FLOAT) for size in shared_sizes]
         + [((rows, columns // shards), FLOAT) for rows, columns in split_sizes],
         [
@@ -669,121 +686,16 @@
             pltpu.VMEM((2, places, cols, unit, LANES), BRAIN),
             pltpu.VMEM((2, places, part, LANES), BRAIN),
         ]
-        + sems,
+        + sems
+        + [
+            pltpu.VMEM((len(streams), cols, own, d_model // cols), BRAIN),
+            pltpu.SemaphoreType.DMA((2, len(streams) * (cols - 1))),
+        ],
         80,
     )
     count = len(shared)
-    split = [value[:, :piece] for value, piece in zip(result[1 + count :], pieces)]
-    return result[0], result[1 : 1 + count], split
-
-
-def opening_kernel(count, routes, *refs):
-    small, refs = refs[:count], refs[count:]
-    tokens, gains, vectors, pack, *refs = refs
-    small_out, refs = refs[:count], refs[count:]
-    tokens_out, gains_out, vectors_out, packs_out, *refs = refs
-    flat, got, others, across_sems, spread_sems, *refs = refs
-    peers, cols = lax.axis_size("row"), lax.axis_size("col")
-    shards = cols // 2
-    row, col = lax.axis_index("row"), lax.axis_index("col")
-    plan = line_plan([value.shape for value in small], flat.shape[1])
-    barrier = pltpu.get_barrier_semaphore()
-    signals = [(row, (col + by) % cols) for by in range(1, cols)]
-    signals += [((row + by) % peers, col) for by in range(1, peers)]
-    for to in signals:
-        pl.semaphore_signal(barrier, inc=1, device_id=to, device_id_type=MESH)
-    flat[...] = jnp.zeros(flat.shape, BRAIN)
-    for at, rows, lanes, index, lines in plan:
-        flat[index, lines] = small[at][rows, lanes]
-    pl.semaphore_wait(barrier, len(signals))
-
-    across, copies = [], []
-    for turn in range(1, shards):
-        to = (row, (col + cols - 2 * turn) % cols)
-        across.append(remote(flat.at[row], got.at[turn - 1], across_sems, turn - 1, to))
-    for copy in across:
-        copy.start()
-    token_got, vector_got, token_sems, gain_sems, vector_sems, pack_sems = refs
-    own, piece = tokens_out.shape[0], tokens.shape[1]
-    for turn in range(1, shards):
-        to = (row, (col + cols - 2 * turn) % cols)
-        copies.append(remote(vectors, vector_got.at[turn - 1], vector_sems, turn - 1, to))
-    copies += shipped(routes, [pack], [packs_out], pack_sems)
-    for by in range(1, cols):
-        to = (col + by) % cols
-        there = pl.ds(pl.multiple_of(to * own, own), own)
-        copies.append(remote(tokens.at[there], token_got.at[col], token_sems, by - 1, (row, to)))
-        copies.append(remote(gains, gains_out.at[col], gain_sems, by - 1, (row, to)))
-    for copy in copies:
-        copy.start()
-    token_got[col] = tokens[pl.ds(pl.multiple_of(col * own, own), own)]
-    gains_out[col] = gains[...]
-    spread = []
-    for turn in range(1, shards):
-        across[turn - 1].wait()
-        for by in range(1, peers):
-            to = ((row + by) % peers, col)
-            slot = (turn - 1) * (peers - 1) + by - 1
-            copy = remote(got.at[turn - 1], others.at[turn - 1, row], spread_sems, slot, to)
-            copy.start()
-            spread.append(copy)
-        others[turn - 1, row] = got[turn - 1]
-    for at in range(count):
-        small_out[at][0] = small[at][...]
-    for copy in copies:
-        copy.wait()
-    for at in range(cols):
-        tokens_out[:, at * piece : (at + 1) * piece] = token_got[at]
-    vectors_out[0] = vectors[...]
-    for turn in range(1, shards):
-        vectors_out[turn] = vector_got[turn - 1]
-    for copy in spread:
-        copy.wait()
-    for turn in range(1, shards):
-        for at, rows, lanes, index, lines in plan:
-            small_out[at][turn, rows, lanes] = others[turn - 1, index, lines]
-
-
-def open_up(ident, small, tokens, gains, vectors, pack):
-    peers, cols = lax.axis_size("row"), lax.axis_size("col")
-    shards = cols // 2
-    rest = max(shards - 1, 1)
-    kept = [value.shape[1] for value in small]
-    small = [
-        jnp.pad(value, ((0, 0), (0, -value.shape[1] % LANES))) if value.shape[1] % LANES else value
-        for value in small
-    ]
-    lines = sum(value.shape[0] * value.shape[1] for value in small) // LANES
-    unit = -(-lines // (peers * 16)) * 16
-    rows, piece = tokens.shape
-    own = rows // cols
-    routes = routes_of(pack.shape[1], range(PARTS), 0, 0)
-    operands = [*small, tokens, gains, vectors, pack]
-    outs = [((shards,) + value.shape, BRAIN) for value in small]
-    outs += [
-        ((own, piece * cols), BRAIN),
-        ((cols,) + gains.shape, FLOAT),
-        ((shards,) + vectors.shape, FLOAT),
-        ((pack.shape[0], pack.shape[1] * shards), BRAIN),
-    ]
-    scratch = [
-        pltpu.VMEM((peers, unit, LANES), BRAIN),
-        pltpu.VMEM((rest, unit, LANES), BRAIN),
-        pltpu.VMEM((rest, peers, unit, LANES), BRAIN),
-        pltpu.SemaphoreType.DMA((2, rest)),
-        pltpu.SemaphoreType.DMA((2, rest * (peers - 1))),
-        pltpu.VMEM((cols, own, piece), BRAIN),
-        pltpu.VMEM((rest,) + vectors.shape, FLOAT),
-    ]
-    scratch += [
-        pltpu.SemaphoreType.DMA((2, size)) for size in (cols - 1, cols - 1, rest, len(routes))
-    ]
-    result = block_call(
-        partial(opening_kernel, len(small), routes), ident, operands, outs, scratch, 30,
-        anywhere=1,
-    )
-    values = [value[:, :, :size] for value, size in zip(result, kept)]
-    return values, result[len(small) :]
+    split = [value[:, :piece] for value, piece in zip(result[2 + count :], pieces)]
+    return result[0], result[1], result[2 : 2 + count], split
 
 
 PARTS = 3
@@ -814,29 +726,164 @@
     return copies
 
 
+def opening_kernel(
+    routes, tokens, gains, vectors, pack,
+    tokens_out, gains_out, vectors_out, packs_out,
+    token_got, token_sems, gain_sems, vector_sems, pack_sems,
+):
+    cols = lax.axis_size("col")
+    shards = cols // 2
+    row, col = lax.axis_index("row"), lax.axis_index("col")
+    own, piece = tokens_out.shape[0], tokens.shape[1]
+    barrier = pltpu.get_barrier_semaphore()
+    for by in range(1, cols):
+        pl.semaphore_signal(barrier, inc=1, device_id=(row, (col + by) % cols), device_id_type=MESH)
+    pl.semaphore_wait(barrier, cols - 1)
+    copies = shipped(routes, [pack], [packs_out], pack_sems)
+    for turn in range(1, shards):
+        to = (row, (col + cols - 2 * turn) % cols)
+        copies.append(remote(vectors, vectors_out.at[turn], vector_sems, turn - 1, to))
+    for by in range(1, cols):
+        to = (col + by) % cols
+        there = pl.ds(pl.multiple_of(to * own, own), own)
+        copies.append(remote(tokens.at[there], token_got.at[col], token_sems, by - 1, (row, to)))
+        copies.append(remote(gains, gains_out.at[col], gain_sems, by - 1, (row, to)))
+    for copy in copies:
+        copy.start()
+    token_got[col] = tokens[pl.ds(pl.multiple_of(col * own, own), own)]
+    gains_out[col] = gains[...]
+    vectors_out[0] = vectors[...]
+    for copy in copies:
+        copy.wait()
+    for at in range(cols):
+        tokens_out[:, at * piece : (at + 1) * piece] = token_got[at]
+
+
+def open_up(ident, tokens, gains, vectors, pack):
+    cols = lax.axis_size("col")
+    shards = cols // 2
+    rows, piece = tokens.shape
+    own = rows // cols
+    routes = routes_of(pack.shape[1], range(PARTS), 0, 0)
+    outs = [
+        ((own, piece * cols), BRAIN),
+        ((cols,) + gains.shape, FLOAT),
+        ((shards,) + vectors.shape, FLOAT),
+        ((pack.shape[0], pack.shape[1] * shards), BRAIN),
+    ]
+    sizes = (cols - 1, cols - 1, max(shards - 1, 1), len(routes))
+    scratch = [pltpu.VMEM((cols, own, piece), BRAIN)]
+    scratch += [pltpu.SemaphoreType.DMA((2, size)) for size in sizes]
+    return block_call(
+        partial(opening_kernel, routes), ident, [tokens, gains, vectors, pack], outs, scratch, 30,
+        anywhere=1,
+    )
+
+
+def settling_kernel(count, routes, *refs):
+    normed, small, pack, refs = refs[0], refs[1 : 1 + count], refs[1 + count], refs[2 + count :]
+    full_out, small_out, packs_out, refs = refs[0], refs[1 : 1 + count], refs[1 + count], refs[2 + count :]
+    flat, got, others, pair_sems, across_sems, spread_sems, pack_sems = refs
+    peers, cols = lax.axis_size("row"), lax.axis_size("col")
+    shards = cols // 2
+    row, col = lax.axis_index("row"), lax.axis_index("col")
+    own = normed.shape[0]
+    plan = line_plan([value.shape for value in small], flat.shape[1])
+    peer = (row, col + 1 - 2 * (col % 2))
+    signals = [peer] + [(row, (col + 2 * turn) % cols) for turn in range(1, shards)]
+    signals += [((row + by) % peers, col) for by in range(1, peers)]
+    barrier = pltpu.get_barrier_semaphore()
+    for to in signals:
+        pl.semaphore_signal(barrier, inc=1, device_id=to, device_id_type=MESH)
+    flat[...] = jnp.zeros(flat.shape, BRAIN)
+    for at, rows, lanes, index, lines in plan:
+        flat[index, lines] = small[at][rows, lanes]
+    pl.semaphore_wait(barrier, len(signals))
+
+    across = []
+    for turn in range(1, shards):
+        to = (row, (col + cols - 2 * turn) % cols)
+        across.append(remote(flat.at[row], got.at[turn - 1], across_sems, turn - 1, to))
+    pair = remote(normed, full_out.at[pl.ds(own, own)], pair_sems, 0, peer)
+    copies = [pair] + shipped(routes, [pack], [packs_out], pack_sems)
+    for copy in across + copies:
+        copy.start()
+    full_out[0:own] = normed[...]
+    for at in range(count):
+        small_out[at][0] = small[at][...]
+    spread = []
+    for turn in range(1, shards):
+        across[turn - 1].wait()
+        for by in range(1, peers):
+            to = ((row + by) % peers, col)
+            slot = (turn - 1) * (peers - 1) + by - 1
+            copy = remote(got.at[turn - 1], others.at[turn - 1, row], spread_sems, slot, to)
+            copy.start()
+            spread.append(copy)
+        others[turn - 1, row] = got[turn - 1]
+    for copy in spread:
+        copy.wait()
+    for turn in range(1, shards):
+        for at, rows, lanes, index, lines in plan:
+            small_out[at][turn, rows, lanes] = others[turn - 1, index, lines]
+    for copy in copies:
+        copy.wait()
+
+
+def settle(ident, normed, small, pack):
+    peers, shards = lax.axis_size("row"), lax.axis_size("col") // 2
+    rest = max(shards - 1, 1)
+    kept = [value.shape[1] for value in small]
+    small = [
+        jnp.pad(value, ((0, 0), (0, -value.shape[1] % LANES))) if value.shape[1] % LANES else value
+        for value in small
+    ]
+    lines = sum(value.shape[0] * value.shape[1] for value in small) // LANES
+    unit = -(-lines // (peers * 16)) * 16
+    own, d_model = normed.shape
+    routes = routes_of(pack.shape[1], range(PARTS), 0, 0)
+    outs = [((2 * own, d_model), BRAIN)]
+    outs += [((shards,) + value.shape, BRAIN) for value in small]
+    outs += [((pack.shape[0], pack.shape[1] * shards), BRAIN)]
+    scratch = [
+        pltpu.VMEM((peers, unit, LANES), BRAIN),
+        pltpu.VMEM((rest, unit, LANES), BRAIN),
+        pltpu.VMEM((rest, peers, unit, LANES), BRAIN),
+    ]
+    sizes = (1, rest, rest * (peers - 1), len(routes))
+    scratch += [pltpu.SemaphoreType.DMA((2, size)) for size in sizes]
+    full, *values, packs = block_call(
+        partial(settling_kernel, len(small), routes), ident, [normed, *small, pack], outs, scratch,
+        40, anywhere=1,
+    )
+    return full, [value[:, :, :size] for value, size in zip(values, kept)], packs
+
+
 TILE = 256
 LINES = 64
 
 
-def turn_kernel(backward, offset, plan, sources, counts, routes, *refs):
-    (x, wide, x2, w2, stream, gain, d_stream), refs = refs[:7], refs[7:]
+def turn_kernel(backward, lefts, offset, plan, sources, counts, routes, *refs):
+    xs, refs = refs[:lefts], refs[lefts:]
+    (wide, x2, w2, stream, gain, d_stream, factor, mask), refs = refs[:8], refs[8:]
     extra, refs = refs[:sources], refs[sources:]
     cargo, refs = refs[: counts[0]], refs[counts[0] :]
-    (new_out, full_out), refs = refs[:2], refs[2:]
+    (new_out, full_out, low_out), refs = refs[:3], refs[3:]
     grad_outs, refs = refs[: len(plan)], refs[len(plan) :]
     cargo_outs, refs = refs[: counts[1]], refs[counts[1] :]
     weights, sending, received, mine, weight_sems, share_sems, spread_sems, cargo_sems = refs
     cols = lax.axis_size("col")
     shards = cols // 2
     own = stream.shape[0]
-    depth = x.shape[1]
+    depths = [x.shape[1] for x in xs]
+    depth = sum(depths)
     tiles = sending.shape[0]
     row, col = lax.axis_index("row"), lax.axis_index("col")
     peer = (row, col + 1 - 2 * (col % 2))
 
     barrier = pltpu.get_barrier_semaphore()
     greeted = [peer]
-    if routes:
+    if any(route[-1] for route in routes):
         greeted += [(row, (col + 2 * other) % cols) for other in range(1, shards)]
     for to in greeted:
         pl.semaphore_signal(barrier, inc=1, device_id=to, device_id_type=MESH)
@@ -874,7 +921,11 @@
     def project(tile, nothing):
         weight_copy(tile).wait()
         at = pl.ds(pl.multiple_of(tile * TILE, TILE), TILE)
-        total = nt(x[...], weights[tile]) + nn(x2[...], w2[:, at])
+        total = nn(x2[...], w2[:, at])
+        begin = 0
+        for x, size in zip(xs, depths):
+            total = total + nt(x[...], weights[tile, :, begin : begin + size])
+            begin += size
         sending[tile] = total[own:].astype(BRAIN)
         mine[tile] = total[:own]
         share_copy(tile).start()
@@ -883,9 +934,8 @@
     lax.fori_loop(0, tiles, project, 0)
 
     def gradients(part):
-        for (left, right, lanes), out in part:
-            value = (x if right is None else extra[right])[:, lanes]
-            out[...] = tn(extra[left][...], value)
+        for (left, right), out in part:
+            out[...] = tn(extra[left][...], (*extra, *xs)[right][...])
 
     pairs = list(zip(plan, grad_outs))
     gradients(pairs[: len(pairs) // 2])
@@ -921,45 +971,52 @@
     lax.fori_loop(0, own // LINES, finish, 0)
     gradients(pairs[len(pairs) // 2 :])
 
+    def lower(lines):
+        low_out[lines] = (nt(full_out[lines], factor[...]) * mask[lines]).astype(BRAIN)
+
+    lower(slice(0, own))
+
     def leave(at, nothing):
         spread_copy(at).wait()
         return nothing
 
     lax.fori_loop(0, own // LINES, leave, 0)
+    lower(slice(own, 2 * own))
     for copy in carried:
         copy.wait()
 
 
 def turn(
-    ident, x, wide, offset, x2, w2, stream, gain, d_stream=None, extra=(), plan=(), cargo=(),
-    widths=(), routes=(),
+    ident, xs, wide, offset, x2, w2, stream, gain, factor, mask, d_stream=None, extra=(), plan=(),
+    cargo=(), widths=(), routes=(),
 ):
     own, d_model = stream.shape
-    depth = x.shape[1]
+    depth = sum(x.shape[1] for x in xs)
     tiles = d_model // TILE
     whole = pl.BlockSpec(memory_space=pltpu.VMEM)
     backward = d_stream is not None
-    operands = [x, wide, x2, w2, stream, gain, d_stream if backward else gain, *extra]
+    operands = [*xs, wide, x2, w2, stream, gain, d_stream if backward else gain, factor, mask]
+    operands += extra
     specs = [whole] * len(operands)
     anywhere = pl.BlockSpec(memory_space=pl.ANY)
-    specs[1] = anywhere
+    specs[len(xs)] = anywhere
     operands += cargo
     specs += [anywhere] * len(cargo)
     plan = tuple(plan)
     sizes = []
-    for left, right, lanes in plan:
-        wide_by = (x if right is None else extra[right]).shape[1]
-        sizes.append((extra[left].shape[1], len(range(wide_by)[lanes])))
+    for left, right in plan:
+        sizes.append((extra[left].shape[1], [*extra, *xs][right].shape[1]))
     return pl.pallas_call(
-        partial(turn_kernel, backward, offset, plan, len(extra), (len(cargo), len(widths)), tuple(routes)),
+        partial(turn_kernel, backward, len(xs), offset, plan, len(extra), (len(cargo), len(widths)), tuple(routes)),
         out_shape=[
             jax.ShapeDtypeStruct((own, d_model), FLOAT),
             jax.ShapeDtypeStruct((2 * own, d_model), BRAIN),
+            jax.ShapeDtypeStruct((2 * own, factor.shape[0]), BRAIN),
         ]
         + [jax.ShapeDtypeStruct(size, FLOAT) for size in sizes]
         + [jax.ShapeDtypeStruct((cargo[0].shape[0], size), cargo[0].dtype) for size in widths],
         in_specs=specs,
-        out_specs=[whole] * (2 + len(plan)) + [anywhere] * len(widths),
+        out_specs=[whole] * (3 + len(plan)) + [anywhere] * len(widths),
         scratch_shapes=[
             pltpu.VMEM((tiles, TILE, depth), BRAIN),
             pltpu.VMEM((tiles, own, TILE), BRAIN),
@@ -1004,14 +1061,6 @@
     return lax.all_to_all(value, "col", split_axis=0, concat_axis=1, tiled=True)
 
 
-def from_sequence(value):
-    return lax.all_to_all(value, "col", split_axis=1, concat_axis=0, tiled=True)
-
-
-def both_halves(value):
-    return jnp.concatenate([value, partner(value)], axis=0)
-
-
 def half_share(own, other):
     return own + partner(other.astype(BRAIN)).astype(FLOAT)
 
@@ -1025,12 +1074,10 @@
     return (value * pick).astype(BRAIN)
 
 
-def recur_branch(normed_full, wide, small, ctx):
-    pick = ctx["pick"]
-    ranks = pick.shape[1]
+def recur_branch(normed_full, low, wide, small, ctx):
+    ranks = ctx["pick"].shape[1]
     width = wide.shape[1] // 3
-    low = nt(normed_full, small["inlet_lower"])
-    inner = [masked(low[:, b * ranks : (b + 1) * ranks], pick) for b in range(2)]
+    inner = [low[:, b * ranks : (b + 1) * ranks] for b in range(2)]
     branch = nn(normed_full, wide[:, : 2 * width])
     lead = branch[:, :width] + nn(inner[0], small["inlet_upper"][0])
     gate = branch[:, width:] + nn(inner[1], small["inlet_upper"][1])
@@ -1038,42 +1085,44 @@
 
 
 def recur_part(
-    ident, stream, lead, gate, wide, small, gain, ctx, ready, cargo, widths, routes
+    ident, stream, lead, gate, wide, small, gain, factor, ctx, ready, cargo, widths, routes
 ):
     pick, offset = ctx["pick"], ctx["offset"]
     width = lead.shape[1]
     conv, decay, hidden, mixed, state_in = recur_forward(lead, gate, offset, small)
     mixed = after(mixed, ready)
     lowrank = masked(nt(mixed, small["outlet_lower"]), pick)
-    middle, normed_two_full, *parts = turn(
-        ident, mixed, wide, 2 * width, lowrank, small["outlet_upper"], stream, gain, cargo=cargo,
-        widths=widths, routes=routes,
+    middle, normed_two_full, low_two, *parts = turn(
+        ident, [mixed], wide, 2 * width, lowrank, small["outlet_upper"], stream, gain, factor,
+        ctx["picks"], cargo=cargo, widths=widths, routes=routes,
     )
     kept = dict(
         conv=conv, decay=decay, hidden=hidden, state_in=state_in, mixed=mixed, lowrank=lowrank,
         middle=middle, normed_two_full=normed_two_full,
     )
-    return middle, normed_two_full, kept, parts
-
-
-def hidden_part(normed_two_full, wide, small, ctx):
+    return middle, normed_two_full, low_two, kept, parts
+
+
+def hidden_part(normed_two_full, low_two, wide, small, ctx):
     pick = ctx["pick"]
     ranks = pick.shape[1]
     spread = wide.shape[1] // 3
-    low_two = nt(normed_two_full, small["expand_lower"])
-    inner_two = [masked(low_two[:, b * ranks : (b + 1) * ranks], pick) for b in range(2)]
+    inner_two = [low_two[:, b * ranks : (b + 1) * ranks] for b in range(2)]
     branch_two = nn(normed_two_full, wide[:, : 2 * spread])
     up_gate = branch_two[:, :spread] + nn(inner_two[0], small["expand_upper"][0])
     up_value = branch_two[:, spread:] + nn(inner_two[1], small["expand_upper"][1])
-    product = (gelu_tanh(up_gate) * up_value).astype(BRAIN)
+    value, slope = gelu_pair(up_gate)
+    product = (value * up_value).astype(BRAIN)
+    factors = [(slope * up_value).astype(BRAIN), value.astype(BRAIN)]
     lowrank_two = masked(nt(product, small["shrink_lower"]), pick)
     return dict(
-        inner_two=inner_two, up_gate=up_gate, up_value=up_value, product=product,
-        lowrank_two=lowrank_two,
-    )
-
-
-def layer_backward(ident, d_stream, d_out, wide, small, gains, kept, ctx, first, pending):
+        inner_two=inner_two, factors=factors, product=product, lowrank_two=lowrank_two,
+    )
+
+
+def layer_backward(
+    ident, d_stream, d_out, d_low_two, wide, small, upper_before, gains, kept, ctx, pending
+):
     recur_wide, hidden_wide = wide
     pick, offset = ctx["pick"], ctx["offset"]
     own = d_stream.shape[0]
@@ -1081,62 +1130,46 @@
     width = recur_wide.shape[1] // 3
     spread = hidden_wide.shape[1] // 3
 
-    d_low_two = masked(nt(d_out, small["shrink_upper"]), pick)
     d_product = nn(d_out, hidden_wide[:, 2 * spread :]) + nn(d_low_two, small["shrink_lower"])
-    value, slope = gelu_pair(kept["up_gate"])
-    d_branch_two = jnp.concatenate(
-        [(slope * kept["up_value"] * d_product).astype(BRAIN), (value * d_product).astype(BRAIN)],
-        axis=1,
-    )
+    d_branch_two = [(part.astype(FLOAT) * d_product).astype(BRAIN) for part in kept["factors"]]
     d_inner_two = jnp.concatenate(
-        [
-            masked(nt(d_branch_two[:, b * spread : (b + 1) * spread], small["expand_upper"][b]), pick)
-            for b in range(2)
-        ],
-        axis=1,
-    )
-    halves = (slice(0, spread), slice(spread, 2 * spread))
-    every = slice(None)
-    d_middle, d_mid, shrink_upper, shrink_lower, expand_lower, expand_a, expand_b = turn(
+        [masked(nt(d_branch_two[b], small["expand_upper"][b]), pick) for b in range(2)], axis=1
+    )
+    d_middle, d_mid, d_low, shrink_upper, shrink_lower, expand_lower, expand_a, expand_b = turn(
         ident, d_branch_two, hidden_wide, 0, d_inner_two, small["expand_lower"], kept["middle"],
-        gains[1:2], d_stream,
+        gains[1:2], small["outlet_upper"], pick, d_stream,
         [kept["lowrank_two"], d_out, d_low_two, kept["product"], d_inner_two,
          kept["normed_two_full"], *kept["inner_two"]],
-        [(0, 1, every), (2, 3, every), (4, 5, every), (6, None, halves[0]), (7, None, halves[1])],
+        [(0, 1), (2, 3), (4, 5), (6, 8), (7, 9)],
     )
     expand_upper = jnp.concatenate([expand_a, expand_b], axis=0)
 
-    d_mid, ctx["last"] = lax.optimization_barrier((d_mid, pending))
-    d_low = masked(nt(d_mid, small["outlet_upper"]), pick)
+    if pending is not None:
+        d_mid, ctx["last"] = lax.optimization_barrier((d_mid, pending))
     d_mixed = nn(d_mid, recur_wide[:, 2 * width :]) + nn(d_low, small["outlet_lower"])
     d_branch = recur_backward(d_mixed, kept, offset, small)
     d_inner = jnp.concatenate(
-        [
-            masked(nt(d_branch[:, b * width : (b + 1) * width], small["inlet_upper"][b]), pick)
-            for b in range(2)
-        ],
-        axis=1,
-    )
-    halves = (slice(0, width), slice(width, 2 * width))
-    if first:
+        [masked(nt(d_branch[b], small["inlet_upper"][b]), pick) for b in range(2)], axis=1
+    )
+    if upper_before is None:
         outlet_upper = tn(kept["lowrank"], d_mid)
         outlet_lower = tn(d_low, kept["mixed"])
         inlet_lower = tn(d_inner, kept["normed_full"])
-        inlet_a, inlet_b = (tn(kept["inner"][b], d_branch[:, halves[b]]) for b in range(2))
+        inlet_a, inlet_b = (tn(kept["inner"][b], d_branch[b]) for b in range(2))
         result = tuple(
-            nt(d_branch[part], recur_wide[:, : 2 * width]) + nn(d_inner[part], small["inlet_lower"])
+            nt(d_branch[0][part], recur_wide[:, :width])
+            + nt(d_branch[1][part], recur_wide[:, width : 2 * width])
+            + nn(d_inner[part], small["inlet_lower"])
             for part in (slice(0, own), slice(own, rows))
         )
     else:
-        d_before, d_out_before, outlet_upper, outlet_lower, inlet_lower, inlet_a, inlet_b = turn(
+        *result, outlet_upper, outlet_lower, inlet_lower, inlet_a, inlet_b = turn(
             ident + 1, d_branch, recur_wide, 0, d_inner, small["inlet_lower"], kept["stream"],
-            gains[0:1], d_middle,
+            gains[0:1], upper_before, pick, d_middle,
             [kept["lowrank"], d_mid, d_low, kept["mixed"], d_inner, kept["normed_full"],
              *kept["inner"]],
-            [(0, 1, every), (2, 3, every), (4, 5, every), (6, None, halves[0]),
-             (7, None, halves[1])],
+            [(0, 1), (2, 3), (4, 5), (6, 8), (7, 9)],
         )
-        result = (d_before, d_out_before)
     inlet_upper = jnp.concatenate([inlet_a, inlet_b], axis=0)
     shared = (inlet_lower, outlet_upper, expand_lower, shrink_upper)
     split = (inlet_upper, outlet_lower, expand_upper, shrink_lower)
@@ -1172,7 +1205,8 @@
     )
     within = (at_home[:, None] >= starts[None, :]) & (at_home[:, None] < ends[None, :])
     pick = jnp.repeat(within.astype(FLOAT), rank, axis=1)
-    ctx = dict(pick=pick, offset=offset, pending={})
+    picks = jnp.concatenate([pick, pick], axis=1)
+    ctx = dict(pick=pick, picks=picks, offset=offset, pending={})
 
 
     def by_doc(factor, axis):
@@ -1221,12 +1255,6 @@
             pack = jnp.pad(pack.reshape(pack.shape[0], PARTS, -1), ((0, 0), (0, 0), (0, short)))
             pack = pack.reshape(pack.shape[0], -1)
         return pack
-
-    def side_packs(pack):
-        parts = all_shards(pack)
-        piece = pack.shape[1] // PARTS
-        columns = [part[:, at * piece : (at + 1) * piece] for at in range(PARTS) for part in parts]
-        return jnp.concatenate(columns, axis=1)
 
     def gathered(packs, piece):
         whole = lax.all_gather(packs, "row", axis=0, tiled=True)
@@ -1256,7 +1284,7 @@
             shrink_upper=lows["shrink_upper"][layer],
         )
 
-    outputs, saved, wides, smalls = [], [], [], []
+    saved, wides, smalls = [], [], []
     recur_packs = [packed(inlet_weight[at], outlet_weight[at]) for at in range(LAYERS)]
     hidden_packs = [packed(expand_weight[at], shrink_weight[at]) for at in range(LAYERS)]
     def side_by_side(value):
@@ -1267,58 +1295,55 @@
             [value[at].reshape((2, -1) + gate_weight.shape[3:]) for at in range(shards)], axis=1
         )
 
-    (narrow, gates, broad), (stream, gains, vectors_all, recur_side) = open_up(
-        20, [narrow_own[0], rows_of(gate_weight[0]), broad_own[0]], tokens, rows_of(norm_gain),
-        rows_of(vectors_own), recur_packs[0],
-    )
-    narrow, gates, broad = side_by_side(narrow), heads_in_turn(gates), side_by_side(broad)
+    stream, gains, vectors_all, recur_side = open_up(
+        20, tokens, rows_of(norm_gain), rows_of(vectors_own), recur_packs[0]
+    )
     gains = jnp.moveaxis(gains, 0, 1).reshape(LAYERS, 2, d_model)
     vectors_all = side_by_side(vectors_all).reshape(LAYERS, -1, shards * part_width)
     wide_one = gathered(recur_side, part_width)
-    hidden_side = side_packs(after(hidden_packs[0], stream))
     stream = stream.astype(FLOAT)
     _, normed = norm_forward(stream, gains[0][0])
-    normed_full = both_halves(normed)
-    normed_full, hidden_side = lax.optimization_barrier((normed_full, hidden_side))
+    small = []
+    for layer in range(LAYERS):
+        small += [narrow_own[layer], rows_of(gate_weight[layer]), broad_own[layer]]
+    normed_full, small, hidden_side = settle(21, normed, small, hidden_packs[0])
+    bits = [
+        (side_by_side(narrow), heads_in_turn(gates), side_by_side(broad))
+        for narrow, gates, broad in zip(small[0::3], small[1::3], small[2::3])
+    ]
+    wide_two = gathered(hidden_side, part_spread)
+    low = masked(nt(normed_full, lows["inlet_lower"][0]), picks)
     for layer in range(LAYERS):
         more_layers = layer + 1 < LAYERS
         kept = dict(stream=stream, normed_full=normed_full)
+        narrow, gates, broad = bits[layer]
         small_one = recur_small(layer, narrow, gates)
-        lead, gate, inner = recur_branch(normed_full, wide_one, small_one, ctx)
+        lead, gate, inner = recur_branch(normed_full, low, wide_one, small_one, ctx)
         ready, cargo, widths, routes = [], [], [], []
-        if layer == 0:
-            wide_two = gathered(after(hidden_side, lead), part_spread)
         if more_layers:
-            narrow_parts, gate_parts = (
-                all_shards(after(value[layer + 1], lead)) for value in (narrow_own, gate_weight)
-            )
-            ready = [narrow_parts[1:], gate_parts[1:]]
-            cargo = [recur_packs[layer + 1], hidden_packs[layer + 1]]
-            spans = [pack.shape[1] for pack in cargo]
-            widths = [spans[0] * shards, spans[1] // PARTS * shards]
-            routes = routes_of(spans[0], range(PARTS), 0, 0) + routes_of(spans[1], [0], 1, 1)
+            packs = all_shards(after(recur_packs[layer + 1], normed_full))
+            lead, packs[1:] = lax.optimization_barrier((lead, packs[1:]))
+            cargo = [*packs, hidden_packs[layer + 1]]
+            piece, spread_piece = (value.shape[1] // PARTS for value in cargo[-2:])
+            widths = [PARTS * shards * piece, shards * spread_piece]
+            routes = [
+                (at, part * piece, piece, 0, (part * shards + at) * piece, 0)
+                for part in range(PARTS)
+                for at in range(shards)
+            ] + routes_of(PARTS * spread_piece, [0], shards, 1)
         elif layer:
             ending = to_sequence(after(cotangent, lead))
             ready = [ending]
-            cargo = [broad_own[layer]]
-            spread_piece = cargo[0].shape[1]
-            if spread_piece % LANES:
-                cargo = [jnp.pad(cargo[0], ((0, 0), (0, -spread_piece % LANES)))]
-            span = cargo[0].shape[1]
-            widths = [span * shards]
-            routes = [(0, 0, span, 0, shard * span, shard) for shard in range(shards)]
-        middle, normed_two_full, more, sides = recur_part(
-            3 + 2 * layer, stream, lead, gate, wide_one, small_one, gains[layer][1:2], ctx, ready,
-            cargo, widths, routes,
+        middle, normed_two_full, low_two, more, sides = recur_part(
+            3 + 2 * layer, stream, lead, gate, wide_one, small_one, gains[layer][1:2],
+            lows["expand_lower"][layer], ctx, ready, cargo, widths, routes,
         )
-        if layer and not more_layers:
-            broad = sides[0].reshape(sides[0].shape[0], shards, -1)[:, :, :spread_piece]
-            broad = broad.reshape(broad.shape[0], -1)
         kept.update(inner=inner, gate=gate, **more)
         if more_layers:
             wide_next = gathered(sides[0], part_width)
+            others = all_shards(after(hidden_packs[layer + 1][:, spread_piece:], middle))[1:]
         small_two = hidden_small(layer, broad)
-        more = hidden_part(normed_two_full, wide_two, small_two, ctx)
+        more = hidden_part(normed_two_full, low_two, wide_two, small_two, ctx)
         kept.update(more)
         wides.append((wide_one, wide_two))
         smalls.append({**small_one, **small_two})
@@ -1326,16 +1351,22 @@
         product, lowrank, upper = more["product"], more["lowrank_two"], small_two["shrink_upper"]
         spread = product.shape[1]
         if more_layers:
-            pack = hidden_packs[layer + 1]
-            span, early = pack.shape[1], sides[1].shape[1]
-            routes = routes_of(span, range(1, PARTS), 0, 0) + [(1, 0, early, 0, 0, 0)]
-            stream, normed_full, hidden_side = turn(
-                4 + 2 * layer, product, wide_two, 2 * spread, lowrank, upper, middle,
-                gains[layer + 1][0:1], cargo=[pack, sides[1]], widths=[span * shards],
+            product, others, kept["factors"] = lax.optimization_barrier(
+                (product, others, more["factors"])
+            )
+            cargo = [hidden_packs[layer + 1], *others, sides[1]]
+            routes = [
+                (at, (part - (at > 0)) * spread_piece, spread_piece, 0,
+                 (part * shards + at) * spread_piece, 0)
+                for part in range(1, PARTS)
+                for at in range(shards)
+            ] + [(shards, 0, shards * spread_piece, 0, 0, 0)]
+            stream, normed_full, low, hidden_side = turn(
+                4 + 2 * layer, [product], wide_two, 2 * spread, lowrank, upper, middle,
+                gains[layer + 1][0:1], lows["inlet_lower"][layer + 1], ctx["picks"], cargo=cargo, widths=[PARTS * shards * spread_piece],
                 routes=routes,
             )
             wide_two_next = gathered(hidden_side, part_spread)
-            narrow, gates = (jnp.concatenate(part, axis=1) for part in (narrow_parts, gate_parts))
             wide_one, wide_two = wide_next, wide_two_next
         else:
             shrink = wide_two[:, 2 * spread :]
@@ -1345,22 +1376,26 @@
             ]
             stream = middle + half_share(*parts)
             last_stream = stream
-        outputs.append(from_sequence(stream.astype(BRAIN)))
-    ctx["pending"] = {LAYERS - 1: last_stream, LAYERS - 2: outputs.pop()}
-    d_stream, d_out = ending.astype(FLOAT), both_halves(after(ending, normed_two_full))
+    ctx["pending"] = {LAYERS - 1: last_stream}
+    d_out = jnp.concatenate(
+        [ending, after(partner(after(ending, normed_two_full)), product)], axis=0
+    )
+    d_stream = ending.astype(FLOAT)
+    d_low_two = masked(nt(d_out, smalls[-1]["shrink_upper"]), pick)
     shared_parts, split_parts = [], []
     for layer in reversed(range(LAYERS)):
         kept = saved[layer]
         d_middle, result, shared_more, split_more = layer_backward(
-            3 + 2 * LAYERS + 2 * layer, d_stream, d_out, wides[layer], smalls[layer], gains[layer],
-            kept, ctx, layer == 0, ctx["pending"].get(layer),
+            3 + 2 * LAYERS + 2 * layer, d_stream, d_out, d_low_two, wides[layer], smalls[layer],
+            lows["shrink_upper"][layer - 1] if layer else None, gains[layer], kept, ctx,
+            ctx["pending"].get(layer),
         )
         shared_parts = [*shared_more, *shared_parts]
         split_parts = [*split_more, *split_parts]
         if layer:
-            d_stream, d_out = result
-    tokens_grad, shared_parts, split_parts = close(
-        result[0], result[1].astype(BRAIN), kept["stream"], d_middle, gains[0][:1], shared_parts,
+            d_stream, d_out, d_low_two = result
+    tokens_grad, states, shared_parts, split_parts = close(
+        [*(kept["stream"] for kept in saved[1:]), ctx["last"]], result[0], result[1].astype(BRAIN), kept["stream"], d_middle, gains[0][:1], shared_parts,
         split_parts,
     )
     inlet_low, outlet_up, expand_low, shrink_up = (
@@ -1385,7 +1420,7 @@
         return jnp.moveaxis(grad, -1, 1)
 
     return (
-        jnp.stack([*outputs, ctx["last"]], axis=0),
+        states,
         tokens_grad,
         lower_out(inlet_low, 2),
         by_adapter(inlet_up, 2),

time: 972 us -> 917 us (0.943)
  waiting for transfers between devices: 62.7 us -> 24.3 us
  Pallas kernels: 603 us -> 620 us
  starting transfers between devices: 27.4 us -> 12.7 us
  local copies, waits for them, and re-layouts: 76 us -> 63.7 us
    pallas_call x6 -> x7, Pallas kernels: 280 us -> 344 us  [block_call(): pl.pallas_call(kernel, out_shape=[jax.ShapeDtypeStruct(*out) for out in o...]
    pallas_call x6, Pallas kernels: 323 us -> 276 us  [turn(): pl.pallas_call(partial(turn_kernel, backward, len(xs), offset, plan, len(...]
    ppermute x3 -> x2, waiting for transfers between devices: 25.4 us -> 0.01 us  [partner(): return lax.ppermute(value, 'col', [(at, at ^ 1) for at in range(peers)])]
    ppermute x3 -> x2, waiting for transfers between devices: 37.2 us -> 22.4 us  [from_shard(): lax.ppermute(value, 'col', [((at + 2 * turn) % peers, at) for at in range...]
    all_to_all x2 -> x0, starting transfers between devices: 11.4 us -> none  [from_sequence(): return lax.all_to_all(value, 'col', split_axis=1, concat_axis=0, tiled=True)]
    unnamed x375 -> x339, local copies, waits for them, and re-layouts: 44.5 us -> 37.1 us
    dot_general x24 -> x20, matrix products: 36.5 us -> 33.4 us  [nt(): lax.dot_general(left, right, (((1,), (1,)), ((), ())), preferred_element_...]
  transfers between devices with their start and end apart: 13 -> 9, of which waited for: 3 -> 3; matrix products, arithmetic and copies ran while one was open for 11% -> 11% of each run, Pallas kernels for 49% -> 36%
where the time goes in v5:
time: 917 us; the launch traced here: 909 us
  Pallas kernels  620 us (68%)
  matrix products  127 us (14%)
  local copies, waits for them, and re-layouts  63.7 us (7%)
  other arithmetic  36 us (4%)
  between operations  25.5 us (3%)
  waiting for transfers between devices  24.3 us (3%)
  starting transfers between devices  12.7 us (1%)
    pallas_call x7, Pallas kernels, block_call(): pl.pallas_call(kernel, out_shape=[jax.ShapeDtypeStruct(*out) for out in o...  344 us
    pallas_call x6, Pallas kernels, turn(): pl.pallas_call(partial(turn_kernel, backward, len(xs), offset, plan, len(...  276 us
    dot_general x24, matrix products, nn(): lax.dot_general(left, right, (((1,), (0,)), ((), ())), preferred_element_...  88.6 us
    unnamed x339, local copies, waits for them, and re-layouts  37.1 us
    dot_general x20, matrix products, nt(): lax.dot_general(left, right, (((1,), (1,)), ((), ())), preferred_element_...  33.4 us
    ppermute x2, waiting for transfers between devices, from_shard(): lax.ppermute(value, 'col', [((at + 2 * turn) % peers, at) for at in range...  22.4 us
  transfers between devices with their start and end apart: 9, of which 3 were waited for; matrix products, arithmetic and copies ran while one was open for 11% of the time, Pallas kernels for 36%

profile of v5, /device:TPU:0, one launch (start us, length us, event | category | flops | bytes accessed | tf_op | source)
XLA Modules:
  0.0 908.9 jit_solution(3740547626183428867)
XLA Ops:
  13.2 46.0 %shard_map.285 = (bf16[256,1536]{1,0:T(8,128)(2,1)S(1)}, f32[4,4,384]{2,1,0:T(4,128)S(1)}, f32[2,16,512]{2,1,0:T(8,128)S(1)}, bf16[192,3072]{1,0:T(8,128)(2,1)}) custom-call(bf16[1024,384]{1,0:T(8,128)(2,1)S(1)} %copy-done.66, f32[4,384]{1,0:T(4,128)S(1)} %reshape.409.gains, f32[16,512]{1,0:T(8,128)S(1)} %maximum_bitcast_fusion.vectors, ...), custom_call_target="tpu_custom_call" | custom-call | flops 32999999488 | bytes 90000000 | tf_op jit(solution)/shard_map/pallas_call | solution.py:350
  76.1 79.1 %shard_map.286 = (bf16[512,1536]{1,0:T(8,128)(2,1)}, bf16[2,192,512]{2,1,0:T(8,128)(2,1)S(1)}, bf16[2,1024,256]{2,1,0:T(8,128)(2,1)}, bf16[2,192,1152]{2,1,0:T(8...) custom-call(bf16[256,1536]{1,0:T(8,128)(2,1)S(1)} %multiply_convert_, ...), custom_call_target="tpu_custom_call" | custom-call | flops 44000002048 | bytes 120000000 | tf_op jit(solution)/shard_map/pallas_call | solution.py:350
  174.0 6.1 fusion.8
  185.5 26.0 %shard_map.287 = (bf16[512,1024]{1,0:T(8,128)(2,1)S(1)}, f32[8,512,128]{2,1,0:T(8,128)S(1)}, f32[8,512,128]{2,1,0:T(8,128)}, bf16[512,1024]{1,0:T(8,128)(2,1)S(1)}, f32[8,128]{1,0:T(8,128)S(1)}) custom-call(f32[512,1024]{1,0:T(8,128)} %slice_add_fusion.3.lead, f32[512,1024]{1,0:T(8,128)} %slice_add_fusion.2.gate, s32[512,1]{1,0:T(8,128)S(1)} %add_subtract_fusion.offset, ...), custom_call_target="tpu_custom_call" | custom-call | flops 29699999744 | bytes 81000000 | tf_op jit(solution)/shard_map/pallas_call | solution.py:350
  214.3 52.4 %shard_map.288 = (f32[256,1536]{1,0:T(8,128)}, bf16[512,1536]{1,0:T(8,128)(2,1)}, bf16[512,128]{1,0:T(8,128)(2,1)S(1)}, bf16[192,3072]{1,0:T(8,128)(2,1)}, bf16[192,2304]{1,0:T(8,128)(2,1)S(1)}) custom-call(bf16[512,1024]{1,0:T(8,128)(2,1)S(1)} %get-tuple-element.113.refs_0_, bf16[1536,3072]{1,0:T(8,128)(2,1)} %all-gather.5.cloned.1.call-done.refs_1_, ...), custom_call_target="tpu_custom_call" | custom-call | flops 44000002048 | bytes 120000000 | tf_op jit(solution)/shard_map/pallas_call | solution.py:1009
  273.3 11.4 %fusion.2 = f32[512,4608]{1,0:T(8,128)S(1)} fusion(bf16[512,1536]{1,0:T(8,128)(2,1)} %get-tuple-element.115.refs_15_, bf16[1536,6912]{1,0:T(8,128)(2,1)} %all-gather.7.cloned.1.call-done.refs_1_.refs_2_), kind=kOutput, calls=%fused_computation.2 | convolution fusion | flops 7247757312 | bytes 25165824 | tf_op jit(solution)/shard_map/dot_general | solution.py:27
  285.5 5.1 multiply_convert_fusion.6
  290.6 20.6 %collective-permute-done.1.refs_10_ = bf16[192,2304]{1,0:T(8,128)(2,1)S(1)} collective-permute-done((bf16[192,2304]{1,0:T(8,128)(2,1)}, bf16[192,2304]{1,0:T(8,128)(2,1)S(1)}, u32[]{:S(2)}, u32[]{:S(2)}) %collective-permute-start.1) | collective-permute-done | bytes 884768 | tf_op jit(solution)/shard_map/ppermute | solution.py:1044
  316.7 40.0 %shard_map.289 = (f32[256,1536]{1,0:T(8,128)S(1)}, bf16[512,1536]{1,0:T(8,128)(2,1)}, bf16[512,128]{1,0:T(8,128)(2,1)S(1)}, bf16[192,6912]{1,0:T(8,128)(2,1)}) custom-call(bf16[512,2304]{1,0:T(8,128)(2,1)} %copy-done.117, bf16[1536,6912]{1,0:T(8,128)(2,1)} %all-gather.7.cloned.1.call-done.refs_1_.refs_2_, bf16[512,64]{1,0:T(8,128)(2,1)S(1)} %copy.137.refs_2_.refs_10_, ...), custom_call_target="tpu_custom_call" | custom-call | flops 44000002048 | bytes 120000000 | tf_op jit(solution)/shard_map/pallas_call | solution.py:1009
  361.9 6.0 fusion.6
  370.8 6.8 all-to-all-start
  381.3 31.7 %shard_map.290 = (bf16[512,1024]{1,0:T(8,128)(2,1)S(1)}, f32[8,512,128]{2,1,0:T(8,128)S(1)}, f32[8,512,128]{2,1,0:T(8,128)}, bf16[512,1024]{1,0:T(8,128)(2,1)S(1)}, f32[8,128]{1,0:T(8,128)S(1)}) custom-call(f32[512,1024]{1,0:T(8,128)} %slice_add_fusion.1.lead, f32[512,1024]{1,0:T(8,128)} %slice_add_fusion.gate, s32[512,1]{1,0:T(8,128)S(1)} %copy-done.23, ...), custom_call_target="tpu_custom_call" | custom-call | flops 29699999744 | bytes 81000000 | tf_op jit(solution)/shard_map/pallas_call | solution.py:350
  421.3 41.5 %shard_map.291 = (f32[256,1536]{1,0:T(8,128)S(1)}, bf16[512,1536]{1,0:T(8,128)(2,1)S(1)}, bf16[512,128]{1,0:T(8,128)(2,1)S(1)}) custom-call(bf16[512,1024]{1,0:T(8,128)(2,1)S(1)} %get-tuple-element.132.refs_0_.refs_13_, bf16[1536,3072]{1,0:T(8,128)(2,1)} %all-gather.9.cloned.1.call-done.refs_1_.refs_2_, bf16[512,64]{1,0:T(8,128)(2,1)S(1)} %copy.139.refs_2_.refs_10_, ...), custom_call_target="tpu_custom_call" | custom-call | flops 44000002048 | bytes 120000000 | tf_op jit(solution)/shard_map/pallas_call | solution.py:1009
  469.6 10.7 %fusion = f32[512,4608]{1,0:T(8,128)S(1)} fusion(bf16[512,1536]{1,0:T(8,128)(2,1)} %copy-done.67, bf16[1536,6912]{1,0:T(8,128)(2,1)} %all-gather.11.cloned.1.call-done.refs_2_), kind=kOutput, calls=%fused_computation | convolution fusion | flops 7247757312 | bytes 25165824 | tf_op jit(solution)/shard_map/dot_general | solution.py:27
  489.5 10.2 %multiply_convert_fusion.2 = (bf16[512,2304]{1,0:T(8,128)(2,1)S(1)}, bf16[512,2304]{1,0:T(8,128)(2,1)}) fusion(f32[512,2304]{1,0:T(8,128)S(1)} %convolution_add_fusion.2, f32[512,2304]{1,0:T(8,128)S(1)} %bitcast.376, f32[512,2304]{1,0:T(8,128)S(1)} %fusion.166, bf16[512,1536]{1,0:T(8,128)(2,1)S(1)} %constant_dynamic-update-slice_fusion.refs_11_, ...), kind=kOutput, calls=%fused_computation.24 | convolution fusion | flops 3655729152 | bytes 27525120 | tf_op jit(solution)/shard_map/dot_general | solution.py:27
  504.7 5.4 fusion.10
  511.4 55.5 %shard_map.292 = (f32[256,1536]{1,0:T(8,128)S(1)}, bf16[512,1536]{1,0:T(8,128)(2,1)}, bf16[512,64]{1,0:T(8,128)(2,1)S(1)}, f32[64,1536]{1,0:T(8,128)S(1)}, f32[6...) custom-call(bf16[512,2304]{1,0:T(8,128)(2,1)} %get-tuple-element.199.refs_0_, ...), custom_call_target="tpu_custom_call" | custom-call | flops 44000002048 | bytes 120000000 | tf_op jit(solution)/shard_map/pallas_call | solution.py:1009
  570.2 5.1 fusion.12
  583.0 30.6 %shard_map.293 = (bf16[512,1024]{1,0:T(8,128)(2,1)S(1)}, bf16[512,1024]{1,0:T(8,128)(2,1)S(1)}) custom-call(f32[512,1024]{1,0:T(8,128)} %convolution_add_fusion.12.grad, f32[512,1024]{1,0:T(8,128)} %slice_add_fusion.gate, f32[8,512,128]{2,1,0:T(8,128)} %get-tuple-element.145.hidden, f32[8,512,128]{2,1,0:T(8,128)} %copy-done.69, ...), custom_call_target="tpu_custom_call" | custom-call | flops 32999999488 | bytes 90000000 | tf_op jit(solution)/shard_map/pallas_call | solution.py:350
  621.8 43.2 %shard_map.294 = (f32[256,1536]{1,0:T(8,128)}, bf16[512,1536]{1,0:T(8,128)(2,1)}, bf16[512,64]{1,0:T(8,128)(2,1)S(1)}, f32[64,1536]{1,0:T(8,128)S(1)}, f32[64,10...) custom-call(bf16[512,1024]{1,0:T(8,128)(2,1)S(1)} %get-tuple-element.149.refs_0_, ...), custom_call_target="tpu_custom_call" | custom-call | flops 44000002048 | bytes 120000000 | tf_op jit(solution)/shard_map/pallas_call | solution.py:1009
  665.1 7.2 fusion.4
  682.5 43.0 %shard_map.295 = (f32[256,1536]{1,0:T(8,128)S(1)}, bf16[512,1536]{1,0:T(8,128)(2,1)}, bf16[512,64]{1,0:T(8,128)(2,1)S(1)}, f32[64,1536]{1,0:T(8,128)S(1)}, f32[6...) custom-call(bf16[512,2304]{1,0:T(8,128)(2,1)} %get-tuple-element.203.refs_0_, ...), custom_call_target="tpu_custom_call" | custom-call | flops 44000002048 | bytes 120000000 | tf_op jit(solution)/shard_map/pallas_call | solution.py:1009
  734.7 35.2 %shard_map.296 = (bf16[512,1024]{1,0:T(8,128)(2,1)S(1)}, bf16[512,1024]{1,0:T(8,128)(2,1)S(1)}) custom-call(f32[512,1024]{1,0:T(8,128)} %convolution_add_fusion.11.grad, f32[512,1024]{1,0:T(8,128)} %slice_add_fusion.2.gate, f32[8,512,128]{2,1,0:T(8,128)} %get-tuple-element.158.hidden, f32[8,512,128]{2,1,0:T(8,128)} %copy-done.68, f32[8,128]{1,0:T(8,128)S(1)} %copy-done.91, ...), custom_call_target="tpu_custom_call" | custom-call | flops 32999999488 | bytes 90000000 | tf_op jit(solution)/shard_map/pallas_call | solution.py:350
  786.2 95.3 %shard_map.297 = (f32[1024,384]{1,0:T(8,128)}, bf16[2,1024,384]{2,1,0:T(8,128)(2,1)}, f32[128,1536]{1,0:T(8,128)}, f32[64,1536]{1,0:T(8,128)S(1)}, f32[128,1536]...) custom-call(f32[256,1536]{1,0:T(8,128)} %copy-done.76, ...), custom_call_target="tpu_custom_call" | custom-call | flops 88000004096 | bytes 240000000 | tf_op jit(solution)/shard_map/pallas_call | solution.py:350
  (510 shorter events, 169.2 us)
Async XLA Ops:
  7.2 166.8 %all-gather.5.cloned.1.call-start = ((), (), s32[]{:S(2)}) async-start(), calls=%async_computation.1 | async-start | bytes 10616832 | tf_op jit(solution)/shard_map/all_gather | solution.py:1260
  13.2 46.1 %copy-start.157 = (s32[4]{0:T(128)S(1)}, s32[4]{0:T(128)}, u32[]{:S(2)}) copy-start(s32[4]{0:T(128)} %param.24) | copy-start | bytes 52
  13.2 55.1 %copy-start.151 = (bf16[2,512,8,16]{1,3,2,0:T(8,128)(2,1)S(1)}, bf16[2,512,8,16]{1,3,2,0:T(8,128)(2,1)}, u32[]{:S(2)}) copy-start(bf16[2,512,8,16]{1,3,2,0:T(8,128)(2,1)} %param.36) | copy-start | bytes 786436
  13.2 55.2 %copy-start.150 = (bf16[2,2,8,16,512]{4,3,2,1,0:T(8,128)(2,1)S(1)}, bf16[2,2,8,16,512]{4,3,2,1,0:T(8,128)(2,1)}, u32[]{:S(2)}) copy-start(bf16[2,2,8,16,512]{4,3,2,1,0:T(8,128)(2,1)} %param.29) | copy-start | bytes 1572868
  59.3 214.0 %all-gather.7.cloned.1.call-start = ((), (), s32[]{:S(2)}) async-start(), calls=%async_computation.2 | async-start | bytes 23887872 | tf_op jit(solution)/shard_map/all_gather | solution.py:1260
  155.2 206.6 %all-gather.9.cloned.1.call-start = ((), (), s32[]{:S(2)}) async-start(), calls=%async_computation.3 | async-start | bytes 10616832 | tf_op jit(solution)/shard_map/all_gather | solution.py:1260
  155.8 27.8 %collective-permute-start = (bf16[192,1536]{1,0:T(8,128)(2,1)}, bf16[192,1536]{1,0:T(8,128)(2,1)}, u32[]{:S(2)}, u32[]{:S(2)}) collective-permute-start(bf16[192,1536]{1,0:T(8,128)(2,1)} %get-tuple-element.109.refs_9_), channel_id=1, source_target_pairs={{2,0},{3,1},{0,2},{1,3},{6,4},{7,5},{4,6},{5,7},{10,8},{11,9},{8,1... | collective-permute-start | bytes 1769480 | tf_op jit(solution)/shard_map/ppermute | solution.py:1044
  159.5 54.3 %copy-start = (f32[512,64]{1,0:T(8,128)}, f32[512,64]{1,0:T(8,128)S(1)}, u32[]{:S(2)}) copy-start(f32[512,64]{1,0:T(8,128)S(1)} %copy.129.refs_9_) | copy-start | bytes 393220
  171.1 43.2 %copy-start.29 = (bf16[1,4,16,1536]{3,2,1,0:T(8,128)(2,1)}, bf16[1,4,16,1536]{3,2,1,0:T(8,128)(2,1)S(1)}, u32[]{:S(2)}) copy-start(bf16[1,4,16,1536]{3,2,1,0:T(8,128)(2,1)S(1)} %get-tuple-element.290) | copy-start | bytes 589828
  213.8 53.0 %copy-start.2 = (bf16[512,1024]{1,0:T(8,128)(2,1)}, bf16[512,1024]{1,0:T(8,128)(2,1)S(1)}, u32[]{:S(2)}) copy-start(bf16[512,1024]{1,0:T(8,128)(2,1)S(1)} %get-tuple-element.113.refs_0_) | copy-start | bytes 3145732
  213.8 53.0 %copy-start.90 = (f32[8,128]{1,0:T(8,128)}, f32[8,128]{1,0:T(8,128)S(1)}, u32[]{:S(2)}) copy-start(f32[8,128]{1,0:T(8,128)S(1)} %get-tuple-element.160.carry) | copy-start | bytes 12292
  214.2 52.6 %copy-start.12 = (bf16[512,64]{1,0:T(8,128)(2,1)}, bf16[512,64]{1,0:T(8,128)(2,1)S(1)}, u32[]{:S(2)}) copy-start(bf16[512,64]{1,0:T(8,128)(2,1)S(1)} %fusion.38.refs_2_) | copy-start | bytes 196612
  214.3 53.7 %copy-start.144 = (bf16[2,1,16,1536]{3,2,1,0:T(8,128)(2,1)S(1)}, bf16[2,1,16,1536]{3,2,1,0:T(8,128)(2,1)}, u32[]{:S(2)}) copy-start(bf16[2,1,16,1536]{3,2,1,0:T(8,128)(2,1)} %get-tuple-element.261) | copy-start | bytes 294916
  214.3 54.7 %copy-start.121 = (bf16[192,1152]{1,0:T(8,128)(2,1)S(1)}, bf16[192,1152]{1,0:T(8,128)(2,1)}, u32[]{:S(2)}) copy-start(bf16[192,1152]{1,0:T(8,128)(2,1)} %get-tuple-element.243) | copy-start | bytes 1327108
  214.3 54.7 %copy-start.123 = (bf16[192,1152]{1,0:T(8,128)(2,1)S(1)}, bf16[192,1152]{1,0:T(8,128)(2,1)}, u32[]{:S(2)}) copy-start(bf16[192,1152]{1,0:T(8,128)(2,1)} %copy-done.122) | copy-start | bytes 1327108
  267.7 201.9 %all-gather.11.cloned.1.call-start = ((), (), s32[]{:S(2)}) async-start(), calls=%async_computation.4 | async-start | bytes 23887872 | tf_op jit(solution)/shard_map/all_gather | solution.py:1260
  270.7 43.6 %copy-start.31 = (bf16[1,4,16,1536]{3,2,1,0:T(8,128)(2,1)}, bf16[1,4,16,1536]{3,2,1,0:T(8,128)(2,1)S(1)}, u32[]{:S(2)}) copy-start(bf16[1,4,16,1536]{3,2,1,0:T(8,128)(2,1)S(1)} %get-tuple-element.288) | copy-start | bytes 589828
  270.8 40.5 %collective-permute-start.1 = (bf16[192,2304]{1,0:T(8,128)(2,1)}, bf16[192,2304]{1,0:T(8,128)(2,1)S(1)}, u32[]{:S(2)}, u32[]{:S(2)}) collective-permute-start(bf16[192,2304]{1,0:T(8,128)(2,1)} %pad_maximum_fusion.6), channel_id=1, source_target_pairs={{2,0},{3,1},{0,2},{1,3},{6,4},{7,5},{4,6},{5,7},{10,8},{11,9},{8,1... | collective-permute-start | bytes 2654216 | tf_op jit(solution)/shard_map/ppermute | solution.py:1044
  314.3 42.4 %copy-start.36 = (bf16[512,64]{1,0:T(8,128)(2,1)}, bf16[512,64]{1,0:T(8,128)(2,1)S(1)}, u32[]{:S(2)}) copy-start(bf16[512,64]{1,0:T(8,128)(2,1)S(1)} %copy.137.refs_2_.refs_10_) | copy-start | bytes 196612
  370.8 45.3 %all-to-all-start = ((bf16[4,256,384]{2,1,0:T(8,128)(2,1)}), bf16[4,256,384]{2,1,0:T(8,128)(2,1)}, u32[]{:S(2)}, u32[]{:S(2)}) async-start(bf16[4,256,384]{2,1,0:T(8,128)(2,1)} %bitcast.82), calls=%async_computation | async-start | bytes 1572864 | tf_op jit(solution)/shard_map/all_to_all | solution.py:1061
  421.3 41.5 %copy-start.38 = (bf16[512,64]{1,0:T(8,128)(2,1)}, bf16[512,64]{1,0:T(8,128)(2,1)S(1)}, u32[]{:S(2)}) copy-start(bf16[512,64]{1,0:T(8,128)(2,1)S(1)} %copy.139.refs_2_.refs_10_) | copy-start | bytes 196612
  464.0 21.7 %collective-permute-start.2 = (bf16[256,1536]{1,0:T(8,128)(2,1)}, bf16[256,1536]{1,0:T(8,128)(2,1)}, u32[]{:S(2)}, u32[]{:S(2)}) collective-permute-start(bf16[256,1536]{1,0:T(8,128)(2,1)} %bitcast.176), channel_id=1, source_target_pairs={{0,1},{1,0},{2,3},{3,2},{4,5},{5,4},{6,7},{7,6},{8,9},{9,8},{10,11... | collective-permute-start | bytes 2359304 | tf_op jit(solution)/shard_map/ppermute | solution.py:1039
  510.4 65.0 %collective-permute-start.3 = (bf16[256,1536]{1,0:T(8,128)(2,1)S(1)}, bf16[256,1536]{1,0:T(8,128)(2,1)S(1)}, u32[]{:S(2)}, u32[]{:S(2)}) collective-permute-start(bf16[256,1536]{1,0:T(8,128)(2,1)S(1)} %fusion.31), channel_id=1, source_target_pairs={{0,1},{1,0},{2,3},{3,2},{4,5},{5,4},{6,7},{7,6},{8,9},{9,8},{10,11... | collective-permute-start | bytes 2359304 | tf_op jit(solution)/shard_map/ppermute | solution.py:1039
  682.5 43.1 %copy-start.13 = (bf16[512,64]{1,0:T(8,128)(2,1)S(1)}, bf16[512,64]{1,0:T(8,128)(2,1)}, u32[]{:S(2)}) copy-start(bf16[512,64]{1,0:T(8,128)(2,1)} %copy-done.12) | copy-start | bytes 196612
  (152 other events, 796.0 us)
Sparse Core Ops, SparseCore 0:
  59.4 88.1 all-gather.4
  155.4 109.6 all-gather.6
  267.9 58.3 all-gather.8
  358.1 111.4 all-gather.10

commit v6 on v5

--- a/solution.py
+++ b/solution.py
@@ -530,7 +530,7 @@
         states_out[layer, mine] = leaving[layer, col]
     pair = remote(other_part, received, pair_sems, 0, (row, col + 1 - 2 * (col % 2)))
     pair.start()
-    for copy in states:
+    for copy in states[0::layers]:
         copy.start()
     paired.wait()
 
@@ -615,6 +615,9 @@
         copy = remote(outgoing.at[to], homing.at[col], token_sems, by - 1, (row, to))
         copy.start()
         returned.append(copy)
+    for layer in range(1, layers):
+        for copy in states[layer::layers]:
+            copy.start()
     homing[col] = outgoing[col]
     for copy in last:
         copy.wait()

time: 917 us -> 919 us (level)
  no operation moved by 1% of the time
where the time goes in v6:
time: 919 us; the launch traced here: 911 us
  Pallas kernels  621 us (68%)
  matrix products  127 us (14%)
  local copies, waits for them, and re-layouts  63.7 us (7%)
  other arithmetic  36 us (4%)
  between operations  25.5 us (3%)
  waiting for transfers between devices  24.3 us (3%)
  starting transfers between devices  12.8 us (1%)
    pallas_call x7, Pallas kernels, block_call(): pl.pallas_call(kernel, out_shape=[jax.ShapeDtypeStruct(*out) for out in o...  346 us
    pallas_call x6, Pallas kernels, turn(): pl.pallas_call(partial(turn_kernel, backward, len(xs), offset, plan, len(...  276 us
    dot_general x24, matrix products, nn(): lax.dot_general(left, right, (((1,), (0,)), ((), ())), preferred_element_...  88.6 us
    unnamed x339, local copies, waits for them, and re-layouts  37.1 us
    dot_general x20, matrix products, nt(): lax.dot_general(left, right, (((1,), (1,)), ((), ())), preferred_element_...  33.4 us
    ppermute x2, waiting for transfers between devices, from_shard(): lax.ppermute(value, 'col', [((at + 2 * turn) % peers, at) for at in range...  22.4 us
  transfers between devices with their start and end apart: 9, of which 3 were waited for; matrix products, arithmetic and copies ran while one was open for 11% of the time, Pallas kernels for 36%

profile of v6, /device:TPU:0, one launch (start us, length us, event | category | flops | bytes accessed | tf_op | source)
XLA Modules:
  0.0 910.6 jit_solution(18122349648871802893)
XLA Ops:
  13.2 46.0 %shard_map.285 = (bf16[256,1536]{1,0:T(8,128)(2,1)S(1)}, f32[4,4,384]{2,1,0:T(4,128)S(1)}, f32[2,16,512]{2,1,0:T(8,128)S(1)}, bf16[192,3072]{1,0:T(8,128)(2,1)}) custom-call(bf16[1024,384]{1,0:T(8,128)(2,1)S(1)} %copy-done.66, f32[4,384]{1,0:T(4,128)S(1)} %reshape.409.gains, f32[16,512]{1,0:T(8,128)S(1)} %maximum_bitcast_fusion.vectors, ...), custom_call_target="tpu_custom_call" | custom-call | flops 32999999488 | bytes 90000000 | tf_op jit(solution)/shard_map/pallas_call | solution.py:350
  76.1 79.1 %shard_map.286 = (bf16[512,1536]{1,0:T(8,128)(2,1)}, bf16[2,192,512]{2,1,0:T(8,128)(2,1)S(1)}, bf16[2,1024,256]{2,1,0:T(8,128)(2,1)}, bf16[2,192,1152]{2,1,0:T(8...) custom-call(bf16[256,1536]{1,0:T(8,128)(2,1)S(1)} %multiply_convert_, ...), custom_call_target="tpu_custom_call" | custom-call | flops 44000002048 | bytes 120000000 | tf_op jit(solution)/shard_map/pallas_call | solution.py:350
  174.0 6.1 fusion.8
  185.5 26.0 %shard_map.287 = (bf16[512,1024]{1,0:T(8,128)(2,1)S(1)}, f32[8,512,128]{2,1,0:T(8,128)S(1)}, f32[8,512,128]{2,1,0:T(8,128)}, bf16[512,1024]{1,0:T(8,128)(2,1)S(1)}, f32[8,128]{1,0:T(8,128)S(1)}) custom-call(f32[512,1024]{1,0:T(8,128)} %slice_add_fusion.3.lead, f32[512,1024]{1,0:T(8,128)} %slice_add_fusion.2.gate, s32[512,1]{1,0:T(8,128)S(1)} %add_subtract_fusion.offset, ...), custom_call_target="tpu_custom_call" | custom-call | flops 29699999744 | bytes 81000000 | tf_op jit(solution)/shard_map/pallas_call | solution.py:350
  214.3 52.4 %shard_map.288 = (f32[256,1536]{1,0:T(8,128)}, bf16[512,1536]{1,0:T(8,128)(2,1)}, bf16[512,128]{1,0:T(8,128)(2,1)S(1)}, bf16[192,3072]{1,0:T(8,128)(2,1)}, bf16[192,2304]{1,0:T(8,128)(2,1)S(1)}) custom-call(bf16[512,1024]{1,0:T(8,128)(2,1)S(1)} %get-tuple-element.113.refs_0_, bf16[1536,3072]{1,0:T(8,128)(2,1)} %all-gather.5.cloned.1.call-done.refs_1_, ...), custom_call_target="tpu_custom_call" | custom-call | flops 44000002048 | bytes 120000000 | tf_op jit(solution)/shard_map/pallas_call | solution.py:1012
  273.3 11.4 %fusion.2 = f32[512,4608]{1,0:T(8,128)S(1)} fusion(bf16[512,1536]{1,0:T(8,128)(2,1)} %get-tuple-element.115.refs_15_, bf16[1536,6912]{1,0:T(8,128)(2,1)} %all-gather.7.cloned.1.call-done.refs_1_.refs_2_), kind=kOutput, calls=%fused_computation.2 | convolution fusion | flops 7247757312 | bytes 25165824 | tf_op jit(solution)/shard_map/dot_general | solution.py:27
  285.5 5.1 multiply_convert_fusion.6
  290.6 20.6 %collective-permute-done.1.refs_10_ = bf16[192,2304]{1,0:T(8,128)(2,1)S(1)} collective-permute-done((bf16[192,2304]{1,0:T(8,128)(2,1)}, bf16[192,2304]{1,0:T(8,128)(2,1)S(1)}, u32[]{:S(2)}, u32[]{:S(2)}) %collective-permute-start.1) | collective-permute-done | bytes 884768 | tf_op jit(solution)/shard_map/ppermute | solution.py:1047
  316.7 40.0 %shard_map.289 = (f32[256,1536]{1,0:T(8,128)S(1)}, bf16[512,1536]{1,0:T(8,128)(2,1)}, bf16[512,128]{1,0:T(8,128)(2,1)S(1)}, bf16[192,6912]{1,0:T(8,128)(2,1)}) custom-call(bf16[512,2304]{1,0:T(8,128)(2,1)} %copy-done.117, bf16[1536,6912]{1,0:T(8,128)(2,1)} %all-gather.7.cloned.1.call-done.refs_1_.refs_2_, bf16[512,64]{1,0:T(8,128)(2,1)S(1)} %copy.137.refs_2_.refs_10_, ...), custom_call_target="tpu_custom_call" | custom-call | flops 44000002048 | bytes 120000000 | tf_op jit(solution)/shard_map/pallas_call | solution.py:1012
  361.9 6.0 fusion.6
  370.7 6.8 all-to-all-start
  381.3 31.7 %shard_map.290 = (bf16[512,1024]{1,0:T(8,128)(2,1)S(1)}, f32[8,512,128]{2,1,0:T(8,128)S(1)}, f32[8,512,128]{2,1,0:T(8,128)}, bf16[512,1024]{1,0:T(8,128)(2,1)S(1)}, f32[8,128]{1,0:T(8,128)S(1)}) custom-call(f32[512,1024]{1,0:T(8,128)} %slice_add_fusion.1.lead, f32[512,1024]{1,0:T(8,128)} %slice_add_fusion.gate, s32[512,1]{1,0:T(8,128)S(1)} %copy-done.23, ...), custom_call_target="tpu_custom_call" | custom-call | flops 29699999744 | bytes 81000000 | tf_op jit(solution)/shard_map/pallas_call | solution.py:350
  421.3 41.4 %shard_map.291 = (f32[256,1536]{1,0:T(8,128)S(1)}, bf16[512,1536]{1,0:T(8,128)(2,1)S(1)}, bf16[512,128]{1,0:T(8,128)(2,1)S(1)}) custom-call(bf16[512,1024]{1,0:T(8,128)(2,1)S(1)} %get-tuple-element.132.refs_0_.refs_13_, bf16[1536,3072]{1,0:T(8,128)(2,1)} %all-gather.9.cloned.1.call-done.refs_1_.refs_2_, bf16[512,64]{1,0:T(8,128)(2,1)S(1)} %copy.139.refs_2_.refs_10_, ...), custom_call_target="tpu_custom_call" | custom-call | flops 44000002048 | bytes 120000000 | tf_op jit(solution)/shard_map/pallas_call | solution.py:1012
  469.6 10.7 %fusion = f32[512,4608]{1,0:T(8,128)S(1)} fusion(bf16[512,1536]{1,0:T(8,128)(2,1)} %copy-done.67, bf16[1536,6912]{1,0:T(8,128)(2,1)} %all-gather.11.cloned.1.call-done.refs_2_), kind=kOutput, calls=%fused_computation | convolution fusion | flops 7247757312 | bytes 25165824 | tf_op jit(solution)/shard_map/dot_general | solution.py:27
  489.4 10.2 %multiply_convert_fusion.2 = (bf16[512,2304]{1,0:T(8,128)(2,1)S(1)}, bf16[512,2304]{1,0:T(8,128)(2,1)}) fusion(f32[512,2304]{1,0:T(8,128)S(1)} %convolution_add_fusion.2, f32[512,2304]{1,0:T(8,128)S(1)} %bitcast.376, f32[512,2304]{1,0:T(8,128)S(1)} %fusion.166, bf16[512,1536]{1,0:T(8,128)(2,1)S(1)} %constant_dynamic-update-slice_fusion.refs_11_, ...), kind=kOutput, calls=%fused_computation.24 | convolution fusion | flops 3655729152 | bytes 27525120 | tf_op jit(solution)/shard_map/dot_general | solution.py:27
  504.7 5.4 fusion.10
  511.4 55.5 %shard_map.292 = (f32[256,1536]{1,0:T(8,128)S(1)}, bf16[512,1536]{1,0:T(8,128)(2,1)}, bf16[512,64]{1,0:T(8,128)(2,1)S(1)}, f32[64,1536]{1,0:T(8,128)S(1)}, f32[6...) custom-call(bf16[512,2304]{1,0:T(8,128)(2,1)} %get-tuple-element.199.refs_0_, ...), custom_call_target="tpu_custom_call" | custom-call | flops 44000002048 | bytes 120000000 | tf_op jit(solution)/shard_map/pallas_call | solution.py:1012
  570.2 5.1 fusion.12
  583.0 30.6 %shard_map.293 = (bf16[512,1024]{1,0:T(8,128)(2,1)S(1)}, bf16[512,1024]{1,0:T(8,128)(2,1)S(1)}) custom-call(f32[512,1024]{1,0:T(8,128)} %convolution_add_fusion.12.grad, f32[512,1024]{1,0:T(8,128)} %slice_add_fusion.gate, f32[8,512,128]{2,1,0:T(8,128)} %get-tuple-element.145.hidden, f32[8,512,128]{2,1,0:T(8,128)} %copy-done.69, ...), custom_call_target="tpu_custom_call" | custom-call | flops 32999999488 | bytes 90000000 | tf_op jit(solution)/shard_map/pallas_call | solution.py:350
  621.8 43.2 %shard_map.294 = (f32[256,1536]{1,0:T(8,128)}, bf16[512,1536]{1,0:T(8,128)(2,1)}, bf16[512,64]{1,0:T(8,128)(2,1)S(1)}, f32[64,1536]{1,0:T(8,128)S(1)}, f32[64,10...) custom-call(bf16[512,1024]{1,0:T(8,128)(2,1)S(1)} %get-tuple-element.149.refs_0_, ...), custom_call_target="tpu_custom_call" | custom-call | flops 44000002048 | bytes 120000000 | tf_op jit(solution)/shard_map/pallas_call | solution.py:1012
  665.1 7.2 fusion.4
  682.5 43.0 %shard_map.295 = (f32[256,1536]{1,0:T(8,128)S(1)}, bf16[512,1536]{1,0:T(8,128)(2,1)}, bf16[512,64]{1,0:T(8,128)(2,1)S(1)}, f32[64,1536]{1,0:T(8,128)S(1)}, f32[6...) custom-call(bf16[512,2304]{1,0:T(8,128)(2,1)} %get-tuple-element.203.refs_0_, ...), custom_call_target="tpu_custom_call" | custom-call | flops 44000002048 | bytes 120000000 | tf_op jit(solution)/shard_map/pallas_call | solution.py:1012
  734.7 35.0 %shard_map.296 = (bf16[512,1024]{1,0:T(8,128)(2,1)S(1)}, bf16[512,1024]{1,0:T(8,128)(2,1)S(1)}) custom-call(f32[512,1024]{1,0:T(8,128)} %convolution_add_fusion.11.grad, f32[512,1024]{1,0:T(8,128)} %slice_add_fusion.2.gate, f32[8,512,128]{2,1,0:T(8,128)} %get-tuple-element.158.hidden, f32[8,512,128]{2,1,0:T(8,128)} %copy-done.68, f32[8,128]{1,0:T(8,128)S(1)} %copy-done.91, ...), custom_call_target="tpu_custom_call" | custom-call | flops 32999999488 | bytes 90000000 | tf_op jit(solution)/shard_map/pallas_call | solution.py:350
  786.0 97.3 %shard_map.297 = (f32[1024,384]{1,0:T(8,128)}, bf16[2,1024,384]{2,1,0:T(8,128)(2,1)}, f32[128,1536]{1,0:T(8,128)}, f32[64,1536]{1,0:T(8,128)S(1)}, f32[128,1536]...) custom-call(f32[256,1536]{1,0:T(8,128)} %copy-done.76, ...), custom_call_target="tpu_custom_call" | custom-call | flops 88000004096 | bytes 240000000 | tf_op jit(solution)/shard_map/pallas_call | solution.py:350
  (510 shorter events, 169.3 us)
Async XLA Ops:
  7.2 166.8 %all-gather.5.cloned.1.call-start = ((), (), s32[]{:S(2)}) async-start(), calls=%async_computation.1 | async-start | bytes 10616832 | tf_op jit(solution)/shard_map/all_gather | solution.py:1263
  13.2 46.1 %copy-start.157 = (s32[4]{0:T(128)S(1)}, s32[4]{0:T(128)}, u32[]{:S(2)}) copy-start(s32[4]{0:T(128)} %param.24) | copy-start | bytes 52
  13.2 55.1 %copy-start.151 = (bf16[2,512,8,16]{1,3,2,0:T(8,128)(2,1)S(1)}, bf16[2,512,8,16]{1,3,2,0:T(8,128)(2,1)}, u32[]{:S(2)}) copy-start(bf16[2,512,8,16]{1,3,2,0:T(8,128)(2,1)} %param.36) | copy-start | bytes 786436
  13.2 55.2 %copy-start.150 = (bf16[2,2,8,16,512]{4,3,2,1,0:T(8,128)(2,1)S(1)}, bf16[2,2,8,16,512]{4,3,2,1,0:T(8,128)(2,1)}, u32[]{:S(2)}) copy-start(bf16[2,2,8,16,512]{4,3,2,1,0:T(8,128)(2,1)} %param.29) | copy-start | bytes 1572868
  59.3 214.0 %all-gather.7.cloned.1.call-start = ((), (), s32[]{:S(2)}) async-start(), calls=%async_computation.2 | async-start | bytes 23887872 | tf_op jit(solution)/shard_map/all_gather | solution.py:1263
  155.2 206.6 %all-gather.9.cloned.1.call-start = ((), (), s32[]{:S(2)}) async-start(), calls=%async_computation.3 | async-start | bytes 10616832 | tf_op jit(solution)/shard_map/all_gather | solution.py:1263
  155.8 27.8 %collective-permute-start = (bf16[192,1536]{1,0:T(8,128)(2,1)}, bf16[192,1536]{1,0:T(8,128)(2,1)}, u32[]{:S(2)}, u32[]{:S(2)}) collective-permute-start(bf16[192,1536]{1,0:T(8,128)(2,1)} %get-tuple-element.109.refs_9_), channel_id=1, source_target_pairs={{2,0},{3,1},{0,2},{1,3},{6,4},{7,5},{4,6},{5,7},{10,8},{11,9},{8,1... | collective-permute-start | bytes 1769480 | tf_op jit(solution)/shard_map/ppermute | solution.py:1047
  159.5 54.3 %copy-start = (f32[512,64]{1,0:T(8,128)}, f32[512,64]{1,0:T(8,128)S(1)}, u32[]{:S(2)}) copy-start(f32[512,64]{1,0:T(8,128)S(1)} %copy.129.refs_9_) | copy-start | bytes 393220
  171.0 43.2 %copy-start.29 = (bf16[1,4,16,1536]{3,2,1,0:T(8,128)(2,1)}, bf16[1,4,16,1536]{3,2,1,0:T(8,128)(2,1)S(1)}, u32[]{:S(2)}) copy-start(bf16[1,4,16,1536]{3,2,1,0:T(8,128)(2,1)S(1)} %get-tuple-element.290) | copy-start | bytes 589828
  213.8 53.0 %copy-start.2 = (bf16[512,1024]{1,0:T(8,128)(2,1)}, bf16[512,1024]{1,0:T(8,128)(2,1)S(1)}, u32[]{:S(2)}) copy-start(bf16[512,1024]{1,0:T(8,128)(2,1)S(1)} %get-tuple-element.113.refs_0_) | copy-start | bytes 3145732
  213.8 53.0 %copy-start.90 = (f32[8,128]{1,0:T(8,128)}, f32[8,128]{1,0:T(8,128)S(1)}, u32[]{:S(2)}) copy-start(f32[8,128]{1,0:T(8,128)S(1)} %get-tuple-element.160.carry) | copy-start | bytes 12292
  214.2 52.6 %copy-start.12 = (bf16[512,64]{1,0:T(8,128)(2,1)}, bf16[512,64]{1,0:T(8,128)(2,1)S(1)}, u32[]{:S(2)}) copy-start(bf16[512,64]{1,0:T(8,128)(2,1)S(1)} %fusion.38.refs_2_) | copy-start | bytes 196612
  214.3 53.7 %copy-start.144 = (bf16[2,1,16,1536]{3,2,1,0:T(8,128)(2,1)S(1)}, bf16[2,1,16,1536]{3,2,1,0:T(8,128)(2,1)}, u32[]{:S(2)}) copy-start(bf16[2,1,16,1536]{3,2,1,0:T(8,128)(2,1)} %get-tuple-element.261) | copy-start | bytes 294916
  214.3 54.7 %copy-start.121 = (bf16[192,1152]{1,0:T(8,128)(2,1)S(1)}, bf16[192,1152]{1,0:T(8,128)(2,1)}, u32[]{:S(2)}) copy-start(bf16[192,1152]{1,0:T(8,128)(2,1)} %get-tuple-element.243) | copy-start | bytes 1327108
  214.3 54.7 %copy-start.123 = (bf16[192,1152]{1,0:T(8,128)(2,1)S(1)}, bf16[192,1152]{1,0:T(8,128)(2,1)}, u32[]{:S(2)}) copy-start(bf16[192,1152]{1,0:T(8,128)(2,1)} %copy-done.122) | copy-start | bytes 1327108
  267.7 201.8 %all-gather.11.cloned.1.call-start = ((), (), s32[]{:S(2)}) async-start(), calls=%async_computation.4 | async-start | bytes 23887872 | tf_op jit(solution)/shard_map/all_gather | solution.py:1263
  270.7 43.6 %copy-start.31 = (bf16[1,4,16,1536]{3,2,1,0:T(8,128)(2,1)}, bf16[1,4,16,1536]{3,2,1,0:T(8,128)(2,1)S(1)}, u32[]{:S(2)}) copy-start(bf16[1,4,16,1536]{3,2,1,0:T(8,128)(2,1)S(1)} %get-tuple-element.288) | copy-start | bytes 589828
  270.8 40.5 %collective-permute-start.1 = (bf16[192,2304]{1,0:T(8,128)(2,1)}, bf16[192,2304]{1,0:T(8,128)(2,1)S(1)}, u32[]{:S(2)}, u32[]{:S(2)}) collective-permute-start(bf16[192,2304]{1,0:T(8,128)(2,1)} %pad_maximum_fusion.6), channel_id=1, source_target_pairs={{2,0},{3,1},{0,2},{1,3},{6,4},{7,5},{4,6},{5,7},{10,8},{11,9},{8,1... | collective-permute-start | bytes 2654216 | tf_op jit(solution)/shard_map/ppermute | solution.py:1047
  314.3 42.4 %copy-start.36 = (bf16[512,64]{1,0:T(8,128)(2,1)}, bf16[512,64]{1,0:T(8,128)(2,1)S(1)}, u32[]{:S(2)}) copy-start(bf16[512,64]{1,0:T(8,128)(2,1)S(1)} %copy.137.refs_2_.refs_10_) | copy-start | bytes 196612
  370.7 45.3 %all-to-all-start = ((bf16[4,256,384]{2,1,0:T(8,128)(2,1)}), bf16[4,256,384]{2,1,0:T(8,128)(2,1)}, u32[]{:S(2)}, u32[]{:S(2)}) async-start(bf16[4,256,384]{2,1,0:T(8,128)(2,1)} %bitcast.82), calls=%async_computation | async-start | bytes 1572864 | tf_op jit(solution)/shard_map/all_to_all | solution.py:1064
  421.2 41.5 %copy-start.38 = (bf16[512,64]{1,0:T(8,128)(2,1)}, bf16[512,64]{1,0:T(8,128)(2,1)S(1)}, u32[]{:S(2)}) copy-start(bf16[512,64]{1,0:T(8,128)(2,1)S(1)} %copy.139.refs_2_.refs_10_) | copy-start | bytes 196612
  463.9 21.7 %collective-permute-start.2 = (bf16[256,1536]{1,0:T(8,128)(2,1)}, bf16[256,1536]{1,0:T(8,128)(2,1)}, u32[]{:S(2)}, u32[]{:S(2)}) collective-permute-start(bf16[256,1536]{1,0:T(8,128)(2,1)} %bitcast.176), channel_id=1, source_target_pairs={{0,1},{1,0},{2,3},{3,2},{4,5},{5,4},{6,7},{7,6},{8,9},{9,8},{10,11... | collective-permute-start | bytes 2359304 | tf_op jit(solution)/shard_map/ppermute | solution.py:1042
  510.4 65.0 %collective-permute-start.3 = (bf16[256,1536]{1,0:T(8,128)(2,1)S(1)}, bf16[256,1536]{1,0:T(8,128)(2,1)S(1)}, u32[]{:S(2)}, u32[]{:S(2)}) collective-permute-start(bf16[256,1536]{1,0:T(8,128)(2,1)S(1)} %fusion.31), channel_id=1, source_target_pairs={{0,1},{1,0},{2,3},{3,2},{4,5},{5,4},{6,7},{7,6},{8,9},{9,8},{10,11... | collective-permute-start | bytes 2359304 | tf_op jit(solution)/shard_map/ppermute | solution.py:1042
  682.4 43.1 %copy-start.13 = (bf16[512,64]{1,0:T(8,128)(2,1)S(1)}, bf16[512,64]{1,0:T(8,128)(2,1)}, u32[]{:S(2)}) copy-start(bf16[512,64]{1,0:T(8,128)(2,1)} %copy-done.12) | copy-start | bytes 196612
  (152 other events, 795.7 us)
Sparse Core Ops, SparseCore 0:
  59.4 88.1 all-gather.4
  155.4 109.6 all-gather.6
  267.9 58.2 all-gather.8
  358.0 111.4 all-gather.10
